TPU v7x, 32 devices: a whole 2x2x4 slice. The times are simulated.
32 devices in a mesh: groups: 2 (over x), xy: 16 (over z, y, core).
Axes of the slice: x: 2, y: 2, z: 4, core: 2. Of those that a mesh axis runs over, the one named last changes fastest.
Arguments:
- field: bfloat16 [128, 512, 512], P(('groups', 'xy')), parts along dimension 0, may hold values from -6 to 6
- spectral_weight: bfloat16 [24, 24, 2048], replicated, may hold values from -9 to 9
- local_weight: bfloat16 [32, 32], replicated, may hold values from -1 to 1
- bias: float32 [32], replicated, may hold values from -3 to 3
- cotangent: bfloat16 [128, 512, 512], P(('groups', 'xy')), parts along dimension 0, may hold values from -6 to 6
Outputs:
- output_field: bfloat16 [128, 512, 512], P(('groups', 'xy')), parts along dimension 0
- field_grad: bfloat16 [128, 512, 512], P(('groups', 'xy')), parts along dimension 0
- spectral_grad: bfloat16 [48, 24, 2048], P('groups'), parts along dimension 0
- local_grad: float32 [64, 32], P('groups'), parts along dimension 0
- bias_grad: float32 [64], P('groups'), parts along dimension 0
There are 2 independent parts, one for each index of `groups`. A program takes and returns all parts, laid end to end along the dimension named above; an argument that names none is the same for every part. Nothing has to cross between parts.
All inputs are finite; a program needn't handle non-finite values.
Results may differ from a plain program's by a relative error of at most 0.012.
The roundings to bfloat16 on the way count: a program that leaves them out, or rounds other values in their place, can miss the bound.
Values may be sent and summed in bfloat16 or wider, within the bound.
No kernel may reach another device: no remote copies, remote signals or barrier semaphores. Data moves between devices by JAX's collectives and lax.ppermute only.
A program may use at most 128 MiB of HBM per device.

v0:
```python
import math

import jax
import jax.numpy as jnp
from jax import lax
from jax.sharding import PartitionSpec as P


def ytable(count, length, weighted):
    modes = jnp.arange(count, dtype=jnp.int32)
    places = jnp.arange(length, dtype=jnp.int32)
    phase = 2.0 * math.pi * (modes[:, None] * places[None, :] % length).astype(jnp.float32) / length
    factor = (
        jnp.where(modes == 0, 1.0, 2.0).astype(jnp.float32)
        if weighted
        else jnp.ones((count,), jnp.float32)
    )
    scale = factor[:, None] / math.sqrt(length)
    return jnp.stack([scale * jnp.cos(phase), -scale * jnp.sin(phase)]).astype(jnp.bfloat16)


def xtable(count, length, places):
    index = jnp.arange(count, dtype=jnp.int32)
    modes = jnp.where(index < count // 2, index, length - count + index)
    phase = 2.0 * math.pi * (modes[:, None] * places[None, :] % length).astype(jnp.float32) / length
    return (jnp.stack([jnp.cos(phase), jnp.sin(phase)]) / math.sqrt(length)).astype(jnp.bfloat16)


def mult(form, left, right):
    return jnp.einsum(form, left, right, preferred_element_type=jnp.float32)


def to_slab(flat, table, planes):
    rows = flat.shape[0]
    count = table.shape[1]
    chans = flat.shape[2] // planes
    coeff = mult("smy,xyq->xsmq", table, flat).astype(jnp.bfloat16)
    coeff = coeff.reshape(rows, 2, count, planes, chans).transpose(0, 2, 3, 1, 4)
    return coeff.reshape(rows, count * planes, 2 * chans)


def from_slab(slab, table, planes):
    rows = slab.shape[0]
    count = table.shape[1]
    chans = slab.shape[2] // 2
    spread = slab.reshape(rows, count, planes, 2, chans)
    return mult("smy,xmpsc->xypc", table, spread).reshape(rows, table.shape[2], planes * chans)


def forward_x(table, pencil):
    proj = mult("ajx,xnsc->ajnsc", table, pencil)
    real_part = proj[0, :, :, 0] + proj[1, :, :, 1]
    imag_part = proj[0, :, :, 1] - proj[1, :, :, 0]
    return jnp.stack([real_part, imag_part], axis=2).astype(jnp.bfloat16)


def inverse_x(table, modes):
    proj = mult("ajx,jnsc->axnsc", table, modes)
    real_part = proj[0, :, :, 0] - proj[1, :, :, 1]
    imag_part = proj[0, :, :, 1] + proj[1, :, :, 0]
    return jnp.stack([real_part, imag_part], axis=2).astype(jnp.bfloat16)


def mix_modes(spectrum, weights):
    real_part = mult("jnc,jnco->jno", spectrum[:, :, 0], weights[:, :, 0]) - mult(
        "jnc,jnco->jno", spectrum[:, :, 1], weights[:, :, 1]
    )
    imag_part = mult("jnc,jnco->jno", spectrum[:, :, 0], weights[:, :, 1]) + mult(
        "jnc,jnco->jno", spectrum[:, :, 1], weights[:, :, 0]
    )
    return jnp.stack([real_part, imag_part], axis=2).astype(jnp.bfloat16)


def adjoint_mix(grads, weights):
    real_part = mult("jnco,jno->jnc", weights[:, :, 0], grads[:, :, 0]) + mult(
        "jnco,jno->jnc", weights[:, :, 1], grads[:, :, 1]
    )
    imag_part = mult("jnco,jno->jnc", weights[:, :, 0], grads[:, :, 1]) - mult(
        "jnco,jno->jnc", weights[:, :, 1], grads[:, :, 0]
    )
    return jnp.stack([real_part, imag_part], axis=2).astype(jnp.bfloat16)


def pair_grad(spectrum, grads):
    real_part = mult("jmpc,jmpo->jmco", spectrum[:, :, :, 0], grads[:, :, :, 0]) + mult(
        "jmpc,jmpo->jmco", spectrum[:, :, :, 1], grads[:, :, :, 1]
    )
    imag_part = mult("jmpc,jmpo->jmco", spectrum[:, :, :, 0], grads[:, :, :, 1]) - mult(
        "jmpc,jmpo->jmco", spectrum[:, :, :, 1], grads[:, :, :, 0]
    )
    return jnp.stack([real_part, imag_part], axis=2)


def to_modes(slab, table_full):
    count = table_full.shape[1]
    pencil = lax.all_to_all(slab, "xy", split_axis=1, concat_axis=0, tiled=True)
    chans = pencil.shape[2] // 2
    items = pencil.shape[1]
    spread = pencil.reshape(pencil.shape[0], items, 2, chans)
    return forward_x(table_full, spread).reshape(count, items, 2 * chans)


def to_space(modes, table_full):
    count, pairs_dev, twice, chans = modes.shape
    pencil = inverse_x(table_full, modes)
    moved = lax.all_to_all(
        pencil.reshape(pencil.shape[0], pairs_dev, 2 * chans),
        "xy",
        split_axis=0,
        concat_axis=1,
        tiled=True,
    )
    return moved


def shards(field, spectral_weight, local_weight, bias, cotangent):
    rows, length_y, width_all = field.shape
    chans = local_weight.shape[0]
    planes = width_all // chans
    modes_x, modes_y = (spectral_weight.shape[0], spectral_weight.shape[1])
    devices = lax.axis_size("xy")
    length_x = rows * devices
    pairs_dev = modes_y * planes // devices
    offset = lax.axis_index("xy")
    table_y = ytable(modes_y, length_y, False)
    table_yw = ytable(modes_y, length_y, True)
    table_x = xtable(modes_x, length_x, jnp.arange(length_x, dtype=jnp.int32))
    weight_all = spectral_weight.reshape(modes_x, modes_y, 2, chans, chans)
    ky_index = (offset * pairs_dev + jnp.arange(pairs_dev, dtype=jnp.int32)) // planes
    weight_pairs = jnp.take(weight_all, ky_index, axis=1)
    spectrum = to_modes(to_slab(field, table_y, planes), table_x).reshape(
        modes_x, pairs_dev, 2, chans
    )
    mixed = mix_modes(spectrum, weight_pairs)
    spatial = from_slab(to_space(mixed, table_x), table_yw, planes)
    field4 = field.reshape(rows, length_y, planes, chans)
    local_term = mult("xypc,co->xypo", field4, local_weight)
    preact = spatial.reshape(rows, length_y, planes, chans) + local_term + bias
    output_field = jax.nn.gelu(preact).astype(jnp.bfloat16).reshape(rows, length_y, width_all)
    unused, pullback = jax.vjp(jax.nn.gelu, preact)
    grad_pre = pullback(cotangent.reshape(rows, length_y, planes, chans).astype(jnp.float32))[
        0
    ].astype(jnp.bfloat16)
    bias_part = jnp.sum(grad_pre.astype(jnp.float32), axis=(0, 1, 2))
    weight_part = mult("xypc,xypo->co", field4, grad_pre)
    back_local = mult("xypo,co->xypc", grad_pre, local_weight)
    grad_slab = to_slab(grad_pre.reshape(rows, length_y, width_all), table_yw, planes)
    grad_modes = to_modes(grad_slab, table_x).reshape(modes_x, pairs_dev, 2, chans)
    grad_spec = adjoint_mix(grad_modes, weight_pairs)
    back_spec = from_slab(to_space(grad_spec, table_x), table_y, planes)
    field_grad = (back_spec + back_local.reshape(rows, length_y, width_all)).astype(jnp.bfloat16)
    per_pair = pair_grad(
        spectrum.reshape(modes_x, pairs_dev, 1, 2, chans),
        grad_modes.reshape(modes_x, pairs_dev, 1, 2, chans),
    )
    onehot = (ky_index[:, None] == jnp.arange(modes_y, dtype=jnp.int32)[None, :]).astype(
        jnp.float32
    )
    partial_grad = jnp.einsum("jnsco,nm->jmsco", per_pair, onehot, precision=lax.Precision.HIGHEST)
    total, local_grad, bias_grad = lax.psum((partial_grad, weight_part, bias_part), "xy")
    spectral_grad = total.reshape(modes_x, modes_y, 2 * chans * chans).astype(jnp.bfloat16)
    return (output_field, field_grad, spectral_grad, local_grad, bias_grad)


def solution(mesh):
    return jax.shard_map(
        shards,
        mesh=mesh,
        in_specs=(P(("groups", "xy"), None, None), P(), P(), P(), P(("groups", "xy"), None, None)),
        out_specs=(
            P(("groups", "xy"), None, None),
            P(("groups", "xy"), None, None),
            P("groups", None, None),
            P("groups", None),
            P("groups"),
        ),
        check_vma=False,
    )
```

profile of v0, /device:TPU:1, one launch (start us, length us, event | category | flops | bytes accessed | tf_op | source)
XLA Modules:
  0.0 593.1 jit_solution(12693009896105762905)
XLA Ops:
  0.9 0.6 copy-done.7
  1.5 2.1 fusion.41
  3.5 0.4 reshape.658
  4.0 1.1 copy.234
  5.1 0.4 reshape.659
  5.5 0.3 copy.236
  5.8 0.9 reshape.708
  6.7 7.4 %all-to-all-start = ((bf16[16,2,3072]{2,1,0:T(2,128)(2,1)}), bf16[16,2,3072]{2,1,0:T(2,128)(2,1)S(1)}, u32[]{:S(2)}, u32[]{:S(2)}) async-start(bf16[16,2,3072]{2,1,0:T(2,128)(2,1)} %reshape.708), calls=%async_computation | async-start | bytes 393216 | tf_op jit(solution)/shard_map/all_to_all | solution.py:96
  14.3 9.0 %reshape.661 = bf16[24,24,2,32,32]{4,3,2,1,0:T(8,128)(2,1)} reshape(bf16[24,24,2048]{2,1,0:T(8,128)(2,1)S(1)} %copy-done.6) | data formatting | bytes 4718592 | tf_op jit(solution)/shard_map/reshape | solution.py:128
  23.3 9.5 %gather_fusion = bf16[24,24,2,32,32]{4,3,2,1,0:T(8,128)(2,1)} fusion(bf16[24,24,2,32,32]{4,3,2,1,0:T(8,128)(2,1)} %reshape.661, s32[1024]{0:T(1024)S(1)} %pad_clamp_fusion), kind=kCustom, calls=%fused_computation | custom fusion | bytes 4718688 | tf_op jit(solution)/shard_map/jit(_take)/gather | solution.py:130
  32.8 8.3 %select_bitcast_fusion = bf16[24,24,2,32,32]{4,3,2,0,1:T(8,128)(2,1)} fusion(bf16[24,24,2,32,32]{4,3,2,1,0:T(8,128)(2,1)} %gather_fusion, pred[24]{0:T(512)(128)(4,1)S(1)} %compare_and_fusion), kind=kLoop, calls=%fused_computation.5 | loop fusion | flops 1179648 | bytes 4718616 | tf_op jit(solution)/shard_map/jit(_take)/select_n | solution.py:130
  41.1 10.3 %slice_bitcast_fusion = (bf16[24,24,32,32]{3,2,0,1:T(8,128)(2,1)}, bf16[24,24,32,32]{3,2,0,1:T(8,128)(2,1)}) fusion(bf16[24,24,2,32,32]{4,3,2,0,1:T(8,128)(2,1)} %select_bitcast_fusion), kind=kLoop, calls=%fused_computation.11 | loop fusion | bytes 4718592 | tf_op jit(solution)/shard_map/squeeze | solution.py:66
  51.8 0.3 reshape.660
  52.1 1.0 copy.96
  53.2 0.7 fusion.61
  53.9 0.9 bitcast_convert_fusion.3
  54.8 4.5 fusion.20
  59.3 1.4 fusion.30
  60.7 1.4 fusion.22
  62.0 1.4 fusion.28
  63.6 0.4 fusion.67
  64.6 0.9 reshape.710
  65.5 6.3 %all-to-all-start.1 = ((bf16[16,2,3072]{2,1,0:T(2,128)(2,1)}), bf16[16,2,3072]{2,1,0:T(2,128)(2,1)S(1)}, u32[]{:S(2)}, u32[]{:S(2)}) async-start(bf16[16,2,3072]{2,1,0:T(2,128)(2,1)} %reshape.710), calls=%async_computation.1 | async-start | bytes 393216 | tf_op jit(solution)/shard_map/all_to_all | solution.py:106
  71.8 2.4 copy.103
  74.2 4.5 copy.105
  78.9 1.1 all-to-all-done.1
  80.4 0.3 reshape.662
  80.7 0.8 fusion.51
  81.5 1.4 copy-done.5
  82.9 7.0 %convert_reduce_fusion = (f32[32]{0:T(128)S(1)}, bf16[4,512,16,32]{1,3,2,0:T(8,128)(2,1)S(1)}, bf16[4,512,16,32]{1,3,2,0:T(8,128)(2,1)}) fusion(f32[4,512,16,32]{1,3,2,0:T(8,128)S(1)} %bitcast.264, f32[32]{0:T(128)S(1)} %copy-done.11, bf16[4,512,16,32]{1,3,2,0:T(8,128)(2,1)} %bitcast.267, bf16[32,32]{1,0:T(8,128)(2,1)S(1)} %copy-done, ...), kind=kOutput, calls=%fused_computation.24 | convolution fusion | flops 94371808 | bytes 14682368 | tf_op jit(solution)/shard_map/xypc,co->xypo/dot_general | solution.py:30
  89.9 0.7 fusion.40
  90.7 1.3 reshape.666
  92.0 2.2 copy.233
  94.2 0.4 reshape.667
  94.6 0.3 copy.235
  94.9 0.9 reshape.712
  95.8 5.4 all-to-all-start.2
  101.3 1.1 copy.118
  102.4 1.9 copy.120
  104.3 4.1 copy.126
  108.5 2.3 fusion.44
  111.1 0.3 reshape.668
  111.5 0.9 copy.111
  112.3 0.7 fusion.59
  113.2 5.0 fusion.26
  118.2 2.5 fusion.16
  120.8 2.5 fusion.24
  123.3 2.5 fusion.18
  126.1 0.4 fusion.70
  126.6 0.8 copy.121
  127.4 0.8 copy.119
  128.6 0.9 reshape.714
  129.5 6.3 %all-to-all-start.3 = ((bf16[16,2,3072]{2,1,0:T(2,128)(2,1)}), bf16[16,2,3072]{2,1,0:T(2,128)(2,1)}, u32[]{:S(2)}, u32[]{:S(2)}) async-start(bf16[16,2,3072]{2,1,0:T(2,128)(2,1)} %reshape.714), calls=%async_computation.3 | async-start | bytes 393216 | tf_op jit(solution)/shard_map/all_to_all | solution.py:106
  135.8 7.7 %add_bitcast_fusion = (f32[24,24,1,32,32]{4,1,3,2,0:T(8,128)S(1)}, f32[24,24,1,32,32]{4,1,3,2,0:T(8,128)}) fusion(f32[24,24,32]{2,1,0:T(8,128)} %copy.121, f32[24,24,32]{1,2,0:T(8,128)} %copy.120, f32[24,24,32]{2,1,0:T(8,128)} %copy.119, f32[24,24,32]{1,2,0:T(8,128)S(1)} %copy.118), kind=kLoop, calls=%fused_computation.7 | loop fusion | flops 3538944 | bytes 5013504 | tf_op jit(solution)/shard_map/stack | solution.py:91
  143.6 15.6 %fusion.4 = f32[24,24,2,32,32]{4,1,3,2,0:T(8,128)} fusion(f32[24,24,1,32,32]{4,1,3,2,0:T(8,128)} %get-tuple-element.42, f32[24,24,1,32,32]{4,1,3,2,0:T(8,128)S(1)} %get-tuple-element.41, s32[24]{0:T(128)S(1)} %and_select_fusion.1), kind=kOutput, calls=%fused_computation.8 | convolution fusion | flops 340918848 | bytes 9437280 | tf_op jit(solution)/shard_map/jnsco,nm->jmsco/dot_general | solution.py:159
  159.2 400.9 %all-reduce.2 = (bf16[24,24,2,32,32]{4,1,3,2,0:T(8,128)(2,1)}, f32[32,32]{0,1:T(8,128)S(1)}, f32[32]{0:T(128)}) all-reduce(f32[24,24,2,32,32]{4,1,3,2,0:T(8,128)} %fusion.4, f32[32,32]{0,1:T(8,128)S(1)} %fusion.44, f32[32]{0:T(128)S(1)} %get-tuple-element.28), channel_id=1, replica_groups=mesh['groups'=2,'xy'=16] {'xy'}, use_global_device_ids=true, to_apply=%region_0.1 | all-reduce | flops 1180704 | bytes 7086336 | tf_op jit(solution)/shard_map/psum | solution.py:160
  560.1 10.1 %copy.123 = bf16[24,24,2,32,32]{4,3,2,1,0:T(8,128)(2,1)} copy(bf16[24,24,2,32,32]{4,1,3,2,0:T(8,128)(2,1)} %get-tuple-element.25) | data formatting | bytes 4718592 | tf_op jit(solution)/shard_map/convert_element_type | solution.py:161
  570.1 13.4 %convert_element_type.134 = bf16[24,24,2048]{2,1,0:T(8,128)(2,1)} reshape(bf16[24,24,2,32,32]{4,3,2,1,0:T(8,128)(2,1)} %copy.123) | data formatting | bytes 4718592 | tf_op jit(solution)/shard_map/convert_element_type | solution.py:161
  583.6 0.7 copy.128
  584.2 1.2 reshape.715
  585.5 0.3 reshape.669
  585.9 0.8 fusion.49
  586.6 2.1 fusion.14
  588.7 4.1 copy.127
  (75 shorter events, 3.4 us)
Async XLA Ops:
  0.6 80.8 %copy-start = (bf16[32,32]{1,0:T(8,128)(2,1)S(1)}, bf16[32,32]{1,0:T(8,128)(2,1)}, u32[]{:S(2)}) copy-start(bf16[32,32]{1,0:T(8,128)(2,1)} %param.7) | copy-start | bytes 6148
  0.9 0.6 copy-start.7
  0.9 0.6 copy-start.9
  5.1 9.2 %copy-start.6 = (bf16[24,24,2048]{2,1,0:T(8,128)(2,1)S(1)}, bf16[24,24,2048]{2,1,0:T(8,128)(2,1)}, u32[]{:S(2)}) copy-start(bf16[24,24,2048]{2,1,0:T(8,128)(2,1)} %param.6) | copy-start | bytes 7077892
  6.7 44.7 %all-to-all-start = ((bf16[16,2,3072]{2,1,0:T(2,128)(2,1)}), bf16[16,2,3072]{2,1,0:T(2,128)(2,1)S(1)}, u32[]{:S(2)}, u32[]{:S(2)}) async-start(bf16[16,2,3072]{2,1,0:T(2,128)(2,1)} %reshape.708), calls=%async_computation | async-start | bytes 393216 | tf_op jit(solution)/shard_map/all_to_all | solution.py:96
  53.2 6.1 %copy-start.4 = (bf16[24,24,32,32]{3,2,0,1:T(8,128)(2,1)S(1)}, bf16[24,24,32,32]{3,2,0,1:T(8,128)(2,1)}, u32[]{:S(2)}) copy-start(bf16[24,24,32,32]{3,2,0,1:T(8,128)(2,1)} %get-tuple-element.39) | copy-start | bytes 3538948
  53.9 6.7 %slice-start = ((s8[4718592]{0:T(1024)(128)(4,1)}), s8[4194304]{0:T(1024)(128)(4,1)S(1)}, s32[]{:S(2)}) async-start(s8[4718592]{0:T(1024)(128)(4,1)} %bitcast.258), calls=%async_computation.4 | async-start | bytes 8388608
  54.8 5.8 slice-start.1
  63.4 8.4 %copy-start.3 = (bf16[4,512,512]{2,1,0:T(8,128)(2,1)S(1)}, bf16[4,512,512]{2,1,0:T(8,128)(2,1)}, u32[]{:S(2)}) copy-start(bf16[4,512,512]{2,1,0:T(8,128)(2,1)} %param.5) | copy-start | bytes 6291460
  65.5 14.5 %all-to-all-start.1 = ((bf16[16,2,3072]{2,1,0:T(2,128)(2,1)}), bf16[16,2,3072]{2,1,0:T(2,128)(2,1)S(1)}, u32[]{:S(2)}, u32[]{:S(2)}) async-start(bf16[16,2,3072]{2,1,0:T(2,128)(2,1)} %reshape.710), calls=%async_computation.1 | async-start | bytes 393216 | tf_op jit(solution)/shard_map/all_to_all | solution.py:106
  78.7 2.8 copy-start.11
  80.7 2.2 copy-start.5
  89.9 18.5 %copy-start.1 = (bf16[4,512,16,32]{1,3,2,0:T(8,128)(2,1)}, bf16[4,512,16,32]{1,3,2,0:T(8,128)(2,1)S(1)}, u32[]{:S(2)}) copy-start(bf16[4,512,16,32]{1,3,2,0:T(8,128)(2,1)S(1)} %get-tuple-element.29) | copy-start | bytes 6291460
  95.8 14.9 %all-to-all-start.2 = ((bf16[16,2,3072]{2,1,0:T(2,128)(2,1)}), bf16[16,2,3072]{2,1,0:T(2,128)(2,1)S(1)}, u32[]{:S(2)}, u32[]{:S(2)}) async-start(bf16[16,2,3072]{2,1,0:T(2,128)(2,1)} %reshape.712), calls=%async_computation.2 | async-start | bytes 393216 | tf_op jit(solution)/shard_map/all_to_all | solution.py:96
  113.1 5.1 slice-start.2
  113.2 5.0 slice-start.3
  113.2 7.6 %slice-start.4 = ((s8[4718592]{0:T(1024)(128)(4,1)}), s8[4194304]{0:T(1024)(128)(4,1)S(1)}, s32[]{:S(2)}) async-start(s8[4718592]{0:T(1024)(128)(4,1)} %bitcast.262), calls=%async_computation.8 | async-start | bytes 8388608
  118.2 2.5 slice-start.5
  129.5 454.7 %all-to-all-start.3 = ((bf16[16,2,3072]{2,1,0:T(2,128)(2,1)}), bf16[16,2,3072]{2,1,0:T(2,128)(2,1)}, u32[]{:S(2)}, u32[]{:S(2)}) async-start(bf16[16,2,3072]{2,1,0:T(2,128)(2,1)} %reshape.714), calls=%async_computation.3 | async-start | bytes 393216 | tf_op jit(solution)/shard_map/all_to_all | solution.py:106
  570.1 15.7 %copy-start.8 = (bf16[1,24,512]{2,1,0:T(8,128)(2,1)S(1)}, bf16[1,24,512]{2,1,0:T(8,128)(2,1)}, u32[]{:S(2)}) copy-start(bf16[1,24,512]{2,1,0:T(8,128)(2,1)} %copy-done.7) | copy-start | bytes 73732
  570.1 15.7 %copy-start.10 = (bf16[1,24,512]{2,1,0:T(8,128)(2,1)S(1)}, bf16[1,24,512]{2,1,0:T(8,128)(2,1)}, u32[]{:S(2)}) copy-start(bf16[1,24,512]{2,1,0:T(8,128)(2,1)} %copy-done.9) | copy-start | bytes 73732
  583.6 3.1 copy-start.2
where the time goes:
time: 601 us; the launch traced here: 593 us
  blocking collectives  401 us (67%)
  local copies, waits for them, and re-layouts  91.1 us (15%)
  matrix products  54.6 us (9%)
  starting transfers between devices  25.4 us (4%)
  other arithmetic  18.4 us (3%)
    psum x1, blocking collectives, shards(): lax.psum((partial_grad, weight_part, bias_part), 'xy')  401 us
    dot_general x19, matrix products, mult(): return jnp.einsum(form, left, right, preferred_element_type=jnp.float32)  39 us
    convert_element_type x2, local copies, waits for them, and re-layouts, shards(): total.reshape(modes_x, modes_y, 2 * chans * chans).astype(jnp.bfloat16)  23.5 us
    unnamed x48, local copies, waits for them, and re-layouts  19.1 us
    dot_general x1, matrix products, shards(): jnp.einsum('jnsco,nm->jmsco', per_pair, onehot, precision=lax.Precision.H...  15.6 us
    all_to_all x2, starting transfers between devices, to_modes(): pencil = lax.all_to_all(slab, 'xy', split_axis=1, concat_axis=0, tiled=True)  12.8 us
    all_to_all x2, starting transfers between devices, to_space(): lax.all_to_all(pencil.reshape(pencil.shape[0], pairs_dev, 2 * chans), 'xy...  12.6 us
  transfers between devices with their start and end apart: 4, of which 1 were waited for; matrix products, arithmetic and copies ran while one was open for 17% of the time, Pallas kernels for 0%

commit v1 on v0

--- a/solution.py
+++ b/solution.py
@@ -2,7 +2,11 @@
 
 import jax
 import jax.numpy as jnp
+import ml_dtypes
+import numpy as np
 from jax import lax
+from jax.experimental import pallas as pl
+from jax.experimental.pallas import tpu as pltpu
 from jax.sharding import PartitionSpec as P
 
 
@@ -113,7 +117,7 @@
     return moved
 
 
-def shards(field, spectral_weight, local_weight, bias, cotangent):
+def general_shards(field, spectral_weight, local_weight, bias, cotangent):
     rows, length_y, width_all = field.shape
     chans = local_weight.shape[0]
     planes = width_all // chans
@@ -162,6 +166,602 @@
     return (output_field, field_grad, spectral_grad, local_grad, bias_grad)
 
 
+F32 = jnp.float32
+BF16 = jnp.bfloat16
+LANES = 128
+VMEM_LIMIT = 48 * 1024 * 1024
+
+
+def dot(left, right):
+    return jnp.dot(left, right, preferred_element_type=F32)
+
+
+def params(**kwargs):
+    return pltpu.CompilerParams(vmem_limit_bytes=VMEM_LIMIT, **kwargs)
+
+
+def cost(flops, bytes_accessed):
+    return pl.CostEstimate(flops=flops, bytes_accessed=bytes_accessed, transcendentals=0)
+
+
+def np_ytable(count, length, weighted):
+    modes = np.arange(count)
+    places = np.arange(length)
+    phase = np.float32(2.0 * math.pi) * (modes[:, None] * places[None, :] % length).astype(np.float32) / np.float32(length)
+    factor = np.where(modes == 0, 1.0, 2.0).astype(np.float32) if weighted else np.ones((count,), np.float32)
+    scale = (factor / np.float32(math.sqrt(length)))[:, None]
+    both = np.stack([scale * np.cos(phase), -scale * np.sin(phase)]).astype(ml_dtypes.bfloat16)
+    return both.reshape(2 * count, length)
+
+
+def np_xtables(count, length):
+    index = np.arange(count)
+    modes = np.where(index < count // 2, index, length - count + index)
+    places = np.arange(length)
+    phase = np.float32(2.0 * math.pi) * (modes[:, None] * places[None, :] % length).astype(np.float32) / np.float32(length)
+    norm = np.float32(math.sqrt(length))
+    cosines = np.cos(phase) / norm
+    sines = np.sin(phase) / norm
+    forward = np.stack([np.stack([cosines, sines], -1), np.stack([-sines, cosines], -1)])
+    forward = forward.reshape(2 * count, 2 * length).astype(ml_dtypes.bfloat16)
+    return forward, np.ascontiguousarray(forward.T)
+
+
+def np_spread(chans):
+    groups = LANES // chans
+    out = np.zeros((groups, chans, chans, groups, chans), np.float32)
+    for g in range(groups):
+        for k in range(chans):
+            out[g, k, k, g, :] = 1
+    return out.reshape(LANES, chans * LANES).astype(ml_dtypes.bfloat16)
+
+
+def np_tile(chans):
+    groups = LANES // chans
+    out = np.zeros((groups, chans, groups, groups, chans), np.float32)
+    for g in range(groups):
+        for k in range(chans):
+            out[g, k, g, :, k] = 1
+    return out.reshape(LANES, groups * LANES).astype(ml_dtypes.bfloat16)
+
+
+def np_widen(chans):
+    groups = LANES // chans
+    step = 2 * LANES // chans
+    parts = chans // step
+    out = np.zeros((parts, groups, chans, groups, step, chans), np.float32)
+    for a in range(parts):
+        for g in range(groups):
+            for k in range(step):
+                out[a, g, a * step + k, g, k, :] = 1
+    return out.reshape(parts, LANES, groups * step * chans).astype(ml_dtypes.bfloat16)
+
+
+def scatter_rows(dst, sums, place, chips, half):
+    tiles = half // LANES
+    for s in range(2):
+        for core in range(2):
+            where = pl.ds(core * 8 + 2 * place + s, chips, stride=16)
+            own = (3 * s + 2 * core) * chips
+            shared = (3 * s + 1) * chips
+            for k in range(2 * tiles):
+                dst[k, where, :] = sums[own : own + chips, k * LANES : (k + 1) * LANES]
+            for k in range(tiles):
+                at = (core * tiles + k) * LANES
+                dst[2 * tiles + k, where, :] = sums[shared : shared + chips, at : at + LANES]
+
+
+def gather_rows(src, place, chips, half):
+    tiles = half // LANES
+    out = []
+    for s in range(2):
+        one = pl.ds(2 * place + s, chips, stride=16)
+        two = pl.ds(8 + 2 * place + s, chips, stride=16)
+        own = range(2 * tiles)
+        shared = range(2 * tiles, 3 * tiles)
+        out.append(jnp.concatenate([src[k, one, :] for k in own], axis=1))
+        out.append(jnp.concatenate([src[k, w, :] for w in (one, two) for k in shared], axis=1))
+        out.append(jnp.concatenate([src[k, two, :] for k in own], axis=1))
+    return jnp.concatenate(out, axis=0).astype(BF16)
+
+
+def cut_lanes(dst, src):
+    for k in range(dst.shape[0]):
+        dst[k] = src[:, k * LANES : (k + 1) * LANES].astype(F32)
+
+
+def join_lanes(dst, src):
+    for k in range(src.shape[0]):
+        dst[:, k * LANES : (k + 1) * LANES] = src[k].astype(BF16)
+
+
+def cut_shape(shape):
+    return (shape[1] // LANES, shape[0], LANES)
+
+
+def rows_to_modes(field, table, chips, half):
+    rows, length, width = field.shape
+
+    def kernel(u_ref, t_ref, out_ref, scr):
+        place = pl.program_id(0)
+        scatter_rows(scr, dot(t_ref[...], u_ref[0]), place, chips, half)
+
+        @pl.when(place == rows - 1)
+        def _():
+            join_lanes(out_ref, scr)
+
+    shape = (chips * 16, 3 * half)
+    return pl.pallas_call(
+        kernel,
+        grid=(rows,),
+        in_specs=[
+            pl.BlockSpec((1, length, width), lambda i: (i, 0, 0)),
+            pl.BlockSpec(table.shape, lambda i: (0, 0)),
+        ],
+        out_specs=pl.BlockSpec(shape, lambda i: (0, 0)),
+        out_shape=jax.ShapeDtypeStruct(shape, BF16),
+        scratch_shapes=[pltpu.VMEM(cut_shape(shape), F32)],
+        compiler_params=params(),
+        cost_estimate=cost(2 * table.size * rows * width, field.size * 2),
+        name="rows_to_modes",
+    )(field, table)
+
+
+def spread_weights(weights, tile):
+    rows, width = weights.shape
+    groups = width // LANES
+
+    def kernel(w_ref, t_ref, out_ref):
+        for g in range(groups):
+            out_ref[g] = dot(w_ref[:, g * LANES : (g + 1) * LANES], t_ref[...])
+
+    shape = (groups, rows, tile.shape[1])
+    return pl.pallas_call(
+        kernel,
+        out_shape=jax.ShapeDtypeStruct(shape, F32),
+        compiler_params=params(),
+        cost_estimate=cost(2 * rows * width * tile.shape[1], rows * width * 2),
+        name="spread_weights",
+    )(weights, tile)
+
+
+def mode_step(pencil, spread_w, spread, forward, inverse, modes_x, adjoint):
+    wide = pencil.shape[1]
+    tiles = wide // LANES
+    chans = spread.shape[1] // LANES
+    groups = LANES // chans
+
+    def kernel(p_ref, w_ref, e_ref, f_ref, i_ref, spec_ref, out_ref):
+        spec = dot(f_ref[...], p_ref[...]).astype(BF16)
+        spec_ref[...] = spec
+        stack = jnp.concatenate([spec[:, k * LANES : (k + 1) * LANES] for k in range(tiles)], axis=0)
+        real = [None] * tiles
+        imag = [None] * tiles
+        for pair in range(chans // 2):
+            wide_rows = dot(stack, e_ref[:, pair * 2 * LANES : (pair + 1) * 2 * LANES])
+            for c in (2 * pair, 2 * pair + 1):
+                lanes = slice((c % 2) * LANES, (c % 2 + 1) * LANES)
+                wl = slice((c % groups) * LANES, (c % groups + 1) * LANES)
+                for k in range(tiles):
+                    own = 0 if k < 2 * tiles // 3 else 1
+                    base = 2 * own * modes_x
+                    wr = w_ref[c // groups, base : base + modes_x, wl]
+                    wi = w_ref[c // groups, base + modes_x : base + 2 * modes_x, wl]
+                    xr = wide_rows[2 * k * modes_x : (2 * k + 1) * modes_x, lanes]
+                    xi = wide_rows[(2 * k + 1) * modes_x : (2 * k + 2) * modes_x, lanes]
+                    if adjoint:
+                        r, i = xr * wr + xi * wi, xi * wr - xr * wi
+                    else:
+                        r, i = xr * wr - xi * wi, xr * wi + xi * wr
+                    real[k] = r if real[k] is None else real[k] + r
+                    imag[k] = i if imag[k] is None else imag[k] + i
+        mixed = jnp.concatenate([jnp.concatenate(real, axis=1), jnp.concatenate(imag, axis=1)], axis=0)
+        out_ref[...] = dot(i_ref[...], mixed.astype(BF16)).astype(BF16)
+
+    return pl.pallas_call(
+        kernel,
+        out_shape=(
+            jax.ShapeDtypeStruct((2 * modes_x, wide), BF16),
+            jax.ShapeDtypeStruct(pencil.shape, BF16),
+        ),
+        compiler_params=params(),
+        cost_estimate=cost(2 * 48 * 6 * 128 * 4096, spread_w.size * 4),
+        name="adjoint_step" if adjoint else "mode_step",
+    )(pencil, spread_w, spread, forward, inverse)
+
+
+def pointwise(field, cotangent, pencil, table_t, table, block_weight, bias_row, chips, half):
+    rows, length, width = field.shape
+    chunk = 64
+
+    def kernel(u_ref, c_ref, p_ref, tt_ref, t_ref, w_ref, b_ref, out_ref, dpre_ref, send_ref, bscr, dscr):
+        place = pl.program_id(0)
+
+        @pl.when(place == 0)
+        def _():
+            cut_lanes(bscr, p_ref)
+
+        coeff = gather_rows(bscr, place, chips, half)
+        bias = b_ref[...]
+        root = math.sqrt(2.0 / math.pi)
+        for k in range(length // chunk):
+            where = pl.ds(k * chunk, chunk)
+            u = u_ref[0, where, :]
+            spec = dot(tt_ref[where, :], coeff)
+            for h in range(2):
+                lanes = slice(h * half, (h + 1) * half)
+                pre = spec[:, lanes] + dot(u[:, lanes], w_ref[...]) + bias[:, lanes]
+                square = pre * pre
+                th = jnp.tanh(pre * (root + (root * 0.044715) * square))
+                cdf = 0.5 * th + 0.5
+                out_ref[0, where, lanes] = (pre * cdf).astype(BF16)
+                slope = pre * (root + (3.0 * root * 0.044715) * square)
+                grad = cdf + slope * (0.5 - 0.5 * (th * th))
+                dpre_ref[0, where, lanes] = (c_ref[0, where, lanes].astype(F32) * grad).astype(BF16)
+        scatter_rows(dscr, dot(t_ref[...], dpre_ref[0]), place, chips, half)
+
+        @pl.when(place == rows - 1)
+        def _():
+            join_lanes(send_ref, dscr)
+
+    slab = pl.BlockSpec((1, length, width), lambda i: (i, 0, 0))
+
+    def whole(a):
+        return pl.BlockSpec(a.shape, lambda i: (0,) * a.ndim)
+
+    return pl.pallas_call(
+        kernel,
+        grid=(rows,),
+        in_specs=[slab, slab] + [whole(a) for a in (pencil, table_t, table, block_weight, bias_row)],
+        out_specs=[slab, slab, whole(pencil)],
+        out_shape=[
+            jax.ShapeDtypeStruct(field.shape, BF16),
+            jax.ShapeDtypeStruct(field.shape, BF16),
+            jax.ShapeDtypeStruct(pencil.shape, BF16),
+        ],
+        scratch_shapes=[pltpu.VMEM(cut_shape(pencil.shape), F32), pltpu.VMEM(cut_shape(pencil.shape), F32)],
+        compiler_params=params(),
+        cost_estimate=cost(field.size * 1000, field.size * 8),
+        name="pointwise",
+    )(field, cotangent, pencil, table_t, table, block_weight, bias_row)
+
+
+def local_sums(field, dpre, chans, half):
+    rows, length, width = field.shape
+    slices = half // chans
+
+    def kernel(u_ref, d_ref, out_ref, acc, bacc):
+        place = pl.program_id(0)
+        for h in range(2):
+            lanes = slice(h * half, (h + 1) * half)
+            part = lax.dot_general(
+                u_ref[0, :, lanes], d_ref[0, :, lanes], (((0,), (0,)), ((), ())), preferred_element_type=F32
+            )
+            acc[h] = jnp.where(place == 0, part, acc[h] + part)
+        ones = jnp.ones((16, length), BF16)
+        part = dot(ones, d_ref[0])[0:8]
+        bacc[...] = jnp.where(place == 0, part, bacc[...] + part)
+
+        @pl.when(place == rows - 1)
+        def _():
+            group = lax.broadcasted_iota(jnp.int32, (chans, half), 1) // chans
+            both = acc[0] + acc[1]
+            total = jnp.zeros((chans, half), F32)
+            for p in range(slices):
+                total = jnp.where(group == p, both[p * chans : (p + 1) * chans], total)
+            total = sum(total[:, k * LANES : (k + 1) * LANES] for k in range(half // LANES))
+            bias = sum(bacc[:, k * LANES : (k + 1) * LANES] for k in range(width // LANES))
+            shift = LANES // 2
+            while shift >= chans:
+                total = total + pltpu.roll(total, shift, 1)
+                bias = bias + pltpu.roll(bias, shift, 1)
+                shift //= 2
+            group8 = lax.broadcasted_iota(jnp.int32, (8, LANES), 1) // chans
+            folded = jnp.zeros((8, LANES), F32)
+            for k in range(chans // 8):
+                folded = jnp.where(group8 == k, total[8 * k : 8 * k + 8], folded)
+            value = jnp.concatenate([folded, bias], axis=0)
+            high = value.astype(BF16).astype(F32)
+            mid = (value - high).astype(BF16).astype(F32)
+            low = value - high - mid
+            left = jnp.concatenate([high, mid[0:8]], axis=0)
+            right = jnp.concatenate([mid[8:16], low], axis=0)
+            out_ref[...] = jnp.concatenate([left, right], axis=1).astype(BF16)
+
+    slab = pl.BlockSpec((1, length, width), lambda i: (i, 0, 0))
+    return pl.pallas_call(
+        kernel,
+        grid=(rows,),
+        in_specs=[slab, slab],
+        out_specs=pl.BlockSpec((24, 2 * LANES), lambda i: (0, 0)),
+        out_shape=jax.ShapeDtypeStruct((24, 2 * LANES), BF16),
+        scratch_shapes=[pltpu.VMEM((2, half, half), F32), pltpu.VMEM((8, width), F32)],
+        compiler_params=params(),
+        cost_estimate=cost(field.size * 1000, field.size * 4),
+        name="local_sums",
+    )(field, dpre)
+
+
+def weight_sums(core, spectrum, grads, widen, tile, modes_x, chans):
+    wide = spectrum.shape[1]
+    tiles = wide // LANES
+    groups = LANES // chans
+    parts = widen.shape[0]
+    step = 2 * LANES
+    full = chans * chans
+
+    def kernel(core_ref, u_ref, d_ref, f_ref, h_ref, own_ref, keep_ref, send_ref):
+        def stack(ref):
+            return jnp.concatenate([ref[:, k * LANES : (k + 1) * LANES] for k in range(tiles)], axis=0)
+
+        first = core_ref[0] == 0
+        left = stack(u_ref)
+        right = dot(stack(d_ref), h_ref[...])
+        for a in range(parts):
+            sums = {}
+            for g in range(groups):
+                spread_u = dot(left, f_ref[a, :, g * step : (g + 1) * step])
+                for k in range(tiles):
+                    kind = 0 if k < 2 * tiles // 3 else 1
+                    re = slice(2 * k * modes_x, (2 * k + 1) * modes_x)
+                    im = slice((2 * k + 1) * modes_x, (2 * k + 2) * modes_x)
+                    for z in range(2):
+                        lanes = slice(z * LANES, (z + 1) * LANES)
+                        ur, ui = spread_u[re, lanes], spread_u[im, lanes]
+                        dr = right[re, g * LANES : (g + 1) * LANES]
+                        di = right[im, g * LANES : (g + 1) * LANES]
+                        for t, term in ((0, ur * dr + ui * di), (1, ur * di - ui * dr)):
+                            key = (kind, t, z)
+                            sums[key] = term if key not in sums else sums[key] + term
+            for t in range(2):
+                own = jnp.concatenate([sums[0, t, 0], sums[0, t, 1]], axis=1)
+                own_ref[:, t * full + a * step : t * full + (a + 1) * step] = own.astype(BF16)
+                shared = jnp.concatenate([sums[1, t, 0], sums[1, t, 1]], axis=1)
+                at = t * (full // 2) + (a % (parts // 2)) * step
+                low = a < parts // 2
+
+                @pl.when(first if low else jnp.logical_not(first))
+                def _():
+                    keep_ref[:, at : at + step] = shared
+
+                @pl.when(jnp.logical_not(first) if low else first)
+                def _():
+                    send_ref[:, at : at + step] = shared
+
+    half_shape = jax.ShapeDtypeStruct((modes_x, full), F32)
+    vmem = pl.BlockSpec(memory_space=pltpu.VMEM)
+    return pl.pallas_call(
+        kernel,
+        in_specs=[pl.BlockSpec(memory_space=pltpu.SMEM)] + [vmem] * 4,
+        out_shape=(jax.ShapeDtypeStruct((modes_x, 2 * full), BF16), half_shape, half_shape),
+        compiler_params=params(),
+        cost_estimate=cost(2 * 288 * 128 * 4096, 4 * 1024 * 1024),
+        name="weight_sums",
+    )(core, spectrum, grads, widen, tile)
+
+
+def make_shard(own, keep, other, stats):
+    rows, full2 = own.shape
+    full = keep.shape[1]
+    width = full2 + full + stats.shape[1]
+
+    def kernel(o_ref, k_ref, r_ref, s_ref, out_ref):
+        out_ref[:, 0:full2] = o_ref[...]
+        out_ref[:, full2 : full2 + full] = (k_ref[...] + r_ref[...]).astype(BF16)
+        out_ref[:, full2 + full :] = s_ref[...]
+
+    return pl.pallas_call(
+        kernel,
+        out_shape=jax.ShapeDtypeStruct((rows, width), BF16),
+        compiler_params=params(),
+        name="make_shard",
+    )(own, keep, other, stats)
+
+
+def assemble(owners, shards_all, modes_y, chans, chips):
+    rows = shards_all[0].shape[0]
+    full = chans * chans
+    count = len(shards_all)
+
+    def kernel(owner_ref, *refs):
+        ins, (g_ref, l_ref, b_ref, scr, stat) = refs[:count], refs[count:]
+        for n in range(count):
+            owner = owner_ref[n]
+            chip, core = owner // 2, owner % 2
+            ref = ins[n]
+            own = pl.ds(chip + 2 * chips * core, rows, stride=modes_y)
+            scr_shared = pl.ds(chip + chips, rows, stride=modes_y)
+            for k in range(2 * full // LANES):
+                lanes = slice(k * LANES, (k + 1) * LANES)
+                scr[k, own, :] = ref[:, lanes].astype(F32)
+            for t in range(2):
+                for k in range(full // 2 // LANES):
+                    at = 2 * full + t * (full // 2) + k * LANES
+                    block = t * (full // LANES) + core * (full // 2 // LANES) + k
+                    scr[block, scr_shared, :] = ref[:, at : at + LANES].astype(F32)
+            left = ref[:, 3 * full : 3 * full + LANES].astype(F32)
+            right = ref[:, 3 * full + LANES :].astype(F32)
+            middle = jnp.concatenate([left[16:24], right[0:8]], axis=0)
+            stat[owner] = left[0:16] + middle + right[8:24]
+        for k in range(2 * full // LANES):
+            for j in range(rows):
+                g_ref[j, :, k * LANES : (k + 1) * LANES] = scr[k, j * modes_y : (j + 1) * modes_y, :].astype(BF16)
+        total = stat[0]
+        for n in range(1, count):
+            total = total + stat[n]
+        for k in range(chans // 8):
+            piece = total[0:8] if k == 0 else pltpu.roll(total[0:8], LANES - k * chans, 1)
+            l_ref[8 * k : 8 * k + 8, :] = piece[:, 0:chans]
+        b_ref[...] = total[8:9, 0:chans]
+
+    vmem = pl.BlockSpec(memory_space=pltpu.VMEM)
+    return pl.pallas_call(
+        kernel,
+        in_specs=[pl.BlockSpec(memory_space=pltpu.SMEM)] + [vmem] * count,
+        out_shape=(
+            jax.ShapeDtypeStruct((rows, modes_y, 2 * full), BF16),
+            jax.ShapeDtypeStruct((chans, chans), F32),
+            jax.ShapeDtypeStruct((1, chans), F32),
+        ),
+        scratch_shapes=[
+            pltpu.VMEM((2 * full // LANES, rows * modes_y, LANES), F32),
+            pltpu.VMEM((count, 16, LANES), F32),
+        ],
+        compiler_params=params(),
+        cost_estimate=cost(1000000, 8 * 1024 * 1024),
+        name="assemble",
+    )(owners, *shards_all)
+
+
+def back_to_field(dpre, pencil, table_t, block_weight, chips, half):
+    rows, length, width = dpre.shape
+    chunk = 128
+
+    def kernel(d_ref, p_ref, tt_ref, w_ref, out_ref, bscr):
+        place = pl.program_id(0)
+
+        @pl.when(place == 0)
+        def _():
+            cut_lanes(bscr, p_ref)
+
+        coeff = gather_rows(bscr, place, chips, half)
+        for k in range(length // chunk):
+            where = pl.ds(k * chunk, chunk)
+            d = d_ref[0, where, :]
+            spec = dot(tt_ref[where, :], coeff)
+            for h in range(2):
+                lanes = slice(h * half, (h + 1) * half)
+                out_ref[0, where, lanes] = (spec[:, lanes] + dot(d[:, lanes], w_ref[...])).astype(BF16)
+
+    slab = pl.BlockSpec((1, length, width), lambda i: (i, 0, 0))
+
+    def whole(a):
+        return pl.BlockSpec(a.shape, lambda i: (0,) * a.ndim)
+
+    return pl.pallas_call(
+        kernel,
+        grid=(rows,),
+        in_specs=[slab] + [whole(a) for a in (pencil, table_t, block_weight)],
+        out_specs=slab,
+        out_shape=jax.ShapeDtypeStruct(dpre.shape, BF16),
+        scratch_shapes=[pltpu.VMEM(cut_shape(pencil.shape), F32)],
+        compiler_params=params(),
+        cost_estimate=cost(dpre.size * 500, dpre.size * 4),
+        name="back_to_field",
+    )(dpre, pencil, table_t, block_weight)
+
+
+def exchange(pencil):
+    return lax.all_to_all(pencil, "xy", split_axis=0, concat_axis=0, tiled=True)
+
+
+def ring_order(chips):
+    return [2 * z for z in range(chips // 2)] + [2 * z + 1 for z in reversed(range(chips // 2))]
+
+
+def gather_ring(shard, chips):
+    order = ring_order(chips)
+    me = lax.axis_index("xy")
+    core = me % 2
+    turn = jnp.asarray(np.array(order), jnp.int32)
+    spot = jnp.asarray(np.argsort(np.array(order)), jnp.int32)[me // 2]
+
+    def hop(way):
+        return [
+            (2 * order[i] + c, 2 * order[(i + way) % chips] + c) for i in range(chips) for c in range(2)
+        ]
+
+    swap = [(i, i ^ 1) for i in range(2 * chips)]
+    ahead = back = shard
+    parts, owners = [shard], [me]
+    for step in range(1, chips // 2 + 1):
+        ahead = lax.ppermute(ahead, "xy", hop(1))
+        parts.append(ahead)
+        owners.append(2 * turn[(spot - step) % chips] + core)
+        if step < chips // 2:
+            back = lax.ppermute(back, "xy", hop(-1))
+            parts.append(back)
+            owners.append(2 * turn[(spot + step) % chips] + core)
+    other = [lax.ppermute(p, "xy", swap) for p in parts]
+    owners = owners + [o ^ 1 for o in owners]
+    return jnp.stack(owners).astype(jnp.int32), parts + other
+
+
+def fast_shards(field, spectral_weight, local_weight, bias, cotangent):
+    rows, length_y, width = field.shape
+    chans = local_weight.shape[0]
+    planes = width // chans
+    modes_x, modes_y = spectral_weight.shape[:2]
+    devices = lax.axis_size("xy")
+    chips = devices // 2
+    half = width // 2
+    full = chans * chans
+    me = lax.axis_index("xy")
+    chip, core = me // 2, me % 2
+    table_y = np_ytable(modes_y, length_y, False)
+    table_yw = np_ytable(modes_y, length_y, True)
+    table_y_t, table_yw_t = (np.ascontiguousarray(t.T) for t in (table_y, table_yw))
+    forward, inverse = np_xtables(modes_x, rows * devices)
+    spread, tile, widen = np_spread(chans), np_tile(chans), np_widen(chans)
+
+    send = rows_to_modes(field, table_y, chips, half)
+    pencil = exchange(send)
+
+    mine = [
+        lax.dynamic_index_in_dim(spectral_weight, m, axis=1, keepdims=False)
+        for m in (chip + 2 * chips * core, chip + chips)
+    ]
+    weights = jnp.stack(mine).reshape(2, modes_x, 2, chans, chans).transpose(0, 2, 1, 3, 4)
+    plain = weights.reshape(4 * modes_x, full)
+    turned = weights.swapaxes(3, 4).reshape(4 * modes_x, full)
+    spread_plain = spread_weights(plain, tile)
+    spread_turned = spread_weights(turned, tile)
+
+    eye = jnp.eye(half // chans, dtype=BF16)
+    block = jnp.einsum("pq,co->pcqo", eye, local_weight).reshape(half, half)
+    block_t = block.T
+    bias_row = jnp.tile(bias, planes)[None, :]
+
+    spectrum, send = mode_step(pencil, spread_plain, spread, forward, inverse, modes_x, False)
+    pencil = exchange(send)
+    output_field, dpre, send = pointwise(
+        field, cotangent, pencil, table_yw_t, table_yw, block, bias_row, chips, half
+    )
+    pencil = exchange(send)
+    stats = local_sums(field, dpre, chans, half)
+    grads, send = mode_step(pencil, spread_turned, spread, forward, inverse, modes_x, True)
+    core_id = core.astype(jnp.int32)[None]
+    own, keep, give = weight_sums(core_id, spectrum, grads, widen, tile, modes_x, chans)
+    got = lax.ppermute(give, "xy", [(i, i ^ 1) for i in range(devices)])
+    shard = make_shard(own, keep, got, stats)
+    owners, parts = gather_ring(shard, chips)
+    pencil = exchange(send)
+    field_grad = back_to_field(dpre, pencil, table_y_t, block_t, chips, half)
+    spectral_grad, local_grad, bias_grad = assemble(owners, parts, modes_y, chans, chips)
+    return output_field, field_grad, spectral_grad, local_grad, bias_grad.reshape(chans)
+
+
+def fits(field, spectral_weight, local_weight, devices):
+    rows, length_y, width = field.shape
+    chans = local_weight.shape[0]
+    modes_x, modes_y = spectral_weight.shape[:2]
+    return (
+        rows == 4
+        and chans == 32
+        and width == 512
+        and length_y % 128 == 0
+        and modes_x == 24
+        and devices == 16
+        and 2 * modes_y == 3 * devices
+    )
+
+
+def shards(field, spectral_weight, local_weight, bias, cotangent):
+    if fits(field, spectral_weight, local_weight, lax.axis_size("xy")):
+        return fast_shards(field, spectral_weight, local_weight, bias, cotangent)
+    return general_shards(field, spectral_weight, local_weight, bias, cotangent)
+
+
 def solution(mesh):
     return jax.shard_map(
         shards,

time: 601 us -> 121 us (0.20)
  blocking collectives: 401 us -> 0 us
  local copies, waits for them, and re-layouts: 91.1 us -> 32.1 us
  matrix products: 54.6 us -> 0 us
  Pallas kernels: 0 us -> 23.2 us
  waiting for transfers between devices: 1.09 us -> 19.6 us
  other arithmetic: 18.4 us -> 0.91 us
  between operations: 1.45 us -> 10.2 us
  starting transfers between devices: 25.4 us -> 33 us
    psum x1 -> x0, blocking collectives: 401 us -> none  [shards(): lax.psum((partial_grad, weight_part, bias_part), 'xy')]
    dot_general x20 -> x0, matrix products: 54.6 us -> none  [the longest x19 39 us: mult(): return jnp.einsum(form, left, right, preferred_element_type=jnp.float32)]
    convert_element_type x5 -> x0, local copies, waits for them, and re-layouts: 28.5 us -> none  [the longest x2 23.5 us: shards(): total.reshape(modes_x, modes_y, 2 * chans * chans).astype(jnp.bfloat16)]
    pallas_call x0 -> x11, Pallas kernels: none -> 23.2 us  [the longest x1 6.74 us: pointwise(): pl.pallas_call(kernel, grid=(rows,), in_specs=[slab, slab] + [whole(a) fo...]
    reshape x15 -> x4, local copies, waits for them, and re-layouts: 18.7 us -> 5 us  [the longest x1 2.65 us: fast_shards(): turned = weights.swapaxes(3, 4).reshape(4 * modes_x, full)]
    ppermute x0 -> x16, waiting for transfers between devices: none -> 13 us  [the longest x4 7.56 us: gather_ring(): ahead = lax.ppermute(ahead, 'xy', hop(1))]
    squeeze x1 -> x0, local copies, waits for them, and re-layouts: 10.3 us -> none  [mix_modes(): weights[:, :, 1]]
    another operation x11 -> x1, other arithmetic: 9.72 us -> 0.01 us  [the longest x1 7.73 us: pair_grad(): return jnp.stack([real_part, imag_part], axis=2)]
  transfers between devices with their start and end apart: 4 -> 20, of which waited for: 1 -> 5; matrix products, arithmetic and copies ran while one was open for 17% -> 13% of each run, Pallas kernels for 0% -> 5%
where the time goes in v1:
time: 121 us; the launch traced here: 119 us
  starting transfers between devices  33 us (27%)
  local copies, waits for them, and re-layouts  32.1 us (27%)
  Pallas kernels  23.2 us (19%)
  waiting for transfers between devices  19.6 us (16%)
  between operations  10.2 us (8%)
    all_to_all x4, starting transfers between devices, exchange(): return lax.all_to_all(pencil, 'xy', split_axis=0, concat_axis=0, tiled=True)  24.4 us
    unnamed x62, local copies, waits for them, and re-layouts  18.1 us
    ppermute x4, waiting for transfers between devices, gather_ring(): ahead = lax.ppermute(ahead, 'xy', hop(1))  7.56 us
    pallas_call x1, Pallas kernels, pointwise(): pl.pallas_call(kernel, grid=(rows,), in_specs=[slab, slab] + [whole(a) fo...  6.74 us
    all_to_all x4, waiting for transfers between devices, exchange(): return lax.all_to_all(pencil, 'xy', split_axis=0, concat_axis=0, tiled=True)  6.51 us
    ppermute x3, waiting for transfers between devices, gather_ring(): back = lax.ppermute(back, 'xy', hop(-1))  5.46 us
    ppermute x3, starting transfers between devices, gather_ring(): back = lax.ppermute(back, 'xy', hop(-1))  4.49 us
    pallas_call x2, Pallas kernels, mode_step(): pl.pallas_call(kernel, out_shape=(jax.ShapeDtypeStruct((2 * modes_x, wide...  4.08 us
  transfers between devices with their start and end apart: 20, of which 5 were waited for; matrix products, arithmetic and copies ran while one was open for 13% of the time, Pallas kernels for 5%

profile of v1, /device:TPU:1, one launch (start us, length us, event | category | flops | bytes accessed | tf_op | source)
XLA Modules:
  0.0 118.9 jit_solution(9196529569079771161)
XLA Ops:
  0.6 1.6 %copy-done = bf16[4,512,512]{2,1,0:T(8,128)(2,1)S(1)} copy-done((bf16[4,512,512]{2,1,0:T(8,128)(2,1)S(1)}, bf16[4,512,512]{2,1,0:T(8,128)(2,1)}, u32[]{:S(2)}) %copy-start) | copy-done | bytes 2097176
  2.2 0.8 copy-done.25
  3.0 1.7 %rows_to_modes.1 = bf16[128,768]{1,0:T(8,128)(2,1)} custom-call(bf16[4,512,512]{2,1,0:T(8,128)(2,1)S(1)} %copy-done, bf16[48,512]{1,0:T(8,128)(2,1)S(1)} %copy-done.25), custom_call_target="tpu_custom_call" | custom-call | flops 100663296 | bytes 2097152 | tf_op jit(solution)/shard_map/rows_to_modes/pallas_call | solution.py:294
  4.7 7.3 %all-to-all-start = ((bf16[16,8,768]{2,1,0:T(8,128)(2,1)}), bf16[16,8,768]{2,1,0:T(8,128)(2,1)S(1)}, u32[]{:S(2)}, u32[]{:S(2)}) async-start(bf16[16,8,768]{2,1,0:T(8,128)(2,1)} %bitcast), calls=%async_computation | async-start | bytes 393216 | tf_op jit(solution)/shard_map/all_to_all | solution.py:655
  12.0 2.6 %dynamic-slice_reduce_fusion = (bf16[24,2048]{1,0:T(8,128)(2,1)S(1)}, bf16[24,2048]{1,0:T(8,128)(2,1)S(1)}) fusion(bf16[24,24,2048]{2,1,0:T(8,128)(2,1)} %param.17, s32[]{:T(128)S(6)} %select_n.76, s32[]{:T(128)S(6)} %select_n.75), kind=kLoop, calls=%fused_computation.1 | loop fusion | bytes 393224 | tf_op jit(solution)/shard_map/jit(dynamic_index_in_dim)/dynamic_slice | solution.py:711
  14.6 0.2 stack.61
  14.9 0.2 stack.60
  15.1 0.8 constant_dynamic-update-slice_fusion.1
  15.9 0.8 constant_dynamic-update-slice_fusion
  16.7 1.3 %copy.24 = bf16[2,2,24,32,32]{4,3,2,1,0:T(8,128)(2,1)S(1)} copy(bf16[2,2,24,32,32]{4,3,1,2,0:T(8,128)(2,1)} %bitcast.2) | data formatting | bytes 393216 | tf_op jit(solution)/shard_map/transpose | solution.py:714
  18.0 0.8 reshape.66.w_ref
  18.8 0.4 spread_weights.2.w_ref
  19.2 1.1 copy-done.7
  20.4 0.7 copy-done.12
  21.0 1.4 %copy-done.8 = f32[8,96,512]{2,1,0:T(8,128)S(1)} copy-done((f32[8,96,512]{2,1,0:T(8,128)S(1)}, f32[8,96,512]{2,1,0:T(8,128)}, u32[]{:S(2)}) %copy-start.8) | copy-done | bytes 1572888
  22.5 0.9 copy-done.13
  23.4 1.1 mode_step.1
  24.6 0.7 copy-done.15
  25.2 6.0 %all-to-all-start.1 = ((bf16[16,8,768]{2,1,0:T(8,128)(2,1)}), bf16[16,8,768]{2,1,0:T(8,128)(2,1)}, u32[]{:S(2)}, u32[]{:S(2)}) async-start(bf16[16,8,768]{2,1,0:T(8,128)(2,1)} %bitcast.56), calls=%async_computation.1 | async-start | bytes 393216 | tf_op jit(solution)/shard_map/all_to_all | solution.py:655
  31.2 0.1 copy.25
  31.3 0.1 broadcast_in_dim_tile.3.b_ref
  31.4 0.9 multiply_bitcast_fusion
  32.3 1.4 %reshape.67 = bf16[256,256]{0,1:T(8,128)(2,1)S(1)} reshape(bf16[8,32,8,32]{1,0,3,2:T(8,128)(2,1)} %multiply_bitcast_fusion) | data formatting | bytes 262144 | tf_op jit(solution)/shard_map/reshape | solution.py:721
  33.7 0.1 copy.26.w_ref
  33.9 5.8 %all-to-all-done.1 = bf16[16,8,768]{2,1,0:T(8,128)(2,1)} async-done(((bf16[16,8,768]{2,1,0:T(8,128)(2,1)}), bf16[16,8,768]{2,1,0:T(8,128)(2,1)}, u32[]{:S(2)}, u32[]{:S(2)}) %all-to-all-start.1) | async-done | bytes 196640 | tf_op jit(solution)/shard_map/all_to_all | solution.py:655
  39.6 0.9 copy-done.20
  40.5 0.8 copy-done.23
  41.3 6.7 %pointwise.1 = (bf16[4,512,512]{2,1,0:T(8,128)(2,1)}, bf16[4,512,512]{2,1,0:T(8,128)(2,1)S(1)}, bf16[128,768]{1,0:T(8,128)(2,1)S(1)}) custom-call(bf16[4,512,512]{2,1,0:T(8,128)(2,1)S(1)} %copy-done.1, bf16[4,512,512]{2,1,0:T(8,128)(2,1)} %c_ref.1, bf16[128,768]{1,0:T(8,128)(2,1)} %bitcast.4.p_ref, bf16[512,48]{1,0:T(8,128)(2,1)S(1)} %copy-done.20, ...), custom_call_target="tpu_custom_call" | custom-call | flops 1048576000 | bytes 8388608 | tf_op jit(solution)/shard_map/pointwise/pallas_call | solution.py:412
  48.1 1.3 %copy-done.2 = bf16[4,512,512]{2,1,0:T(8,128)(2,1)} copy-done((bf16[4,512,512]{2,1,0:T(8,128)(2,1)}, bf16[4,512,512]{2,1,0:T(8,128)(2,1)S(1)}, u32[]{:S(2)}) %copy-start.2) | copy-done | bytes 2097176
  49.4 0.7 copy-done.16
  50.1 4.7 %all-to-all-start.2 = ((bf16[16,8,768]{2,1,0:T(8,128)(2,1)}), bf16[16,8,768]{2,1,0:T(8,128)(2,1)}, u32[]{:S(2)}, u32[]{:S(2)}) async-start(bf16[16,8,768]{2,1,0:T(8,128)(2,1)} %bitcast.57), calls=%async_computation.2 | async-start | bytes 393216 | tf_op jit(solution)/shard_map/all_to_all | solution.py:655
  54.8 2.3 %copy.27 = bf16[2,2,24,32,32]{4,3,2,1,0:T(8,128)(2,1)} copy(bf16[2,2,24,32,32]{3,4,1,2,0:T(8,128)(2,1)} %bitcast.8) | data formatting | bytes 393216 | tf_op jit(solution)/shard_map/transpose;transpose | solution.py:716
  57.1 2.6 %reshape.68.w_ref = bf16[96,1024]{1,0:T(8,128)(2,1)} reshape(bf16[2,2,24,32,32]{4,3,2,1,0:T(8,128)(2,1)} %copy.27) | data formatting | bytes 393216 | tf_op jit(solution)/shard_map/reshape | solution.py:716
  59.8 0.9 copy-done.14
  60.7 0.4 spread_weights.3.w_ref
  61.0 1.1 copy-done.5
  62.2 0.7 all-to-all-done.2
  62.9 1.4 %copy-done.6 = f32[8,96,512]{2,1,0:T(8,128)S(1)} copy-done((f32[8,96,512]{2,1,0:T(8,128)S(1)}, f32[8,96,512]{2,1,0:T(8,128)}, u32[]{:S(2)}) %copy-start.6) | copy-done | bytes 1572888
  64.3 2.9 %adjoint_step.1 = (bf16[48,768]{1,0:T(8,128)(2,1)S(1)}, bf16[128,768]{1,0:T(8,128)(2,1)}) custom-call(bf16[128,768]{1,0:T(8,128)(2,1)} %bitcast.7.p_ref, f32[8,96,512]{2,1,0:T(8,128)S(1)} %copy-done.6, bf16[128,4096]{1,0:T(8,128)(2,1)S(1)} %copy-done.9, bf16[48,128]{1,0:T(8,128)(2,1)S(1)} %copy-done.24, bf16[128,48]{1,0:T(8,128)(2,1)S(1)} %copy-done.18), custom_call_target="tpu_custom_call" | custom-call | flops 301989888 | bytes 1572864 | tf_op jit(solution)/shard_map/adjoint_step/pallas_call | solution.py:361
  67.2 1.2 %copy-done.11 = bf16[4,128,1024]{2,1,0:T(8,128)(2,1)S(1)} copy-done((bf16[4,128,1024]{2,1,0:T(8,128)(2,1)S(1)}, bf16[4,128,1024]{2,1,0:T(8,128)(2,1)}, u32[]{:S(2)}) %copy-start.11) | copy-done | bytes 1048600
  68.5 1.4 %weight_sums.1 = (bf16[24,2048]{1,0:T(8,128)(2,1)S(1)}, f32[24,1024]{1,0:T(8,128)S(1)}, f32[24,1024]{1,0:T(8,128)S(1)}) custom-call(s32[1]{0:T(128)} %bitcast.42.core_ref, bf16[48,768]{1,0:T(8,128)(2,1)S(1)} %copy-done.22, bf16[48,768]{1,0:T(8,128)(2,1)S(1)} %get-tuple-element.24.d_ref, bf16[4,128,1024]{2,1,0:T(8,128)(2,1)S(1)} %copy-done.11, ...), custom_call_target="tpu_custom_call" | custom-call | flops 301989888 | bytes 4194304 | tf_op jit(solution)/shard_map/weight_sums/pallas_call | solution.py:533
  69.9 1.3 %collective-permute-start = (f32[24,1024]{1,0:T(8,128)S(1)}, f32[24,1024]{1,0:T(8,128)S(1)}, u32[]{:S(2)}, u32[]{:S(2)}) collective-permute-start(f32[24,1024]{1,0:T(8,128)S(1)} %get-tuple-element.27), channel_id=1, source_target_pairs={{0,1},{1,0},{2,3},{3,2},{4,5},{5,4},{6,7},{7,6},{8,9},{9,8},{10,11... | collective-permute-start | bytes 294920 | tf_op jit(solution)/shard_map/ppermute | solution.py:735
  71.1 1.8 %local_sums.1.s_ref = bf16[24,256]{1,0:T(8,128)(2,1)S(1)} custom-call(bf16[4,512,512]{2,1,0:T(8,128)(2,1)S(1)} %copy-done.1, bf16[4,512,512]{2,1,0:T(8,128)(2,1)S(1)} %copy-done.3), custom_call_target="tpu_custom_call" | custom-call | flops 1048576000 | bytes 4194304 | tf_op jit(solution)/shard_map/local_sums/pallas_call | solution.py:472
  72.9 0.1 collective-permute-start.1
  73.0 1.5 %collective-permute-start.2 = (bf16[24,3328]{1,0:T(8,128)(2,1)S(1)}, bf16[24,3328]{1,0:T(8,128)(2,1)S(1)}, u32[]{:S(2)}, u32[]{:S(2)}) collective-permute-start(bf16[24,3328]{1,0:T(8,128)(2,1)S(1)} %make_shard.1.refs_0_), channel_id=1, source_target_pairs={{0,2},{1,3},{4,0},{5,1},{8,4},{9,5},{12,8},{13,9},{14,12},{15,13},... | collective-permute-start | bytes 479240 | tf_op jit(solution)/shard_map/ppermute | solution.py:682
  74.4 4.2 %collective-permute-done.1.refs_1_ = bf16[24,3328]{1,0:T(8,128)(2,1)S(1)} collective-permute-done((bf16[24,3328]{1,0:T(8,128)(2,1)S(1)}, bf16[24,3328]{1,0:T(8,128)(2,1)S(1)}, u32[]{:S(2)}, u32[]{:S(2)}) %collective-permute-start.1) | collective-permute-done | bytes 159776 | tf_op jit(solution)/shard_map/ppermute | solution.py:678
  78.7 1.5 %collective-permute-start.4 = (bf16[24,3328]{1,0:T(8,128)(2,1)S(1)}, bf16[24,3328]{1,0:T(8,128)(2,1)S(1)}, u32[]{:S(2)}, u32[]{:S(2)}) collective-permute-start(bf16[24,3328]{1,0:T(8,128)(2,1)S(1)} %collective-permute-done.2.refs_2_), channel_id=1, source_target_pairs={{0,2},{1,3},{4,0},{5,1},{8,4},{9,5},{12,8},{13,9},{14,12},{15,13},... | collective-permute-start | bytes 479240 | tf_op jit(solution)/shard_map/ppermute | solution.py:682
  80.1 3.3 %collective-permute-done.3.refs_3_ = bf16[24,3328]{1,0:T(8,128)(2,1)S(1)} collective-permute-done((bf16[24,3328]{1,0:T(8,128)(2,1)S(1)}, bf16[24,3328]{1,0:T(8,128)(2,1)S(1)}, u32[]{:S(2)}, u32[]{:S(2)}) %collective-permute-start.3) | collective-permute-done | bytes 159776 | tf_op jit(solution)/shard_map/ppermute | solution.py:678
  83.5 6.4 %all-to-all-start.3 = ((bf16[16,8,768]{2,1,0:T(8,128)(2,1)}), bf16[16,8,768]{2,1,0:T(8,128)(2,1)S(1)}, u32[]{:S(2)}, u32[]{:S(2)}) async-start(bf16[16,8,768]{2,1,0:T(8,128)(2,1)} %bitcast.9), calls=%async_computation.3 | async-start | bytes 393216 | tf_op jit(solution)/shard_map/all_to_all | solution.py:655
  89.8 0.2 collective-permute-start.8
  90.0 0.3 collective-permute-start.10
  90.3 0.2 collective-permute-start.9
  90.5 1.6 %collective-permute-start.6 = (bf16[24,3328]{1,0:T(8,128)(2,1)S(1)}, bf16[24,3328]{1,0:T(8,128)(2,1)S(1)}, u32[]{:S(2)}, u32[]{:S(2)}) collective-permute-start(bf16[24,3328]{1,0:T(8,128)(2,1)S(1)} %collective-permute-done.4.refs_4_), channel_id=1, source_target_pairs={{0,2},{1,3},{4,0},{5,1},{8,4},{9,5},{12,8},{13,9},{14,12},{15,13},... | collective-permute-start | bytes 479240 | tf_op jit(solution)/shard_map/ppermute | solution.py:682
  92.2 0.7 collective-permute-start.12
  92.9 0.1 collective-permute-start.11
  93.0 0.4 collective-permute-start.13
  93.4 5.5 %collective-permute-done.6.refs_6_ = bf16[24,3328]{1,0:T(8,128)(2,1)S(1)} collective-permute-done((bf16[24,3328]{1,0:T(8,128)(2,1)S(1)}, bf16[24,3328]{1,0:T(8,128)(2,1)S(1)}, u32[]{:S(2)}, u32[]{:S(2)}) %collective-permute-start.6) | collective-permute-done | bytes 159776 | tf_op jit(solution)/shard_map/ppermute | solution.py:682
  98.9 0.8 collective-permute-start.14
  99.7 0.7 dynamic_slice.33
  105.2 0.7 fusion.1
  110.3 0.1 stack.79.owner_ref
  110.5 1.6 %copy-done.4 = bf16[4,512,512]{2,1,0:T(8,128)(2,1)S(1)} copy-done((bf16[4,512,512]{2,1,0:T(8,128)(2,1)S(1)}, bf16[4,512,512]{2,1,0:T(8,128)(2,1)}, u32[]{:S(2)}) %copy-start.4) | copy-done | bytes 2097176
  112.0 3.0 %back_to_field.1 = bf16[4,512,512]{2,1,0:T(8,128)(2,1)} custom-call(bf16[4,512,512]{2,1,0:T(8,128)(2,1)S(1)} %copy-done.4, bf16[128,768]{1,0:T(8,128)(2,1)S(1)} %bitcast.54, bf16[512,48]{1,0:T(8,128)(2,1)S(1)} %copy-done.19, bf16[256,256]{1,0:T(8,128)(2,1)S(1)} %bitcast.53), custom_call_target="tpu_custom_call" | custom-call | flops 524288000 | bytes 4194304 | tf_op jit(solution)/shard_map/back_to_field/pallas_call | solution.py:641
  115.0 3.9 %assemble.1 = (bf16[24,24,2048]{2,1,0:T(8,128)(2,1)}, f32[32,32]{1,0:T(8,128)}, f32[1,32]{1,0:T(1,128)}) custom-call(s32[16]{0:T(128)S(1)} %stack.79.owner_ref, bf16[24,3328]{1,0:T(8,128)(2,1)S(1)} %make_shard.1.refs_0_, bf16[24,3328]{1,0:T(8,128)(2,1)S(1)} %collective-permute-done.1.refs_1_, bf16[24,3328]{1,0:T(8,128)(2,1)S(1)} %collective-permute-done.2.refs_2_, ...), custom_call_target="tpu_custom_call" | custom-call | flops 1000000 | bytes 8388608 | tf_op jit(solution)/shard_map/assemble/pallas_call | solution.py:598
  (66 shorter events, 0.3 us)
Async XLA Ops:
  0.6 1.6 %copy-start = (bf16[4,512,512]{2,1,0:T(8,128)(2,1)S(1)}, bf16[4,512,512]{2,1,0:T(8,128)(2,1)}, u32[]{:S(2)}) copy-start(bf16[4,512,512]{2,1,0:T(8,128)(2,1)} %u_ref.5) | copy-start | bytes 6291460
  2.2 0.8 copy-start.25
  4.7 15.7 %all-to-all-start = ((bf16[16,8,768]{2,1,0:T(8,128)(2,1)}), bf16[16,8,768]{2,1,0:T(8,128)(2,1)S(1)}, u32[]{:S(2)}, u32[]{:S(2)}) async-start(bf16[16,8,768]{2,1,0:T(8,128)(2,1)} %bitcast), calls=%async_computation | async-start | bytes 393216 | tf_op jit(solution)/shard_map/all_to_all | solution.py:655
  15.1 3.7 %copy-start.10 = (bf16[128,512]{1,0:T(8,128)(2,1)S(1)}, bf16[128,512]{1,0:T(8,128)(2,1)}, u32[]{:S(2)}) copy-start(bf16[128,512]{1,0:T(8,128)(2,1)} %constant.129.clone.t_ref.h_ref) | copy-start | bytes 393220
  16.7 4.4 %copy-start.9 = (bf16[128,4096]{1,0:T(8,128)(2,1)S(1)}, bf16[128,4096]{1,0:T(8,128)(2,1)}, u32[]{:S(2)}) copy-start(bf16[128,4096]{1,0:T(8,128)(2,1)} %constant.130.clone.e_ref) | copy-start | bytes 3145732
  16.7 4.4 %copy-start.17 = (bf16[128,48]{1,0:T(8,128)(2,1)S(1)}, bf16[128,48]{1,0:T(8,128)(2,1)}, u32[]{:S(2)}) copy-start(bf16[128,48]{1,0:T(8,128)(2,1)} %constant.132.clone.i_ref) | copy-start | bytes 36868
  16.7 4.4 %copy-start.24 = (bf16[48,128]{1,0:T(8,128)(2,1)S(1)}, bf16[48,128]{1,0:T(8,128)(2,1)}, u32[]{:S(2)}) copy-start(bf16[48,128]{1,0:T(8,128)(2,1)} %constant.131.clone.f_ref) | copy-start | bytes 36868
  18.8 12.4 %copy-start.27 = (bf16[32,32]{1,0:T(8,128)(2,1)S(1)}, bf16[32,32]{1,0:T(8,128)(2,1)}, u32[]{:S(2)}) copy-start(bf16[32,32]{1,0:T(8,128)(2,1)} %param.18) | copy-start | bytes 6148
  19.2 1.1 copy-start.7
  20.3 11.0 %copy-start.28 = (f32[32]{0:T(128)S(1)}, f32[32]{0:T(128)}, u32[]{:S(2)}) copy-start(f32[32]{0:T(128)} %param.19) | copy-start | bytes 388
  20.4 0.7 copy-start.12
  21.0 1.4 %copy-start.8 = (f32[8,96,512]{2,1,0:T(8,128)S(1)}, f32[8,96,512]{2,1,0:T(8,128)}, u32[]{:S(2)}) copy-start(f32[8,96,512]{2,1,0:T(8,128)} %copy-done.7) | copy-start | bytes 4718596
  22.5 0.9 copy-start.13
  23.4 16.3 %copy-start.1 = (bf16[4,512,512]{2,1,0:T(8,128)(2,1)S(1)}, bf16[4,512,512]{2,1,0:T(8,128)(2,1)}, u32[]{:S(2)}) copy-start(bf16[4,512,512]{2,1,0:T(8,128)(2,1)} %u_ref.5) | copy-start | bytes 6291460
  24.5 0.7 copy-start.15
  24.5 6.9 %copy-start.21 = (bf16[48,768]{1,0:T(8,128)(2,1)}, bf16[48,768]{1,0:T(8,128)(2,1)S(1)}, u32[]{:S(2)}) copy-start(bf16[48,768]{1,0:T(8,128)(2,1)S(1)} %get-tuple-element.23.u_ref) | copy-start | bytes 221188
  25.2 14.4 %all-to-all-start.1 = ((bf16[16,8,768]{2,1,0:T(8,128)(2,1)}), bf16[16,8,768]{2,1,0:T(8,128)(2,1)}, u32[]{:S(2)}, u32[]{:S(2)}) async-start(bf16[16,8,768]{2,1,0:T(8,128)(2,1)} %bitcast.56), calls=%async_computation.1 | async-start | bytes 393216 | tf_op jit(solution)/shard_map/all_to_all | solution.py:655
  39.6 0.9 copy-start.20
  40.5 0.8 copy-start.23
  48.1 1.3 %copy-start.2 = (bf16[4,512,512]{2,1,0:T(8,128)(2,1)}, bf16[4,512,512]{2,1,0:T(8,128)(2,1)S(1)}, u32[]{:S(2)}) copy-start(bf16[4,512,512]{2,1,0:T(8,128)(2,1)S(1)} %get-tuple-element.20.d_ref) | copy-start | bytes 6291460
  49.4 0.7 copy-start.16
  50.1 12.8 %all-to-all-start.2 = ((bf16[16,8,768]{2,1,0:T(8,128)(2,1)}), bf16[16,8,768]{2,1,0:T(8,128)(2,1)}, u32[]{:S(2)}, u32[]{:S(2)}) async-start(bf16[16,8,768]{2,1,0:T(8,128)(2,1)} %bitcast.57), calls=%async_computation.2 | async-start | bytes 393216 | tf_op jit(solution)/shard_map/all_to_all | solution.py:655
  54.8 8.1 %copy-start.18 = (bf16[128,48]{1,0:T(8,128)(2,1)S(1)}, bf16[128,48]{1,0:T(8,128)(2,1)}, u32[]{:S(2)}) copy-start(bf16[128,48]{1,0:T(8,128)(2,1)} %constant.132.clone.i_ref) | copy-start | bytes 36868
  59.7 0.9 copy-start.14
  60.7 6.6 %copy-start.22 = (bf16[48,768]{1,0:T(8,128)(2,1)S(1)}, bf16[48,768]{1,0:T(8,128)(2,1)}, u32[]{:S(2)}) copy-start(bf16[48,768]{1,0:T(8,128)(2,1)} %copy-done.21) | copy-start | bytes 221188
  61.0 1.1 copy-start.5
  62.9 1.4 %copy-start.6 = (f32[8,96,512]{2,1,0:T(8,128)S(1)}, f32[8,96,512]{2,1,0:T(8,128)}, u32[]{:S(2)}) copy-start(f32[8,96,512]{2,1,0:T(8,128)} %copy-done.5) | copy-start | bytes 4718596
  64.3 6.8 %copy-start.3 = (bf16[4,512,512]{2,1,0:T(8,128)(2,1)S(1)}, bf16[4,512,512]{2,1,0:T(8,128)(2,1)}, u32[]{:S(2)}) copy-start(bf16[4,512,512]{2,1,0:T(8,128)(2,1)} %copy-done.2) | copy-start | bytes 6291460
  67.2 1.2 %copy-start.11 = (bf16[4,128,1024]{2,1,0:T(8,128)(2,1)S(1)}, bf16[4,128,1024]{2,1,0:T(8,128)(2,1)}, u32[]{:S(2)}) copy-start(bf16[4,128,1024]{2,1,0:T(8,128)(2,1)} %constant.135.clone.f_ref) | copy-start | bytes 3145732
  69.9 3.0 %collective-permute-start = (f32[24,1024]{1,0:T(8,128)S(1)}, f32[24,1024]{1,0:T(8,128)S(1)}, u32[]{:S(2)}, u32[]{:S(2)}) collective-permute-start(f32[24,1024]{1,0:T(8,128)S(1)} %get-tuple-element.27), channel_id=1, source_target_pairs={{0,1},{1,0},{2,3},{3,2},{4,5},{5,4},{6,7},{7,6},{8,9},{9,8},{10,11... | collective-permute-start | bytes 294920 | tf_op jit(solution)/shard_map/ppermute | solution.py:735
  71.1 28.6 %copy-start.29 = (s32[8]{0:T(128)S(1)}, s32[8]{0:T(128)}, u32[]{:S(2)}) copy-start(s32[8]{0:T(128)} %constant.137.clone) | copy-start | bytes 100
  71.1 34.1 %copy-start.26 = (s32[8]{0:T(128)S(1)}, s32[8]{0:T(128)}, u32[]{:S(2)}) copy-start(s32[8]{0:T(128)} %constant.136.clone) | copy-start | bytes 100
  71.1 39.3 %copy-start.19 = (bf16[512,48]{1,0:T(8,128)(2,1)S(1)}, bf16[512,48]{1,0:T(8,128)(2,1)}, u32[]{:S(2)}) copy-start(bf16[512,48]{1,0:T(8,128)(2,1)} %constant.138.clone.tt_ref) | copy-start | bytes 147460
  72.9 5.7 %collective-permute-start.1 = (bf16[24,3328]{1,0:T(8,128)(2,1)S(1)}, bf16[24,3328]{1,0:T(8,128)(2,1)S(1)}, u32[]{:S(2)}, u32[]{:S(2)}) collective-permute-start(bf16[24,3328]{1,0:T(8,128)(2,1)S(1)} %make_shard.1.refs_0_), channel_id=1, source_target_pairs={{0,4},{1,5},{4,8},{5,9},{8,12},{9,13},{12,14},{13,15},{14,10},{15,... | collective-permute-start | bytes 479240 | tf_op jit(solution)/shard_map/ppermute | solution.py:678
  73.0 5.7 %collective-permute-start.2 = (bf16[24,3328]{1,0:T(8,128)(2,1)S(1)}, bf16[24,3328]{1,0:T(8,128)(2,1)S(1)}, u32[]{:S(2)}, u32[]{:S(2)}) collective-permute-start(bf16[24,3328]{1,0:T(8,128)(2,1)S(1)} %make_shard.1.refs_0_), channel_id=1, source_target_pairs={{0,2},{1,3},{4,0},{5,1},{8,4},{9,5},{12,8},{13,9},{14,12},{15,13},... | collective-permute-start | bytes 479240 | tf_op jit(solution)/shard_map/ppermute | solution.py:682
  78.7 4.8 %collective-permute-start.3 = (bf16[24,3328]{1,0:T(8,128)(2,1)S(1)}, bf16[24,3328]{1,0:T(8,128)(2,1)S(1)}, u32[]{:S(2)}, u32[]{:S(2)}) collective-permute-start(bf16[24,3328]{1,0:T(8,128)(2,1)S(1)} %collective-permute-done.1.refs_1_), channel_id=1, source_target_pairs={{0,4},{1,5},{4,8},{5,9},{8,12},{9,13},{12,14},{13,15},{14,10},{15,... | collective-permute-start | bytes 479240 | tf_op jit(solution)/shard_map/ppermute | solution.py:678
  78.7 11.8 %collective-permute-start.4 = (bf16[24,3328]{1,0:T(8,128)(2,1)S(1)}, bf16[24,3328]{1,0:T(8,128)(2,1)S(1)}, u32[]{:S(2)}, u32[]{:S(2)}) collective-permute-start(bf16[24,3328]{1,0:T(8,128)(2,1)S(1)} %collective-permute-done.2.refs_2_), channel_id=1, source_target_pairs={{0,2},{1,3},{4,0},{5,1},{8,4},{9,5},{12,8},{13,9},{14,12},{15,13},... | collective-permute-start | bytes 479240 | tf_op jit(solution)/shard_map/ppermute | solution.py:682
  83.5 8.6 %collective-permute-start.5 = (bf16[24,3328]{1,0:T(8,128)(2,1)S(1)}, bf16[24,3328]{1,0:T(8,128)(2,1)S(1)}, u32[]{:S(2)}, u32[]{:S(2)}) collective-permute-start(bf16[24,3328]{1,0:T(8,128)(2,1)S(1)} %collective-permute-done.3.refs_3_), channel_id=1, source_target_pairs={{0,4},{1,5},{4,8},{5,9},{8,12},{9,13},{12,14},{13,15},{14,10},{15,... | collective-permute-start | bytes 479240 | tf_op jit(solution)/shard_map/ppermute | solution.py:678
  83.5 27.0 %all-to-all-start.3 = ((bf16[16,8,768]{2,1,0:T(8,128)(2,1)}), bf16[16,8,768]{2,1,0:T(8,128)(2,1)S(1)}, u32[]{:S(2)}, u32[]{:S(2)}) async-start(bf16[16,8,768]{2,1,0:T(8,128)(2,1)} %bitcast.9), calls=%async_computation.3 | async-start | bytes 393216 | tf_op jit(solution)/shard_map/all_to_all | solution.py:655
  89.8 2.3 %collective-permute-start.8 = (bf16[24,3328]{1,0:T(8,128)(2,1)S(1)}, bf16[24,3328]{1,0:T(8,128)(2,1)S(1)}, u32[]{:S(2)}, u32[]{:S(2)}) collective-permute-start(bf16[24,3328]{1,0:T(8,128)(2,1)S(1)} %make_shard.1.refs_0_), channel_id=1, source_target_pairs={{0,1},{1,0},{2,3},{3,2},{4,5},{5,4},{6,7},{7,6},{8,9},{9,8},{10,11... | collective-permute-start | bytes 479240 | tf_op jit(solution)/shard_map/ppermute | solution.py:685
  90.0 2.9 %collective-permute-start.10 = (bf16[24,3328]{1,0:T(8,128)(2,1)S(1)}, bf16[24,3328]{1,0:T(8,128)(2,1)S(1)}, u32[]{:S(2)}, u32[]{:S(2)}) collective-permute-start(bf16[24,3328]{1,0:T(8,128)(2,1)S(1)} %collective-permute-done.2.refs_2_), channel_id=1, source_target_pairs={{0,1},{1,0},{2,3},{3,2},{4,5},{5,4},{6,7},{7,6},{8,9},{9,8},{10,11... | collective-permute-start | bytes 479240 | tf_op jit(solution)/shard_map/ppermute | solution.py:685
  90.3 2.6 %collective-permute-start.9 = (bf16[24,3328]{1,0:T(8,128)(2,1)S(1)}, bf16[24,3328]{1,0:T(8,128)(2,1)S(1)}, u32[]{:S(2)}, u32[]{:S(2)}) collective-permute-start(bf16[24,3328]{1,0:T(8,128)(2,1)S(1)} %collective-permute-done.1.refs_1_), channel_id=1, source_target_pairs={{0,1},{1,0},{2,3},{3,2},{4,5},{5,4},{6,7},{7,6},{8,9},{9,8},{10,11... | collective-permute-start | bytes 479240 | tf_op jit(solution)/shard_map/ppermute | solution.py:685
  90.5 8.4 %collective-permute-start.6 = (bf16[24,3328]{1,0:T(8,128)(2,1)S(1)}, bf16[24,3328]{1,0:T(8,128)(2,1)S(1)}, u32[]{:S(2)}, u32[]{:S(2)}) collective-permute-start(bf16[24,3328]{1,0:T(8,128)(2,1)S(1)} %collective-permute-done.4.refs_4_), channel_id=1, source_target_pairs={{0,2},{1,3},{4,0},{5,1},{8,4},{9,5},{12,8},{13,9},{14,12},{15,13},... | collective-permute-start | bytes 479240 | tf_op jit(solution)/shard_map/ppermute | solution.py:682
  92.1 7.6 %collective-permute-start.7 = (bf16[24,3328]{1,0:T(8,128)(2,1)S(1)}, bf16[24,3328]{1,0:T(8,128)(2,1)S(1)}, u32[]{:S(2)}, u32[]{:S(2)}) collective-permute-start(bf16[24,3328]{1,0:T(8,128)(2,1)S(1)} %collective-permute-done.5.refs_5_), channel_id=1, source_target_pairs={{0,4},{1,5},{4,8},{5,9},{8,12},{9,13},{12,14},{13,15},{14,10},{15,... | collective-permute-start | bytes 479240 | tf_op jit(solution)/shard_map/ppermute | solution.py:678
  92.2 22.8 %collective-permute-start.12 = (bf16[24,3328]{1,0:T(8,128)(2,1)S(1)}, bf16[24,3328]{1,0:T(8,128)(2,1)S(1)}, u32[]{:S(2)}, u32[]{:S(2)}) collective-permute-start(bf16[24,3328]{1,0:T(8,128)(2,1)S(1)} %collective-permute-done.4.refs_4_), channel_id=1, source_target_pairs={{0,1},{1,0},{2,3},{3,2},{4,5},{5,4},{6,7},{7,6},{8,9},{9,8},{10,11... | collective-permute-start | bytes 479240 | tf_op jit(solution)/shard_map/ppermute | solution.py:685
  92.9 22.1 %collective-permute-start.11 = (bf16[24,3328]{1,0:T(8,128)(2,1)S(1)}, bf16[24,3328]{1,0:T(8,128)(2,1)S(1)}, u32[]{:S(2)}, u32[]{:S(2)}) collective-permute-start(bf16[24,3328]{1,0:T(8,128)(2,1)S(1)} %collective-permute-done.3.refs_3_), channel_id=1, source_target_pairs={{0,1},{1,0},{2,3},{3,2},{4,5},{5,4},{6,7},{7,6},{8,9},{9,8},{10,11... | collective-permute-start | bytes 479240 | tf_op jit(solution)/shard_map/ppermute | solution.py:685
  93.0 22.0 %collective-permute-start.13 = (bf16[24,3328]{1,0:T(8,128)(2,1)S(1)}, bf16[24,3328]{1,0:T(8,128)(2,1)S(1)}, u32[]{:S(2)}, u32[]{:S(2)}) collective-permute-start(bf16[24,3328]{1,0:T(8,128)(2,1)S(1)} %collective-permute-done.5.refs_5_), channel_id=1, source_target_pairs={{0,1},{1,0},{2,3},{3,2},{4,5},{5,4},{6,7},{7,6},{8,9},{9,8},{10,11... | collective-permute-start | bytes 479240 | tf_op jit(solution)/shard_map/ppermute | solution.py:685
  98.9 16.1 %collective-permute-start.14 = (bf16[24,3328]{1,0:T(8,128)(2,1)S(1)}, bf16[24,3328]{1,0:T(8,128)(2,1)S(1)}, u32[]{:S(2)}, u32[]{:S(2)}) collective-permute-start(bf16[24,3328]{1,0:T(8,128)(2,1)S(1)} %collective-permute-done.6.refs_6_), channel_id=1, source_target_pairs={{0,1},{1,0},{2,3},{3,2},{4,5},{5,4},{6,7},{7,6},{8,9},{9,8},{10,11... | collective-permute-start | bytes 479240 | tf_op jit(solution)/shard_map/ppermute | solution.py:685
  99.7 15.4 %collective-permute-start.15 = (bf16[24,3328]{1,0:T(8,128)(2,1)S(1)}, bf16[24,3328]{1,0:T(8,128)(2,1)S(1)}, u32[]{:S(2)}, u32[]{:S(2)}) collective-permute-start(bf16[24,3328]{1,0:T(8,128)(2,1)S(1)} %collective-permute-done.7.refs_7_), channel_id=1, source_target_pairs={{0,1},{1,0},{2,3},{3,2},{4,5},{5,4},{6,7},{7,6},{8,9},{9,8},{10,11... | collective-permute-start | bytes 479240 | tf_op jit(solution)/shard_map/ppermute | solution.py:685
  110.4 1.6 %copy-start.4 = (bf16[4,512,512]{2,1,0:T(8,128)(2,1)S(1)}, bf16[4,512,512]{2,1,0:T(8,128)(2,1)}, u32[]{:S(2)}) copy-start(bf16[4,512,512]{2,1,0:T(8,128)(2,1)} %copy-done.2) | copy-start | bytes 6291460

commit v2 on v0

--- a/solution.py
+++ b/solution.py
@@ -2,7 +2,11 @@
 
 import jax
 import jax.numpy as jnp
+import ml_dtypes
+import numpy as np
 from jax import lax
+from jax.experimental import pallas as pl
+from jax.experimental.pallas import tpu as pltpu
 from jax.sharding import PartitionSpec as P
 
 
@@ -113,7 +117,7 @@
     return moved
 
 
-def shards(field, spectral_weight, local_weight, bias, cotangent):
+def general_shards(field, spectral_weight, local_weight, bias, cotangent):
     rows, length_y, width_all = field.shape
     chans = local_weight.shape[0]
     planes = width_all // chans
@@ -162,6 +166,781 @@
     return (output_field, field_grad, spectral_grad, local_grad, bias_grad)
 
 
+F32 = jnp.float32
+BF16 = jnp.bfloat16
+LANES = 128
+VMEM_LIMIT = 24 * 1024 * 1024
+
+
+def dot(left, right):
+    return jnp.dot(left, right, preferred_element_type=F32)
+
+
+def params(**kwargs):
+    return pltpu.CompilerParams(vmem_limit_bytes=VMEM_LIMIT, **kwargs)
+
+
+def cost(flops, bytes_accessed):
+    return pl.CostEstimate(flops=flops, bytes_accessed=bytes_accessed, transcendentals=0)
+
+
+def np_ytable(count, length, weighted):
+    modes = np.arange(count)
+    places = np.arange(length)
+    phase = np.float32(2.0 * math.pi) * (modes[:, None] * places[None, :] % length).astype(np.float32) / np.float32(length)
+    factor = np.where(modes == 0, 1.0, 2.0).astype(np.float32) if weighted else np.ones((count,), np.float32)
+    scale = (factor / np.float32(math.sqrt(length)))[:, None]
+    both = np.stack([scale * np.cos(phase), -scale * np.sin(phase)]).astype(ml_dtypes.bfloat16)
+    return both.reshape(2 * count, length)
+
+
+def np_xtables(count, length):
+    index = np.arange(count)
+    modes = np.where(index < count // 2, index, length - count + index)
+    places = np.arange(length)
+    phase = np.float32(2.0 * math.pi) * (modes[:, None] * places[None, :] % length).astype(np.float32) / np.float32(length)
+    norm = np.float32(math.sqrt(length))
+    cosines = np.cos(phase) / norm
+    sines = np.sin(phase) / norm
+    forward = np.stack([np.stack([cosines, sines], -1), np.stack([-sines, cosines], -1)])
+    forward = forward.reshape(2 * count, 2 * length).astype(ml_dtypes.bfloat16)
+    return forward, np.ascontiguousarray(forward.T)
+
+
+def lane_equals(rows, lanes, divide, offset):
+    row = lax.broadcasted_iota(jnp.int32, (rows, lanes), 0)
+    lane = lax.broadcasted_iota(jnp.int32, (rows, lanes), 1)
+    return jnp.where(row - divide(lane) == offset, 1.0, 0.0).astype(BF16)
+
+
+def start_all(pairs, sem):
+    copies = [pltpu.make_async_copy(src, dst, sem.at[n]) for n, (src, dst) in enumerate(pairs)]
+    for copy in copies:
+        copy.start()
+    return copies
+
+
+def hbm():
+    return pl.BlockSpec(memory_space=pltpu.HBM)
+
+
+def in_hbm(*arrays):
+    return [pltpu.with_memory_space_constraint(a, pltpu.HBM) for a in arrays]
+
+
+def vmem():
+    return pl.BlockSpec(memory_space=pltpu.VMEM)
+
+
+def smem():
+    return pl.BlockSpec(memory_space=pltpu.SMEM)
+
+
+def scatter_rows(dst, sums, place, chips, half):
+    tiles = half // LANES
+    for s in range(2):
+        for core in range(2):
+            where = pl.ds(core * 8 + 2 * place + s, chips, stride=16)
+            own = (3 * s + 2 * core) * chips
+            shared = (3 * s + 1) * chips
+            for k in range(2 * tiles):
+                dst[k, where, :] = sums[own : own + chips, k * LANES : (k + 1) * LANES]
+            for k in range(tiles):
+                at = (core * tiles + k) * LANES
+                dst[2 * tiles + k, where, :] = sums[shared : shared + chips, at : at + LANES]
+
+
+def gather_rows(src, place, chips, half):
+    tiles = half // LANES
+    out = []
+    for s in range(2):
+        one = pl.ds(2 * place + s, chips, stride=16)
+        two = pl.ds(8 + 2 * place + s, chips, stride=16)
+        own = range(2 * tiles)
+        shared = range(2 * tiles, 3 * tiles)
+        out.append(jnp.concatenate([src[k, one, :] for k in own], axis=1))
+        out.append(jnp.concatenate([src[k, w, :] for w in (one, two) for k in shared], axis=1))
+        out.append(jnp.concatenate([src[k, two, :] for k in own], axis=1))
+    return jnp.concatenate(out, axis=0).astype(BF16)
+
+
+def cut_lanes(dst, src):
+    for k in range(dst.shape[0]):
+        dst[k] = src[:, k * LANES : (k + 1) * LANES].astype(F32)
+
+
+def join_lanes(dst, src):
+    for k in range(src.shape[0]):
+        dst[:, k * LANES : (k + 1) * LANES] = src[k].astype(BF16)
+
+
+def cut_shape(shape):
+    return (shape[1] // LANES, shape[0], LANES)
+
+
+def rows_to_modes(field, table, chips, half):
+    rows, length, width = field.shape
+    shape = (chips * 16, 3 * half)
+
+    def kernel(u_hbm, t_hbm, out_hbm, u_ref, t_ref, scr, out_ref, sem, out_sem):
+        copies = start_all([(t_hbm, t_ref)] + [(u_hbm.at[x], u_ref.at[x]) for x in range(rows)], sem)
+        copies[0].wait()
+        for x in range(rows):
+            copies[1 + x].wait()
+            scatter_rows(scr, dot(t_ref[...], u_ref[x]), x, chips, half)
+        join_lanes(out_ref, scr)
+        copy = pltpu.make_async_copy(out_ref, out_hbm, out_sem)
+        copy.start()
+        copy.wait()
+
+    return pl.pallas_call(
+        kernel,
+        in_specs=[hbm(), hbm()],
+        out_specs=hbm(),
+        out_shape=pltpu.HBM(shape, BF16),
+        scratch_shapes=[
+            pltpu.VMEM(field.shape, BF16),
+            pltpu.VMEM(table.shape, BF16),
+            pltpu.VMEM(cut_shape(shape), F32),
+            pltpu.VMEM(shape, BF16),
+            pltpu.SemaphoreType.DMA((1 + rows,)),
+            pltpu.SemaphoreType.DMA,
+        ],
+        compiler_params=params(),
+        cost_estimate=cost(2 * table.size * rows * width, field.size * 2),
+        name="rows_to_modes",
+    )(*in_hbm(field, table))
+
+
+def prepare(me, weights, local_weight, bias, chips, half):
+    modes_x, modes_y, full2 = weights.shape
+    chans = local_weight.shape[0]
+    tiles = full2 // LANES
+    rows = 4 * modes_x
+    groups = full2 // 2 // LANES
+    batch = 6
+
+    def kernel(
+        me_ref, w_hbm, l_ref, b_ref, plain_hbm, turned_hbm, block_hbm, block_t_hbm, bias_hbm,
+        w_ref, scr, pick, one, two, plain_ref, turned_ref, block_ref, block_t_ref, bias_ref, sem, out_sem,
+    ):
+        cuts = [pl.ds(j, batch) for j in range(0, modes_x, batch)]
+        copies = start_all([(w_hbm.at[cut], w_ref.at[cut]) for cut in cuts], sem)
+
+        spread = lane_equals(chans, half, lambda l: l % chans, 0)
+        row = lax.broadcasted_iota(jnp.int32, (half, half), 0) // chans
+        lane = lax.broadcasted_iota(jnp.int32, (half, half), 1) // chans
+        local = l_ref[...]
+        for ref, dims in ((block_ref, 1), (block_t_ref, 0)):
+            wide = lax.dot_general(local, spread, (((dims,), (0,)), ((), ())), preferred_element_type=F32)
+            wide = jnp.concatenate([wide] * (half // chans), axis=0)
+            ref[...] = jnp.where(row == lane, wide, 0.0).astype(BF16)
+        value = jnp.concatenate([b_ref[...]] * 8, axis=0)
+        high = value.astype(BF16)
+        mid = (value - high.astype(F32)).astype(BF16)
+        low = (value - high.astype(F32) - mid.astype(F32)).astype(BF16)
+        wide = dot(high, spread) + dot(mid, spread) + dot(low, spread)
+        bias_ref[...] = jnp.concatenate([wide, wide], axis=1)
+        out_copies = start_all(
+            [(block_ref, block_hbm), (block_t_ref, block_t_hbm), (bias_ref, bias_hbm)], out_sem
+        )
+
+        for n, first in enumerate(range(0, modes_x, batch)):
+            copies[n].wait()
+            for j in range(first, first + batch):
+                for k in range(tiles):
+                    scr[k, j * modes_y : (j + 1) * modes_y, :] = w_ref[j, :, k * LANES : (k + 1) * LANES].astype(F32)
+        chip, core = me_ref[0] // 2, me_ref[0] % 2
+        for w, mode in enumerate((chip + 2 * chips * core, chip + chips)):
+            for k in range(tiles):
+                s, g = divmod(k, groups)
+                base = (2 * w + s) * modes_x
+                pick[g, base : base + modes_x, :] = scr[k, pl.ds(mode, modes_x, stride=modes_y), :]
+        per = LANES // chans
+        repeat = jnp.concatenate(
+            [lane_equals(LANES, LANES, lambda l: l % chans, chans * g) for g in range(per)], axis=1
+        )
+        pad = jnp.zeros((LANES - rows, LANES), F32)
+        for g in range(groups):
+            plain_ref[g] = dot(pick[g].astype(BF16), repeat).astype(BF16)
+            one[g * LANES : (g + 1) * LANES, :] = jnp.transpose(jnp.concatenate([pick[g], pad]))
+        out_copies.append(pltpu.make_async_copy(plain_ref, plain_hbm, out_sem.at[3]))
+        out_copies[-1].start()
+        for b in range(chans):
+            two[b * chans : (b + 1) * chans, :] = one[pl.ds(b, chans, stride=chans), :]
+        for g in range(groups):
+            part = jnp.transpose(two[g * LANES : (g + 1) * LANES, :])[0:rows]
+            turned_ref[g] = dot(part.astype(BF16), repeat).astype(BF16)
+        out_copies.append(pltpu.make_async_copy(turned_ref, turned_hbm, out_sem.at[4]))
+        out_copies[-1].start()
+        for copy in out_copies:
+            copy.wait()
+
+    shape = (groups, rows, LANES * LANES // chans)
+    wide = pltpu.HBM(shape, BF16)
+    block = pltpu.HBM((half, half), BF16)
+    return pl.pallas_call(
+        kernel,
+        in_specs=[smem(), hbm(), vmem(), vmem()],
+        out_specs=(hbm(),) * 5,
+        out_shape=(wide, wide, block, block, pltpu.HBM((8, 2 * half), F32)),
+        scratch_shapes=[
+            pltpu.VMEM(weights.shape, BF16),
+            pltpu.VMEM((tiles, modes_x * modes_y, LANES), F32),
+            pltpu.VMEM((groups, rows, LANES), F32),
+            pltpu.VMEM((full2 // 2, LANES), F32),
+            pltpu.VMEM((full2 // 2, LANES), F32),
+            pltpu.VMEM(shape, BF16),
+            pltpu.VMEM(shape, BF16),
+            pltpu.VMEM((half, half), BF16),
+            pltpu.VMEM((half, half), BF16),
+            pltpu.VMEM((8, 2 * half), F32),
+            pltpu.SemaphoreType.DMA((modes_x // batch,)),
+            pltpu.SemaphoreType.DMA((5,)),
+        ],
+        compiler_params=params(),
+        cost_estimate=cost(1000000, 4 * 1024 * 1024),
+        name="prepare",
+    )(me, *in_hbm(weights), local_weight, bias)
+
+
+def weigh(spec, w_ref, chans, modes_x, adjoint):
+    tiles = spec.shape[1] // LANES
+    groups = LANES // chans
+    stack = jnp.concatenate([spec[:, k * LANES : (k + 1) * LANES] for k in range(tiles)], axis=0)
+    real = [None] * tiles
+    imag = [None] * tiles
+    for pair in range(chans // 2):
+        two = [lane_equals(LANES, LANES, lambda l: l // chans * chans, c) for c in (2 * pair, 2 * pair + 1)]
+        wide_rows = dot(stack, jnp.concatenate(two, axis=1))
+        for c in (2 * pair, 2 * pair + 1):
+            lanes = slice((c % 2) * LANES, (c % 2 + 1) * LANES)
+            wl = slice((c % groups) * LANES, (c % groups + 1) * LANES)
+            for own in range(2):
+                base = 2 * own * modes_x
+                wr = w_ref[c // groups, base : base + modes_x, wl].astype(F32)
+                wi = w_ref[c // groups, base + modes_x : base + 2 * modes_x, wl].astype(F32)
+                for k in range(0, 2 * tiles // 3) if own == 0 else range(2 * tiles // 3, tiles):
+                    xr = wide_rows[2 * k * modes_x : (2 * k + 1) * modes_x, lanes]
+                    xi = wide_rows[(2 * k + 1) * modes_x : (2 * k + 2) * modes_x, lanes]
+                    if adjoint:
+                        r, i = xr * wr + xi * wi, xi * wr - xr * wi
+                    else:
+                        r, i = xr * wr - xi * wi, xr * wi + xi * wr
+                    real[k] = r if real[k] is None else real[k] + r
+                    imag[k] = i if imag[k] is None else imag[k] + i
+    return jnp.concatenate([jnp.concatenate(real, axis=1), jnp.concatenate(imag, axis=1)], axis=0).astype(BF16)
+
+
+def mode_step(pencil, spread_w, forward, inverse, chans, adjoint):
+    modes_x = forward.shape[0] // 2
+
+    def kernel(p_ref, w_hbm, f_hbm, i_hbm, spec_ref, out_hbm, w_ref, f_ref, i_ref, out_ref, sem, out_sem):
+        copies = start_all([(f_hbm, f_ref), (w_hbm, w_ref), (i_hbm, i_ref)], sem)
+        copies[0].wait()
+        spec = dot(f_ref[...], p_ref[...]).astype(BF16)
+        spec_ref[...] = spec
+        copies[1].wait()
+        copies[2].wait()
+        mixed = weigh(spec, w_ref, chans, modes_x, adjoint)
+        out_ref[...] = dot(i_ref[...], mixed).astype(BF16)
+        copy = pltpu.make_async_copy(out_ref, out_hbm, out_sem)
+        copy.start()
+        copy.wait()
+
+    return pl.pallas_call(
+        kernel,
+        in_specs=[vmem()] + [hbm()] * 3,
+        out_specs=(vmem(), hbm()),
+        out_shape=(
+            jax.ShapeDtypeStruct((2 * modes_x, pencil.shape[1]), BF16),
+            pltpu.HBM(pencil.shape, BF16),
+        ),
+        scratch_shapes=[
+            pltpu.VMEM(spread_w.shape, BF16),
+            pltpu.VMEM(forward.shape, BF16),
+            pltpu.VMEM(inverse.shape, BF16),
+            pltpu.VMEM(pencil.shape, BF16),
+            pltpu.SemaphoreType.DMA((3,)),
+            pltpu.SemaphoreType.DMA,
+        ],
+        compiler_params=params(),
+        cost_estimate=cost(2 * 48 * 6 * 128 * 4096, spread_w.size * 4),
+        name="adjoint_step" if adjoint else "mode_step",
+    )(pencil, *in_hbm(spread_w, forward, inverse))
+
+
+def pointwise(field, cotangent, pencil, table_t, table, block_weight, bias_row, chips, half):
+    rows, length, width = field.shape
+    chunk = 64
+
+    def kernel(
+        u_hbm, c_hbm, p_ref, tt_hbm, t_hbm, w_hbm, b_hbm, out_hbm, dpre_hbm, send_hbm,
+        u_ref, c_ref, tt_ref, t_ref, w_ref, b_ref, out_ref, dpre_ref, send_ref, bscr, dscr, sem, out_sem,
+    ):
+        copies = start_all([(tt_hbm, tt_ref), (w_hbm, w_ref), (b_hbm, b_ref), (t_hbm, t_ref)], sem)
+        for x in range(rows):
+            pltpu.make_async_copy(u_hbm.at[x], u_ref.at[x], sem.at[5 + x]).start()
+            pltpu.make_async_copy(c_hbm.at[x], c_ref.at[x], sem.at[5 + rows + x]).start()
+        for copy in copies:
+            copy.wait()
+        cut_lanes(bscr, p_ref)
+        root = math.sqrt(2.0 / math.pi)
+
+        def one_row(x):
+            pltpu.make_async_copy(u_hbm.at[x], u_ref.at[x], sem.at[5 + x]).wait()
+            pltpu.make_async_copy(c_hbm.at[x], c_ref.at[x], sem.at[5 + rows + x]).wait()
+            bias = b_ref[0:1, :]
+            coeff = gather_rows(bscr, x, chips, half)
+            for k in range(length // chunk):
+                where = pl.ds(k * chunk, chunk)
+                u = u_ref[x, where, :]
+                spec = dot(tt_ref[where, :], coeff)
+                for h in range(2):
+                    lanes = slice(h * half, (h + 1) * half)
+                    pre = spec[:, lanes] + dot(u[:, lanes], w_ref[...]) + bias[:, lanes]
+                    inner = pre * (root + (root * 0.044715) * (pre * pre))
+                    th = jnp.tanh(inner)
+                    cdf = 0.5 * th + 0.5
+                    out_ref[x, where, lanes] = (pre * cdf).astype(BF16)
+                    slope = 6.0 * inner - (4.0 * root) * pre
+                    grad = cdf + (cdf - cdf * cdf) * slope
+                    dpre_ref[x, where, lanes] = (c_ref[x, where, lanes].astype(F32) * grad).astype(BF16)
+            pltpu.make_async_copy(out_ref.at[x], out_hbm.at[x], out_sem.at[x]).start()
+            pltpu.make_async_copy(dpre_ref.at[x], dpre_hbm.at[x], out_sem.at[rows + x]).start()
+            scatter_rows(dscr, dot(t_ref[...], dpre_ref[x]), x, chips, half)
+
+        pl.loop(0, rows)(one_row)
+        join_lanes(send_ref, dscr)
+        pltpu.make_async_copy(send_ref, send_hbm, out_sem.at[2 * rows]).start()
+        for x in range(rows):
+            pltpu.make_async_copy(out_ref.at[x], out_hbm.at[x], out_sem.at[x]).wait()
+            pltpu.make_async_copy(dpre_ref.at[x], dpre_hbm.at[x], out_sem.at[rows + x]).wait()
+        pltpu.make_async_copy(send_ref, send_hbm, out_sem.at[2 * rows]).wait()
+
+    return pl.pallas_call(
+        kernel,
+        in_specs=[hbm(), hbm(), vmem()] + [hbm()] * 4,
+        out_specs=(hbm(), hbm(), hbm()),
+        out_shape=(
+            pltpu.HBM(field.shape, BF16),
+            pltpu.HBM(field.shape, BF16),
+            pltpu.HBM(pencil.shape, BF16),
+        ),
+        scratch_shapes=[
+            pltpu.VMEM(field.shape, BF16),
+            pltpu.VMEM(field.shape, BF16),
+            pltpu.VMEM(table_t.shape, BF16),
+            pltpu.VMEM(table.shape, BF16),
+            pltpu.VMEM(block_weight.shape, BF16),
+            pltpu.VMEM(bias_row.shape, F32),
+            pltpu.VMEM(field.shape, BF16),
+            pltpu.VMEM(field.shape, BF16),
+            pltpu.VMEM(pencil.shape, BF16),
+            pltpu.VMEM(cut_shape(pencil.shape), F32),
+            pltpu.VMEM(cut_shape(pencil.shape), F32),
+            pltpu.SemaphoreType.DMA((5 + 2 * rows,)),
+            pltpu.SemaphoreType.DMA((2 * rows + 1,)),
+        ],
+        compiler_params=params(),
+        cost_estimate=cost(field.size * 1000, field.size * 8),
+        name="pointwise",
+    )(*in_hbm(field, cotangent), pencil, *in_hbm(table_t, table, block_weight, bias_row))
+
+
+def local_sums(field, dpre, chans, half):
+    rows, length, width = field.shape
+    slices = half // chans
+
+    def kernel(u_hbm, d_hbm, out_ref, u_ref, d_ref, sem):
+        copies = start_all(
+            [(u_hbm.at[x], u_ref.at[x]) for x in range(rows)] + [(d_hbm.at[x], d_ref.at[x]) for x in range(rows)], sem
+        )
+        both = bias = None
+        ones = jnp.ones((16, length), BF16)
+        for x in range(rows):
+            copies[x].wait()
+            copies[rows + x].wait()
+            for h in range(2):
+                lanes = slice(h * half, (h + 1) * half)
+                part = lax.dot_general(
+                    u_ref[x, :, lanes], d_ref[x, :, lanes], (((0,), (0,)), ((), ())), preferred_element_type=F32
+                )
+                both = part if both is None else both + part
+            part = dot(ones, d_ref[x])[0:8]
+            bias = part if bias is None else bias + part
+        group = lax.broadcasted_iota(jnp.int32, (chans, half), 1) // chans
+        total = jnp.zeros((chans, half), F32)
+        for p in range(slices):
+            total = jnp.where(group == p, both[p * chans : (p + 1) * chans], total)
+        total = sum(total[:, k * LANES : (k + 1) * LANES] for k in range(half // LANES))
+        bias = sum(bias[:, k * LANES : (k + 1) * LANES] for k in range(width // LANES))
+        shift = LANES // 2
+        while shift >= chans:
+            total = total + pltpu.roll(total, shift, 1)
+            bias = bias + pltpu.roll(bias, shift, 1)
+            shift //= 2
+        group8 = lax.broadcasted_iota(jnp.int32, (8, LANES), 1) // chans
+        folded = jnp.zeros((8, LANES), F32)
+        for k in range(chans // 8):
+            folded = jnp.where(group8 == k, total[8 * k : 8 * k + 8], folded)
+        value = jnp.concatenate([folded, bias], axis=0)
+        high = value.astype(BF16).astype(F32)
+        mid = (value - high).astype(BF16).astype(F32)
+        low = value - high - mid
+        left = jnp.concatenate([high, mid[0:8]], axis=0)
+        right = jnp.concatenate([mid[8:16], low], axis=0)
+        out_ref[...] = jnp.concatenate([left, right], axis=1).astype(BF16)
+
+    return pl.pallas_call(
+        kernel,
+        in_specs=[hbm(), hbm()],
+        out_specs=vmem(),
+        out_shape=jax.ShapeDtypeStruct((24, 2 * LANES), BF16),
+        scratch_shapes=[
+            pltpu.VMEM(field.shape, BF16),
+            pltpu.VMEM(field.shape, BF16),
+            pltpu.SemaphoreType.DMA((2 * rows,)),
+        ],
+        compiler_params=params(),
+        cost_estimate=cost(field.size * 1000, field.size * 4),
+        name="local_sums",
+    )(*in_hbm(field, dpre))
+
+
+def weight_sums(me, spectrum, grads, chans):
+    modes_x = spectrum.shape[0] // 2
+    tiles = spectrum.shape[1] // LANES
+    groups = LANES // chans
+    step = 2 * LANES
+    full = chans * chans
+    parts = full // step
+
+    def kernel(me_ref, u_ref, d_ref, own_ref, keep_ref, send_ref):
+        def stack(ref):
+            return jnp.concatenate([ref[:, k * LANES : (k + 1) * LANES] for k in range(tiles)], axis=0)
+
+        first = me_ref[0] % 2 == 0
+        left = stack(u_ref)
+        repeat = jnp.concatenate(
+            [lane_equals(LANES, LANES, lambda l: l % chans, chans * g) for g in range(groups)], axis=1
+        )
+        right = dot(stack(d_ref), repeat)
+        for a in range(parts):
+            sums = {}
+            for g in range(groups):
+                pick = lane_equals(LANES, step, lambda l: l // chans, g * chans + a * (step // chans))
+                spread_u = dot(left, pick)
+                for k in range(tiles):
+                    kind = 0 if k < 2 * tiles // 3 else 1
+                    re = slice(2 * k * modes_x, (2 * k + 1) * modes_x)
+                    im = slice((2 * k + 1) * modes_x, (2 * k + 2) * modes_x)
+                    for z in range(2):
+                        lanes = slice(z * LANES, (z + 1) * LANES)
+                        ur, ui = spread_u[re, lanes], spread_u[im, lanes]
+                        dr = right[re, g * LANES : (g + 1) * LANES]
+                        di = right[im, g * LANES : (g + 1) * LANES]
+                        for t, term in ((0, ur * dr + ui * di), (1, ur * di - ui * dr)):
+                            key = (kind, t, z)
+                            sums[key] = term if key not in sums else sums[key] + term
+            for t in range(2):
+                own = jnp.concatenate([sums[0, t, 0], sums[0, t, 1]], axis=1)
+                own_ref[:, t * full + a * step : t * full + (a + 1) * step] = own.astype(BF16)
+                shared = jnp.concatenate([sums[1, t, 0], sums[1, t, 1]], axis=1)
+                at = t * (full // 2) + (a % (parts // 2)) * step
+                low = a < parts // 2
+
+                @pl.when(first if low else jnp.logical_not(first))
+                def _():
+                    keep_ref[:, at : at + step] = shared
+
+                @pl.when(jnp.logical_not(first) if low else first)
+                def _():
+                    send_ref[:, at : at + step] = shared
+
+    half_shape = jax.ShapeDtypeStruct((modes_x, full), F32)
+    return pl.pallas_call(
+        kernel,
+        in_specs=[smem(), vmem(), vmem()],
+        out_shape=(jax.ShapeDtypeStruct((modes_x, 2 * full), BF16), half_shape, half_shape),
+        compiler_params=params(),
+        cost_estimate=cost(2 * 288 * 128 * 4096, 4 * 1024 * 1024),
+        name="weight_sums",
+    )(me, spectrum, grads)
+
+
+def make_shard(own, keep, other, stats):
+    rows, full2 = own.shape
+    full = keep.shape[1]
+    width = full2 + full + stats.shape[1]
+
+    def kernel(o_ref, k_ref, r_ref, s_ref, out_ref):
+        out_ref[:, 0:full2] = o_ref[...]
+        out_ref[:, full2 : full2 + full] = (k_ref[...] + r_ref[...]).astype(BF16)
+        out_ref[:, full2 + full :] = s_ref[...]
+
+    return pl.pallas_call(
+        kernel,
+        out_shape=jax.ShapeDtypeStruct((rows, width), BF16),
+        compiler_params=params(),
+        name="make_shard",
+    )(own, keep, other, stats)
+
+
+def ring_chip(spot, chips):
+    return jnp.where(spot < chips // 2, 2 * spot, 2 * (chips - 1 - spot) + 1)
+
+
+def ring_spot(chip, chips):
+    return jnp.where(chip % 2 == 0, chip // 2, chips - 1 - chip // 2)
+
+
+def assemble(me, shards_all, turns, modes_y, chans, chips):
+    rows = shards_all[0].shape[0]
+    full = chans * chans
+    count = len(shards_all)
+    step = 2 * LANES
+    blocks = 2 * full // LANES
+
+    def kernel(me_ref, *refs):
+        ins, (g_ref, l_ref, b_ref, scr, stat, out, sem) = refs[:count], refs[count:]
+        spot = ring_spot(me_ref[0] // 2, chips)
+        places = []
+        for back, swapped in turns:
+            chip = ring_chip((spot + chips - back) % chips, chips)
+            core = me_ref[0] % 2
+            places.append((chip, 1 - core if swapped else core))
+        copies = []
+        for k in range(blocks):
+            for n in range(count):
+                chip, core = places[n]
+                own = pl.ds(chip + 2 * chips * core, rows, stride=modes_y)
+                scr[k, own, :] = ins[n][:, k * LANES : (k + 1) * LANES].astype(F32)
+            part = k % (blocks // 2)
+            from_core = part // (blocks // 4)
+            at = 2 * full + (k // (blocks // 2)) * (full // 2) + (part % (blocks // 4)) * LANES
+            for n in range(count):
+                if turns[n][1]:
+                    continue
+                chip, core = places[n]
+                mate = turns.index((turns[n][0], True))
+                here = ins[n][:, at : at + LANES].astype(F32)
+                there = ins[mate][:, at : at + LANES].astype(F32)
+                where = pl.ds(chip + chips, rows, stride=modes_y)
+                scr[k, where, :] = jnp.where(core == from_core, here, there)
+            lanes = slice(k * LANES, (k + 1) * LANES)
+            for j in range(rows):
+                out[j, :, lanes] = scr[k, j * modes_y : (j + 1) * modes_y, :].astype(BF16)
+            if k % 4 == 3:
+                lanes = pl.ds((k - 3) * LANES, 4 * LANES)
+                copies.append(pltpu.make_async_copy(out.at[:, :, lanes], g_ref.at[:, :, lanes], sem.at[k // 4]))
+                copies[-1].start()
+        for n in range(count):
+            chip, core = places[n]
+            left = ins[n][:, 3 * full : 3 * full + LANES].astype(F32)
+            right = ins[n][:, 3 * full + LANES :].astype(F32)
+            middle = jnp.concatenate([left[16:24], right[0:8]], axis=0)
+            stat[2 * chip + core] = left[0:16] + middle + right[8:24]
+        total = stat[0]
+        for n in range(1, count):
+            total = total + stat[n]
+        for k in range(chans // 8):
+            piece = total[0:8] if k == 0 else pltpu.roll(total[0:8], LANES - k * chans, 1)
+            l_ref[8 * k : 8 * k + 8, :] = piece[:, 0:chans]
+        b_ref[...] = total[8:9, 0:chans]
+        for copy in copies:
+            copy.wait()
+
+    vmem = pl.BlockSpec(memory_space=pltpu.VMEM)
+    shape = (rows, modes_y, 2 * full)
+    return pl.pallas_call(
+        kernel,
+        in_specs=[pl.BlockSpec(memory_space=pltpu.SMEM)] + [vmem] * count,
+        out_specs=(pl.BlockSpec(memory_space=pl.ANY), vmem, vmem),
+        out_shape=(
+            jax.ShapeDtypeStruct(shape, BF16),
+            jax.ShapeDtypeStruct((chans, chans), F32),
+            jax.ShapeDtypeStruct((1, chans), F32),
+        ),
+        scratch_shapes=[
+            pltpu.VMEM((blocks, rows * modes_y, LANES), F32),
+            pltpu.VMEM((count, 16, LANES), F32),
+            pltpu.VMEM(shape, BF16),
+            pltpu.SemaphoreType.DMA((blocks // 4,)),
+        ],
+        compiler_params=params(),
+        cost_estimate=cost(1000000, 8 * 1024 * 1024),
+        name="assemble",
+    )(me, *shards_all)
+
+
+def back_to_field(dpre, pencil, table_t, block_weight, chips, half):
+    rows, length, width = dpre.shape
+    chunk = 128
+
+    def kernel(d_hbm, p_ref, tt_hbm, w_hbm, out_hbm, d_ref, tt_ref, w_ref, out_ref, bscr, sem, out_sem):
+        copies = start_all(
+            [(tt_hbm, tt_ref), (w_hbm, w_ref)] + [(d_hbm.at[x], d_ref.at[x]) for x in range(rows)], sem
+        )
+        for copy in copies[0:2]:
+            copy.wait()
+        cut_lanes(bscr, p_ref)
+        out_copies = []
+        for x in range(rows):
+            copies[2 + x].wait()
+            coeff = gather_rows(bscr, x, chips, half)
+            for k in range(length // chunk):
+                where = pl.ds(k * chunk, chunk)
+                d = d_ref[x, where, :]
+                spec = dot(tt_ref[where, :], coeff)
+                for h in range(2):
+                    lanes = slice(h * half, (h + 1) * half)
+                    out_ref[x, where, lanes] = (spec[:, lanes] + dot(d[:, lanes], w_ref[...])).astype(BF16)
+            out_copies.append(pltpu.make_async_copy(out_ref.at[x], out_hbm.at[x], out_sem.at[x]))
+            out_copies[-1].start()
+        for copy in out_copies:
+            copy.wait()
+
+    return pl.pallas_call(
+        kernel,
+        in_specs=[hbm(), vmem(), hbm(), hbm()],
+        out_specs=hbm(),
+        out_shape=pltpu.HBM(dpre.shape, BF16),
+        scratch_shapes=[
+            pltpu.VMEM(dpre.shape, BF16),
+            pltpu.VMEM(table_t.shape, BF16),
+            pltpu.VMEM(block_weight.shape, BF16),
+            pltpu.VMEM(dpre.shape, BF16),
+            pltpu.VMEM(cut_shape(pencil.shape), F32),
+            pltpu.SemaphoreType.DMA((2 + rows,)),
+            pltpu.SemaphoreType.DMA((rows,)),
+        ],
+        compiler_params=params(),
+        cost_estimate=cost(dpre.size * 500, dpre.size * 4),
+        name="back_to_field",
+    )(*in_hbm(dpre), pencil, *in_hbm(table_t, block_weight))
+
+
+def exchange(pencil):
+    return lax.all_to_all(pencil, "xy", split_axis=0, concat_axis=0, tiled=True)
+
+
+class Ring:
+    def __init__(self, shard, chips):
+        order = [ring_chip_int(i, chips) for i in range(chips)]
+        self.chips = chips
+        self.hops = {
+            way: [(2 * order[i] + c, 2 * order[(i + way) % chips] + c) for i in range(chips) for c in range(2)]
+            for way in (1, -1)
+        }
+        self.swap = [(i, i ^ 1) for i in range(2 * chips)]
+        self.step = 0
+        self.ahead = self.back = shard
+        self.parts, self.turns = [], []
+        self.keep(shard, 0)
+
+    def keep(self, piece, turn):
+        self.parts.append(piece)
+        self.turns.append((turn, False))
+        self.parts.append(lax.ppermute(piece, "xy", self.swap))
+        self.turns.append((turn, True))
+
+    def hop(self):
+        self.step += 1
+        self.ahead = lax.ppermute(self.ahead, "xy", self.hops[1])
+        if self.step < self.chips // 2:
+            self.back = lax.ppermute(self.back, "xy", self.hops[-1])
+
+    def settle(self):
+        self.keep(self.ahead, self.step)
+        if self.step < self.chips // 2:
+            self.keep(self.back, self.chips - self.step)
+
+    def tie(self, other):
+        self.ahead, self.back, other = lax.optimization_barrier((self.ahead, self.back, other))
+        return other
+
+    def hold(self, other):
+        self.ahead, other = lax.optimization_barrier((self.ahead, other))
+        return other
+
+
+def ring_chip_int(spot, chips):
+    return 2 * spot if spot < chips // 2 else 2 * (chips - 1 - spot) + 1
+
+
+def fast_shards(field, spectral_weight, local_weight, bias, cotangent):
+    rows, length_y, width = field.shape
+    chans = local_weight.shape[0]
+    planes = width // chans
+    modes_x, modes_y = spectral_weight.shape[:2]
+    devices = lax.axis_size("xy")
+    chips = devices // 2
+    half = width // 2
+    me = lax.axis_index("xy")
+    table_y = np_ytable(modes_y, length_y, False)
+    table_yw = np_ytable(modes_y, length_y, True)
+    table_y_t, table_yw_t = (np.ascontiguousarray(t.T) for t in (table_y, table_yw))
+    forward, inverse = np_xtables(modes_x, rows * devices)
+    me_id = me.astype(jnp.int32)[None]
+
+    send = rows_to_modes(field, table_y, chips, half)
+    pencil = exchange(send)
+    plain, turned, block, block_t, bias_row = prepare(
+        me_id, spectral_weight, local_weight, bias[None, :], chips, half
+    )
+    spectrum, send = mode_step(pencil, plain, forward, inverse, chans, False)
+    pencil = exchange(send)
+    output_field, dpre, send = pointwise(
+        field, cotangent, pencil, table_yw_t, table_yw, block, bias_row, chips, half
+    )
+    pencil = exchange(send)
+    stats = local_sums(field, dpre, chans, half)
+    pencil, stats = lax.optimization_barrier((pencil, stats))
+    grads, send = mode_step(pencil, turned, forward, inverse, chans, True)
+    pencil = exchange(send)
+    own, keep, give = weight_sums(me_id, spectrum, grads, chans)
+    got = lax.ppermute(give, "xy", [(i, i ^ 1) for i in range(devices)])
+    shard = make_shard(own, keep, got, stats)
+
+    ring = Ring(shard, chips)
+    ring.hop()
+    pencil = ring.tie(pencil)
+    ring.settle()
+    ring.hop()
+    field_grad = back_to_field(dpre, pencil, table_y_t, block_t, chips, half)
+    field_grad = ring.tie(field_grad)
+    ring.settle()
+    ring.hop()
+    ring.settle()
+    ring.hop()
+    ring.settle()
+    parts, turns = ring.parts, ring.turns
+    spectral_grad, local_grad, bias_grad = assemble(me_id, parts, turns, modes_y, chans, chips)
+    return output_field, field_grad, spectral_grad, local_grad, bias_grad.reshape(chans)
+
+
+def fits(field, spectral_weight, local_weight, devices):
+    rows, length_y, width = field.shape
+    chans = local_weight.shape[0]
+    modes_x, modes_y = spectral_weight.shape[:2]
+    return (
+        rows == 4
+        and chans == 32
+        and width == 512
+        and length_y % 128 == 0
+        and modes_x == 24
+        and devices == 16
+        and 2 * modes_y == 3 * devices
+    )
+
+
+def shards(field, spectral_weight, local_weight, bias, cotangent):
+    if fits(field, spectral_weight, local_weight, lax.axis_size("xy")):
+        return fast_shards(field, spectral_weight, local_weight, bias, cotangent)
+    return general_shards(field, spectral_weight, local_weight, bias, cotangent)
+
+
 def solution(mesh):
     return jax.shard_map(
         shards,

time: 601 us -> 94.8 us (0.16); the launches traced: 593 us -> 93.8 us
  blocking collectives: 401 us -> 12.1 us
  local copies, waits for them, and re-layouts: 91.1 us -> 0.01 us
  matrix products: 54.6 us -> 0 us
  Pallas kernels: 0 us -> 31.3 us
  other arithmetic: 18.4 us -> 0 us
  waiting for transfers between devices: 1.09 us -> 17.8 us
  starting transfers between devices: 25.4 us -> 31.8 us
    psum x1 -> x0, blocking collectives: 401 us -> none  [shards(): lax.psum((partial_grad, weight_part, bias_part), 'xy')]
    dot_general x20 -> x0, matrix products: 54.6 us -> none  [the longest x19 39 us: mult(): return jnp.einsum(form, left, right, preferred_element_type=jnp.float32)]
    pallas_call x0 -> x10, Pallas kernels: none -> 31.3 us  [the longest x1 7.07 us: pointwise(): pl.pallas_call(kernel, in_specs=[hbm(), hbm(), vmem()] + [hbm()] * 4, out...]
    convert_element_type x5 -> x0, local copies, waits for them, and re-layouts: 28.5 us -> none  [the longest x2 23.5 us: shards(): total.reshape(modes_x, modes_y, 2 * chans * chans).astype(jnp.bfloat16)]
    unnamed x48 -> x4, local copies, waits for them, and re-layouts: 19.1 us -> 0.01 us
    reshape x15 -> x0, local copies, waits for them, and re-layouts: 18.7 us -> none  [the longest x1 9.03 us: shards(): weight_all = spectral_weight.reshape(modes_x, modes_y, 2, chans, chans)]
    ppermute x0 -> x16, starting transfers between devices: none -> 15.4 us  [the longest x8 9.33 us: keep(): self.parts.append(lax.ppermute(piece, 'xy', self.swap))]
    all_to_all x0 -> x1, blocking collectives: none -> 12.1 us  [exchange(): return lax.all_to_all(pencil, 'xy', split_axis=0, concat_axis=0, tiled=True)]
  transfers between devices with their start and end apart: 4 -> 19, of which waited for: 1 -> 8; matrix products, arithmetic and copies ran while one was open for 17% -> 0% of each run, Pallas kernels for 0% -> 13%
where the time goes in v2:
time: 94.8 us; the launch traced here: 93.8 us
  starting transfers between devices  31.8 us (34%)
  Pallas kernels  31.3 us (33%)
  waiting for transfers between devices  17.8 us (19%)
  blocking collectives  12.1 us (13%)
    all_to_all x3, starting transfers between devices, exchange(): return lax.all_to_all(pencil, 'xy', split_axis=0, concat_axis=0, tiled=True)  16.4 us
    all_to_all x1, blocking collectives, exchange(): return lax.all_to_all(pencil, 'xy', split_axis=0, concat_axis=0, tiled=True)  12.1 us
    ppermute x8, starting transfers between devices, keep(): self.parts.append(lax.ppermute(piece, 'xy', self.swap))  9.33 us
    all_to_all x3, waiting for transfers between devices, exchange(): return lax.all_to_all(pencil, 'xy', split_axis=0, concat_axis=0, tiled=True)  9.18 us
    pallas_call x1, Pallas kernels, pointwise(): pl.pallas_call(kernel, in_specs=[hbm(), hbm(), vmem()] + [hbm()] * 4, out...  7.07 us
    ppermute x3, waiting for transfers between devices, hop(): self.back = lax.ppermute(self.back, 'xy', self.hops[-1])  6.02 us
    pallas_call x2, Pallas kernels, mode_step(): pl.pallas_call(kernel, in_specs=[vmem()] + [hbm()] * 3, out_specs=(vmem()...  6.01 us
    pallas_call x1, Pallas kernels, back_to_field(): pl.pallas_call(kernel, in_specs=[hbm(), vmem(), hbm(), hbm()], out_specs=...  3.82 us
  transfers between devices with their start and end apart: 19, of which 8 were waited for; matrix products, arithmetic and copies ran while one was open for 0% of the time, Pallas kernels for 13%

profile of v2, /device:TPU:1, one launch (start us, length us, event | category | flops | bytes accessed | tf_op | source)
XLA Modules:
  0.0 93.8 jit_solution(6677498224108861149)
XLA Ops:
  0.6 0.0 copy-start.1
  0.6 0.0 copy-start
  0.7 2.8 %rows_to_modes.1 = bf16[128,768]{1,0:T(8,128)(2,1)} custom-call(bf16[4,512,512]{2,1,0:T(8,128)(2,1)} %u_hbm.5, bf16[48,512]{1,0:T(8,128)(2,1)} %constant.16.clone.t_hbm), custom_call_target="tpu_custom_call" | custom-call | flops 100663296 | bytes 2097152 | tf_op jit(solution)/shard_map/rows_to_modes/pallas_call | solution.py:296
  3.4 7.4 %all-to-all-start = ((bf16[16,8,768]{2,1,0:T(8,128)(2,1)}), bf16[16,8,768]{2,1,0:T(8,128)(2,1)S(1)}, u32[]{:S(2)}, u32[]{:S(2)}) async-start(bf16[16,8,768]{2,1,0:T(8,128)(2,1)} %bitcast.16), calls=%async_computation | async-start | bytes 393216 | tf_op jit(solution)/shard_map/all_to_all | solution.py:825
  10.8 0.0 copy-done.1
  10.8 0.0 copy-done
  10.8 3.6 %prepare.1 = (bf16[8,96,512]{2,1,0:T(8,128)(2,1)}, bf16[8,96,512]{2,1,0:T(8,128)(2,1)}, bf16[256,256]{1,0:T(8,128)(2,1)}, bf16[256,256]{1,0:T(8,128)(2,1)}, f32[8,512]{1,0:T(8,128)}) custom-call(s32[1]{0:T(128)} %bitcast.2.me_ref, bf16[24,24,2048]{2,1,0:T(8,128)(2,1)} %w_hbm.1, bf16[32,32]{1,0:T(8,128)(2,1)S(1)} %copy-done, f32[1,32]{1,0:T(1,128)S(1)} %bitcast.15), custom_call_target="tpu_custom_call" | custom-call | flops 1000000 | bytes 4194304 | tf_op jit(solution)/shard_map/prepare/pallas_call | solution.py:382
  14.4 4.7 %all-to-all-done = bf16[16,8,768]{2,1,0:T(8,128)(2,1)S(1)} async-done(((bf16[16,8,768]{2,1,0:T(8,128)(2,1)}), bf16[16,8,768]{2,1,0:T(8,128)(2,1)S(1)}, u32[]{:S(2)}, u32[]{:S(2)}) %all-to-all-start) | async-done | bytes 196640 | tf_op jit(solution)/shard_map/all_to_all | solution.py:825
  19.1 3.0 %mode_step.1 = (bf16[48,768]{1,0:T(8,128)(2,1)S(1)}, bf16[128,768]{1,0:T(8,128)(2,1)}) custom-call(bf16[128,768]{1,0:T(8,128)(2,1)S(1)} %bitcast.13, bf16[8,96,512]{2,1,0:T(8,128)(2,1)} %get-tuple-element.31.w_hbm, bf16[48,128]{1,0:T(8,128)(2,1)} %constant.17.clone.f_hbm, bf16[128,48]{1,0:T(8,128)(2,1)} %constant.18.clone.i_hbm), custom_call_target="tpu_custom_call" | custom-call | flops 301989888 | bytes 1572864 | tf_op jit(solution)/shard_map/mode_step/pallas_call | solution.py:451
  22.1 12.1 %all_to_all.46 = bf16[16,8,768]{2,1,0:T(8,128)(2,1)S(1)} all-to-all(bf16[16,8,768]{2,1,0:T(8,128)(2,1)} %bitcast.19), channel_id=1, replica_groups=mesh['groups'=2,'xy'=16] {'xy'}, dimensions={0} | all-to-all | bytes 393216 | tf_op jit(solution)/shard_map/all_to_all | solution.py:825
  34.2 7.1 %pointwise.1 = (bf16[4,512,512]{2,1,0:T(8,128)(2,1)}, bf16[4,512,512]{2,1,0:T(8,128)(2,1)}, bf16[128,768]{1,0:T(8,128)(2,1)}) custom-call(bf16[4,512,512]{2,1,0:T(8,128)(2,1)} %u_hbm.5, bf16[4,512,512]{2,1,0:T(8,128)(2,1)} %c_hbm.1, bf16[128,768]{1,0:T(8,128)(2,1)S(1)} %bitcast.12, bf16[512,48]{1,0:T(8,128)(2,1)} %constant.19.clone.tt_hbm, ...), custom_call_target="tpu_custom_call" | custom-call | flops 1048576000 | bytes 8388608 | tf_op jit(solution)/shard_map/pointwise/pallas_call | solution.py:521
  41.3 4.5 %all-to-all-start.2 = ((bf16[16,8,768]{2,1,0:T(8,128)(2,1)}), bf16[16,8,768]{2,1,0:T(8,128)(2,1)S(1)}, u32[]{:S(2)}, u32[]{:S(2)}) async-start(bf16[16,8,768]{2,1,0:T(8,128)(2,1)} %bitcast.18), calls=%async_computation.2 | async-start | bytes 393216 | tf_op jit(solution)/shard_map/all_to_all | solution.py:825
  45.8 3.5 %local_sums.1.s_ref = bf16[24,256]{1,0:T(8,128)(2,1)S(1)} custom-call(bf16[4,512,512]{2,1,0:T(8,128)(2,1)} %u_hbm.5, bf16[4,512,512]{2,1,0:T(8,128)(2,1)} %get-tuple-element.38.d_hbm), custom_call_target="tpu_custom_call" | custom-call | flops 1048576000 | bytes 4194304 | tf_op jit(solution)/shard_map/local_sums/pallas_call | solution.py:595
  49.3 4.5 %all-to-all-done.2 = bf16[16,8,768]{2,1,0:T(8,128)(2,1)S(1)} async-done(((bf16[16,8,768]{2,1,0:T(8,128)(2,1)}), bf16[16,8,768]{2,1,0:T(8,128)(2,1)S(1)}, u32[]{:S(2)}, u32[]{:S(2)}) %all-to-all-start.2) | async-done | bytes 196640 | tf_op jit(solution)/shard_map/all_to_all | solution.py:825
  53.8 3.0 %adjoint_step.1 = (bf16[48,768]{1,0:T(8,128)(2,1)S(1)}, bf16[128,768]{1,0:T(8,128)(2,1)}) custom-call(bf16[128,768]{1,0:T(8,128)(2,1)S(1)} %bitcast.14, bf16[8,96,512]{2,1,0:T(8,128)(2,1)} %get-tuple-element.40.w_hbm, bf16[48,128]{1,0:T(8,128)(2,1)} %constant.17.clone.f_hbm, bf16[128,48]{1,0:T(8,128)(2,1)} %constant.18.clone.i_hbm), custom_call_target="tpu_custom_call" | custom-call | flops 301989888 | bytes 1572864 | tf_op jit(solution)/shard_map/adjoint_step/pallas_call | solution.py:451
  56.8 4.5 %all-to-all-start.3 = ((bf16[16,8,768]{2,1,0:T(8,128)(2,1)}), bf16[16,8,768]{2,1,0:T(8,128)(2,1)S(1)}, u32[]{:S(2)}, u32[]{:S(2)}) async-start(bf16[16,8,768]{2,1,0:T(8,128)(2,1)} %bitcast.17), calls=%async_computation.3 | async-start | bytes 393216 | tf_op jit(solution)/shard_map/all_to_all | solution.py:825
  61.3 1.4 %weight_sums.1 = (bf16[24,2048]{1,0:T(8,128)(2,1)S(1)}, f32[24,1024]{1,0:T(8,128)S(1)}, f32[24,1024]{1,0:T(8,128)S(1)}) custom-call(s32[1]{0:T(128)} %bitcast.2.me_ref, bf16[48,768]{1,0:T(8,128)(2,1)S(1)} %get-tuple-element.36.u_ref, bf16[48,768]{1,0:T(8,128)(2,1)S(1)} %get-tuple-element.41.d_ref), custom_call_target="tpu_custom_call" | custom-call | flops 301989888 | bytes 4194304 | tf_op jit(solution)/shard_map/weight_sums/pallas_call | solution.py:662
  62.7 0.3 collective-permute-start
  63.0 1.1 %collective-permute-done.r_ref = f32[24,1024]{1,0:T(8,128)S(1)} collective-permute-done((f32[24,1024]{1,0:T(8,128)S(1)}, f32[24,1024]{1,0:T(8,128)S(1)}, u32[]{:S(2)}, u32[]{:S(2)}) %collective-permute-start) | collective-permute-done | bytes 98336 | tf_op jit(solution)/shard_map/ppermute | solution.py:903
  64.1 1.4 %collective-permute-start.2 = (bf16[24,3328]{1,0:T(8,128)(2,1)S(1)}, bf16[24,3328]{1,0:T(8,128)(2,1)S(1)}, u32[]{:S(2)}, u32[]{:S(2)}) collective-permute-start(bf16[24,3328]{1,0:T(8,128)(2,1)S(1)} %make_shard.1.refs_0_), channel_id=1, source_target_pairs={{0,2},{1,3},{4,0},{5,1},{8,4},{9,5},{12,8},{13,9},{14,12},{15,13},... | collective-permute-start | bytes 479240 | tf_op jit(solution)/shard_map/ppermute | solution.py:852
  65.5 0.1 collective-permute-start.1
  65.6 5.2 %collective-permute-done.2.refs_4_ = bf16[24,3328]{1,0:T(8,128)(2,1)S(1)} collective-permute-done((bf16[24,3328]{1,0:T(8,128)(2,1)S(1)}, bf16[24,3328]{1,0:T(8,128)(2,1)S(1)}, u32[]{:S(2)}, u32[]{:S(2)}) %collective-permute-start.2) | collective-permute-done | bytes 159776 | tf_op jit(solution)/shard_map/ppermute | solution.py:852
  70.8 0.5 collective-permute-done.1.refs_2_
  71.4 0.0 all-to-all-done.3
  71.4 1.2 %collective-permute-start.3 = (bf16[24,3328]{1,0:T(8,128)(2,1)S(1)}, bf16[24,3328]{1,0:T(8,128)(2,1)S(1)}, u32[]{:S(2)}, u32[]{:S(2)}) collective-permute-start(bf16[24,3328]{1,0:T(8,128)(2,1)S(1)} %collective-permute-done.1.refs_2_), channel_id=1, source_target_pairs={{0,4},{1,5},{4,8},{5,9},{8,12},{9,13},{12,14},{13,15},{14,10},{15,... | collective-permute-start | bytes 479240 | tf_op jit(solution)/shard_map/ppermute | solution.py:850
  72.6 0.3 collective-permute-start.4
  72.8 3.8 %back_to_field.1 = bf16[4,512,512]{2,1,0:T(8,128)(2,1)} custom-call(bf16[4,512,512]{2,1,0:T(8,128)(2,1)} %get-tuple-element.38.d_hbm, bf16[128,768]{1,0:T(8,128)(2,1)S(1)} %bitcast.11, bf16[512,48]{1,0:T(8,128)(2,1)} %constant.21.clone.tt_hbm, bf16[256,256]{1,0:T(8,128)(2,1)} %get-tuple-element.50.w_hbm), custom_call_target="tpu_custom_call" | custom-call | flops 524288000 | bytes 4194304 | tf_op jit(solution)/shard_map/back_to_field/pallas_call | solution.py:804
  76.7 0.0 collective-permute-done.3.refs_6_
  76.7 0.3 collective-permute-done.4.refs_8_
  77.0 0.9 collective-permute-start.10
  77.9 1.7 %collective-permute-start.5 = (bf16[24,3328]{1,0:T(8,128)(2,1)S(1)}, bf16[24,3328]{1,0:T(8,128)(2,1)S(1)}, u32[]{:S(2)}, u32[]{:S(2)}) collective-permute-start(bf16[24,3328]{1,0:T(8,128)(2,1)S(1)} %make_shard.1.refs_0_), channel_id=1, source_target_pairs={{0,1},{1,0},{2,3},{3,2},{4,5},{5,4},{6,7},{7,6},{8,9},{9,8},{10,11... | collective-permute-start | bytes 479240 | tf_op jit(solution)/shard_map/ppermute | solution.py:845
  79.6 0.0 collective-permute-start.6
  79.6 0.5 collective-permute-start.7
  80.1 1.2 %collective-permute-start.12 = (bf16[24,3328]{1,0:T(8,128)(2,1)S(1)}, bf16[24,3328]{1,0:T(8,128)(2,1)S(1)}, u32[]{:S(2)}, u32[]{:S(2)}) collective-permute-start(bf16[24,3328]{1,0:T(8,128)(2,1)S(1)} %collective-permute-done.4.refs_8_), channel_id=1, source_target_pairs={{0,2},{1,3},{4,0},{5,1},{8,4},{9,5},{12,8},{13,9},{14,12},{15,13},... | collective-permute-start | bytes 479240 | tf_op jit(solution)/shard_map/ppermute | solution.py:852
  81.3 0.0 collective-permute-done.10.refs_10_
  81.3 0.7 collective-permute-start.14
  82.1 0.0 collective-permute-done.5.refs_1_
  82.1 2.9 %collective-permute-start.8 = (bf16[24,3328]{1,0:T(8,128)(2,1)S(1)}, bf16[24,3328]{1,0:T(8,128)(2,1)S(1)}, u32[]{:S(2)}, u32[]{:S(2)}) collective-permute-start(bf16[24,3328]{1,0:T(8,128)(2,1)S(1)} %collective-permute-done.3.refs_6_), channel_id=1, source_target_pairs={{0,1},{1,0},{2,3},{3,2},{4,5},{5,4},{6,7},{7,6},{8,9},{9,8},{10,11... | collective-permute-start | bytes 479240 | tf_op jit(solution)/shard_map/ppermute | solution.py:845
  84.9 0.0 collective-permute-done.6.refs_3_
  84.9 0.1 collective-permute-start.9
  85.0 0.0 collective-permute-done.7.refs_5_
  85.0 0.4 collective-permute-start.11
  85.4 0.5 collective-permute-done.12.refs_12_
  85.9 0.8 collective-permute-start.13
  86.7 0.0 collective-permute-done.14.refs_14_
  86.7 3.0 %collective-permute-start.15 = (bf16[24,3328]{1,0:T(8,128)(2,1)S(1)}, bf16[24,3328]{1,0:T(8,128)(2,1)S(1)}, u32[]{:S(2)}, u32[]{:S(2)}) collective-permute-start(bf16[24,3328]{1,0:T(8,128)(2,1)S(1)} %collective-permute-done.14.refs_14_), channel_id=1, source_target_pairs={{0,1},{1,0},{2,3},{3,2},{4,5},{5,4},{6,7},{7,6},{8,9},{9,8},{10,11... | collective-permute-start | bytes 479240 | tf_op jit(solution)/shard_map/ppermute | solution.py:845
  89.6 0.0 collective-permute-done.8.refs_7_
  89.6 0.0 collective-permute-done.9.refs_9_
  89.6 0.0 collective-permute-done.11.refs_11_
  89.6 0.0 collective-permute-done.13.refs_13_
  89.7 1.0 %collective-permute-done.15.refs_15_ = bf16[24,3328]{1,0:T(8,128)(2,1)S(1)} collective-permute-done((bf16[24,3328]{1,0:T(8,128)(2,1)S(1)}, bf16[24,3328]{1,0:T(8,128)(2,1)S(1)}, u32[]{:S(2)}, u32[]{:S(2)}) %collective-permute-start.15) | collective-permute-done | bytes 159776 | tf_op jit(solution)/shard_map/ppermute | solution.py:845
  90.7 3.1 %assemble.1 = (bf16[24,24,2048]{2,1,0:T(8,128)(2,1)}, f32[32,32]{1,0:T(8,128)}, f32[1,32]{1,0:T(1,128)}) custom-call(s32[1]{0:T(128)} %bitcast.2.me_ref, bf16[24,3328]{1,0:T(8,128)(2,1)S(1)} %make_shard.1.refs_0_, bf16[24,3328]{1,0:T(8,128)(2,1)S(1)} %collective-permute-done.5.refs_1_, bf16[24,3328]{1,0:T(8,128)(2,1)S(1)} %collective-permute-done.1.refs_2_, ...), custom_call_target="tpu_custom_call" | custom-call | flops 1000000 | bytes 8388608 | tf_op jit(solution)/shard_map/assemble/pallas_call | solution.py:756
  (1 shorter events, 0.0 us)
Async XLA Ops:
  0.6 10.2 %copy-start.1 = (f32[32]{0:T(128)S(1)}, f32[32]{0:T(128)}, u32[]{:S(2)}) copy-start(f32[32]{0:T(128)} %param.14) | copy-start | bytes 388
  0.6 10.2 %copy-start = (bf16[32,32]{1,0:T(8,128)(2,1)S(1)}, bf16[32,32]{1,0:T(8,128)(2,1)}, u32[]{:S(2)}) copy-start(bf16[32,32]{1,0:T(8,128)(2,1)} %l_ref.1) | copy-start | bytes 6148
  3.4 15.7 %all-to-all-start = ((bf16[16,8,768]{2,1,0:T(8,128)(2,1)}), bf16[16,8,768]{2,1,0:T(8,128)(2,1)S(1)}, u32[]{:S(2)}, u32[]{:S(2)}) async-start(bf16[16,8,768]{2,1,0:T(8,128)(2,1)} %bitcast.16), calls=%async_computation | async-start | bytes 393216 | tf_op jit(solution)/shard_map/all_to_all | solution.py:825
  41.3 12.5 %all-to-all-start.2 = ((bf16[16,8,768]{2,1,0:T(8,128)(2,1)}), bf16[16,8,768]{2,1,0:T(8,128)(2,1)S(1)}, u32[]{:S(2)}, u32[]{:S(2)}) async-start(bf16[16,8,768]{2,1,0:T(8,128)(2,1)} %bitcast.18), calls=%async_computation.2 | async-start | bytes 393216 | tf_op jit(solution)/shard_map/all_to_all | solution.py:825
  56.8 14.5 %all-to-all-start.3 = ((bf16[16,8,768]{2,1,0:T(8,128)(2,1)}), bf16[16,8,768]{2,1,0:T(8,128)(2,1)S(1)}, u32[]{:S(2)}, u32[]{:S(2)}) async-start(bf16[16,8,768]{2,1,0:T(8,128)(2,1)} %bitcast.17), calls=%async_computation.3 | async-start | bytes 393216 | tf_op jit(solution)/shard_map/all_to_all | solution.py:825
  62.7 1.4 %collective-permute-start = (f32[24,1024]{1,0:T(8,128)S(1)}, f32[24,1024]{1,0:T(8,128)S(1)}, u32[]{:S(2)}, u32[]{:S(2)}) collective-permute-start(f32[24,1024]{1,0:T(8,128)S(1)} %get-tuple-element.44), channel_id=1, source_target_pairs={{0,1},{1,0},{2,3},{3,2},{4,5},{5,4},{6,7},{7,6},{8,9},{9,8},{10,11... | collective-permute-start | bytes 294920 | tf_op jit(solution)/shard_map/ppermute | solution.py:903
  64.1 6.7 %collective-permute-start.2 = (bf16[24,3328]{1,0:T(8,128)(2,1)S(1)}, bf16[24,3328]{1,0:T(8,128)(2,1)S(1)}, u32[]{:S(2)}, u32[]{:S(2)}) collective-permute-start(bf16[24,3328]{1,0:T(8,128)(2,1)S(1)} %make_shard.1.refs_0_), channel_id=1, source_target_pairs={{0,2},{1,3},{4,0},{5,1},{8,4},{9,5},{12,8},{13,9},{14,12},{15,13},... | collective-permute-start | bytes 479240 | tf_op jit(solution)/shard_map/ppermute | solution.py:852
  65.5 5.8 %collective-permute-start.1 = (bf16[24,3328]{1,0:T(8,128)(2,1)S(1)}, bf16[24,3328]{1,0:T(8,128)(2,1)S(1)}, u32[]{:S(2)}, u32[]{:S(2)}) collective-permute-start(bf16[24,3328]{1,0:T(8,128)(2,1)S(1)} %make_shard.1.refs_0_), channel_id=1, source_target_pairs={{0,4},{1,5},{4,8},{5,9},{8,12},{9,13},{12,14},{13,15},{14,10},{15,... | collective-permute-start | bytes 479240 | tf_op jit(solution)/shard_map/ppermute | solution.py:850
  71.4 5.3 %collective-permute-start.3 = (bf16[24,3328]{1,0:T(8,128)(2,1)S(1)}, bf16[24,3328]{1,0:T(8,128)(2,1)S(1)}, u32[]{:S(2)}, u32[]{:S(2)}) collective-permute-start(bf16[24,3328]{1,0:T(8,128)(2,1)S(1)} %collective-permute-done.1.refs_2_), channel_id=1, source_target_pairs={{0,4},{1,5},{4,8},{5,9},{8,12},{9,13},{12,14},{13,15},{14,10},{15,... | collective-permute-start | bytes 479240 | tf_op jit(solution)/shard_map/ppermute | solution.py:850
  72.6 4.5 %collective-permute-start.4 = (bf16[24,3328]{1,0:T(8,128)(2,1)S(1)}, bf16[24,3328]{1,0:T(8,128)(2,1)S(1)}, u32[]{:S(2)}, u32[]{:S(2)}) collective-permute-start(bf16[24,3328]{1,0:T(8,128)(2,1)S(1)} %collective-permute-done.2.refs_4_), channel_id=1, source_target_pairs={{0,2},{1,3},{4,0},{5,1},{8,4},{9,5},{12,8},{13,9},{14,12},{15,13},... | collective-permute-start | bytes 479240 | tf_op jit(solution)/shard_map/ppermute | solution.py:852
  77.0 4.3 %collective-permute-start.10 = (bf16[24,3328]{1,0:T(8,128)(2,1)S(1)}, bf16[24,3328]{1,0:T(8,128)(2,1)S(1)}, u32[]{:S(2)}, u32[]{:S(2)}) collective-permute-start(bf16[24,3328]{1,0:T(8,128)(2,1)S(1)} %collective-permute-done.3.refs_6_), channel_id=1, source_target_pairs={{0,4},{1,5},{4,8},{5,9},{8,12},{9,13},{12,14},{13,15},{14,10},{15,... | collective-permute-start | bytes 479240 | tf_op jit(solution)/shard_map/ppermute | solution.py:850
  77.9 4.1 %collective-permute-start.5 = (bf16[24,3328]{1,0:T(8,128)(2,1)S(1)}, bf16[24,3328]{1,0:T(8,128)(2,1)S(1)}, u32[]{:S(2)}, u32[]{:S(2)}) collective-permute-start(bf16[24,3328]{1,0:T(8,128)(2,1)S(1)} %make_shard.1.refs_0_), channel_id=1, source_target_pairs={{0,1},{1,0},{2,3},{3,2},{4,5},{5,4},{6,7},{7,6},{8,9},{9,8},{10,11... | collective-permute-start | bytes 479240 | tf_op jit(solution)/shard_map/ppermute | solution.py:845
  79.6 5.3 %collective-permute-start.6 = (bf16[24,3328]{1,0:T(8,128)(2,1)S(1)}, bf16[24,3328]{1,0:T(8,128)(2,1)S(1)}, u32[]{:S(2)}, u32[]{:S(2)}) collective-permute-start(bf16[24,3328]{1,0:T(8,128)(2,1)S(1)} %collective-permute-done.1.refs_2_), channel_id=1, source_target_pairs={{0,1},{1,0},{2,3},{3,2},{4,5},{5,4},{6,7},{7,6},{8,9},{9,8},{10,11... | collective-permute-start | bytes 479240 | tf_op jit(solution)/shard_map/ppermute | solution.py:845
  79.6 5.4 %collective-permute-start.7 = (bf16[24,3328]{1,0:T(8,128)(2,1)S(1)}, bf16[24,3328]{1,0:T(8,128)(2,1)S(1)}, u32[]{:S(2)}, u32[]{:S(2)}) collective-permute-start(bf16[24,3328]{1,0:T(8,128)(2,1)S(1)} %collective-permute-done.2.refs_4_), channel_id=1, source_target_pairs={{0,1},{1,0},{2,3},{3,2},{4,5},{5,4},{6,7},{7,6},{8,9},{9,8},{10,11... | collective-permute-start | bytes 479240 | tf_op jit(solution)/shard_map/ppermute | solution.py:845
  80.1 5.7 %collective-permute-start.12 = (bf16[24,3328]{1,0:T(8,128)(2,1)S(1)}, bf16[24,3328]{1,0:T(8,128)(2,1)S(1)}, u32[]{:S(2)}, u32[]{:S(2)}) collective-permute-start(bf16[24,3328]{1,0:T(8,128)(2,1)S(1)} %collective-permute-done.4.refs_8_), channel_id=1, source_target_pairs={{0,2},{1,3},{4,0},{5,1},{8,4},{9,5},{12,8},{13,9},{14,12},{15,13},... | collective-permute-start | bytes 479240 | tf_op jit(solution)/shard_map/ppermute | solution.py:852
  81.3 5.3 %collective-permute-start.14 = (bf16[24,3328]{1,0:T(8,128)(2,1)S(1)}, bf16[24,3328]{1,0:T(8,128)(2,1)S(1)}, u32[]{:S(2)}, u32[]{:S(2)}) collective-permute-start(bf16[24,3328]{1,0:T(8,128)(2,1)S(1)} %collective-permute-done.10.refs_10_), channel_id=1, source_target_pairs={{0,4},{1,5},{4,8},{5,9},{8,12},{9,13},{12,14},{13,15},{14,10},{15,... | collective-permute-start | bytes 479240 | tf_op jit(solution)/shard_map/ppermute | solution.py:850
  82.1 7.6 %collective-permute-start.8 = (bf16[24,3328]{1,0:T(8,128)(2,1)S(1)}, bf16[24,3328]{1,0:T(8,128)(2,1)S(1)}, u32[]{:S(2)}, u32[]{:S(2)}) collective-permute-start(bf16[24,3328]{1,0:T(8,128)(2,1)S(1)} %collective-permute-done.3.refs_6_), channel_id=1, source_target_pairs={{0,1},{1,0},{2,3},{3,2},{4,5},{5,4},{6,7},{7,6},{8,9},{9,8},{10,11... | collective-permute-start | bytes 479240 | tf_op jit(solution)/shard_map/ppermute | solution.py:845
  84.9 4.7 %collective-permute-start.9 = (bf16[24,3328]{1,0:T(8,128)(2,1)S(1)}, bf16[24,3328]{1,0:T(8,128)(2,1)S(1)}, u32[]{:S(2)}, u32[]{:S(2)}) collective-permute-start(bf16[24,3328]{1,0:T(8,128)(2,1)S(1)} %collective-permute-done.4.refs_8_), channel_id=1, source_target_pairs={{0,1},{1,0},{2,3},{3,2},{4,5},{5,4},{6,7},{7,6},{8,9},{9,8},{10,11... | collective-permute-start | bytes 479240 | tf_op jit(solution)/shard_map/ppermute | solution.py:845
  85.0 4.6 %collective-permute-start.11 = (bf16[24,3328]{1,0:T(8,128)(2,1)S(1)}, bf16[24,3328]{1,0:T(8,128)(2,1)S(1)}, u32[]{:S(2)}, u32[]{:S(2)}) collective-permute-start(bf16[24,3328]{1,0:T(8,128)(2,1)S(1)} %collective-permute-done.10.refs_10_), channel_id=1, source_target_pairs={{0,1},{1,0},{2,3},{3,2},{4,5},{5,4},{6,7},{7,6},{8,9},{9,8},{10,11... | collective-permute-start | bytes 479240 | tf_op jit(solution)/shard_map/ppermute | solution.py:845
  85.9 3.8 %collective-permute-start.13 = (bf16[24,3328]{1,0:T(8,128)(2,1)S(1)}, bf16[24,3328]{1,0:T(8,128)(2,1)S(1)}, u32[]{:S(2)}, u32[]{:S(2)}) collective-permute-start(bf16[24,3328]{1,0:T(8,128)(2,1)S(1)} %collective-permute-done.12.refs_12_), channel_id=1, source_target_pairs={{0,1},{1,0},{2,3},{3,2},{4,5},{5,4},{6,7},{7,6},{8,9},{9,8},{10,11... | collective-permute-start | bytes 479240 | tf_op jit(solution)/shard_map/ppermute | solution.py:845
  86.7 4.0 %collective-permute-start.15 = (bf16[24,3328]{1,0:T(8,128)(2,1)S(1)}, bf16[24,3328]{1,0:T(8,128)(2,1)S(1)}, u32[]{:S(2)}, u32[]{:S(2)}) collective-permute-start(bf16[24,3328]{1,0:T(8,128)(2,1)S(1)} %collective-permute-done.14.refs_14_), channel_id=1, source_target_pairs={{0,1},{1,0},{2,3},{3,2},{4,5},{5,4},{6,7},{7,6},{8,9},{9,8},{10,11... | collective-permute-start | bytes 479240 | tf_op jit(solution)/shard_map/ppermute | solution.py:845

commit v3 on v2

--- a/solution.py
+++ b/solution.py
@@ -432,7 +432,7 @@
     return jnp.concatenate([jnp.concatenate(real, axis=1), jnp.concatenate(imag, axis=1)], axis=0).astype(BF16)
 
 
-def mode_step(pencil, spread_w, forward, inverse, chans, adjoint):
+def mode_step(pencil, spread_w, forward, inverse, chans):
     modes_x = forward.shape[0] // 2
 
     def kernel(p_ref, w_hbm, f_hbm, i_hbm, spec_ref, out_hbm, w_ref, f_ref, i_ref, out_ref, sem, out_sem):
@@ -442,7 +442,7 @@
         spec_ref[...] = spec
         copies[1].wait()
         copies[2].wait()
-        mixed = weigh(spec, w_ref, chans, modes_x, adjoint)
+        mixed = weigh(spec, w_ref, chans, modes_x, False)
         out_ref[...] = dot(i_ref[...], mixed).astype(BF16)
         copy = pltpu.make_async_copy(out_ref, out_hbm, out_sem)
         copy.start()
@@ -466,13 +466,46 @@
         ],
         compiler_params=params(),
         cost_estimate=cost(2 * 48 * 6 * 128 * 4096, spread_w.size * 4),
-        name="adjoint_step" if adjoint else "mode_step",
+        name="mode_step",
     )(pencil, *in_hbm(spread_w, forward, inverse))
+
+
+def adjoint_step(grads, spread_w, inverse, chans):
+    modes_x = grads.shape[0] // 2
+    shape = (inverse.shape[0], grads.shape[1])
+
+    def kernel(g_ref, w_hbm, i_hbm, out_hbm, w_ref, i_ref, out_ref, sem, out_sem):
+        for copy in start_all([(w_hbm, w_ref), (i_hbm, i_ref)], sem):
+            copy.wait()
+        mixed = weigh(g_ref[...], w_ref, chans, modes_x, True)
+        out_ref[...] = dot(i_ref[...], mixed).astype(BF16)
+        copy = pltpu.make_async_copy(out_ref, out_hbm, out_sem)
+        copy.start()
+        copy.wait()
+
+    return pl.pallas_call(
+        kernel,
+        in_specs=[vmem(), hbm(), hbm()],
+        out_specs=hbm(),
+        out_shape=pltpu.HBM(shape, BF16),
+        scratch_shapes=[
+            pltpu.VMEM(spread_w.shape, BF16),
+            pltpu.VMEM(inverse.shape, BF16),
+            pltpu.VMEM(shape, BF16),
+            pltpu.SemaphoreType.DMA((2,)),
+            pltpu.SemaphoreType.DMA,
+        ],
+        compiler_params=params(),
+        cost_estimate=cost(2 * 48 * 6 * 128 * 4096, spread_w.size * 4),
+        name="adjoint_step",
+    )(grads, *in_hbm(spread_w, inverse))
 
 
 def pointwise(field, cotangent, pencil, table_t, table, block_weight, bias_row, chips, half):
     rows, length, width = field.shape
-    chunk = 64
+    chunk, sub = 128, 16
+    modes = table.shape[0]
+    depth = table_t.shape[1]
 
     def kernel(
         u_hbm, c_hbm, p_ref, tt_hbm, t_hbm, w_hbm, b_hbm, out_hbm, dpre_hbm, send_hbm,
@@ -480,37 +513,49 @@
     ):
         copies = start_all([(tt_hbm, tt_ref), (w_hbm, w_ref), (b_hbm, b_ref), (t_hbm, t_ref)], sem)
         for x in range(rows):
-            pltpu.make_async_copy(u_hbm.at[x], u_ref.at[x], sem.at[5 + x]).start()
-            pltpu.make_async_copy(c_hbm.at[x], c_ref.at[x], sem.at[5 + rows + x]).start()
+            pltpu.make_async_copy(u_hbm.at[x], u_ref.at[x], sem.at[4 + x]).start()
+            pltpu.make_async_copy(c_hbm.at[x], c_ref.at[x], sem.at[4 + rows + x]).start()
         for copy in copies:
             copy.wait()
         cut_lanes(bscr, p_ref)
         root = math.sqrt(2.0 / math.pi)
+        bias = b_ref[0:1, :]
+        high = bias.astype(BF16)
+        mid = (bias - high.astype(F32)).astype(BF16)
+        low = (bias - high.astype(F32) - mid.astype(F32)).astype(BF16)
+        parts = [t.astype(F32) for t in (high, mid, low)]
+        bias = jnp.concatenate(parts + [jnp.zeros((depth - modes - 3, width), F32)], axis=0)
+        bias = (0.5 * bias).astype(BF16)
+        weight = (0.5 * w_ref[...].astype(F32)).astype(BF16)
 
         def one_row(x):
-            pltpu.make_async_copy(u_hbm.at[x], u_ref.at[x], sem.at[5 + x]).wait()
-            pltpu.make_async_copy(c_hbm.at[x], c_ref.at[x], sem.at[5 + rows + x]).wait()
-            bias = b_ref[0:1, :]
-            coeff = gather_rows(bscr, x, chips, half)
+            pltpu.make_async_copy(u_hbm.at[x], u_ref.at[x], sem.at[4 + x]).wait()
+            pltpu.make_async_copy(c_hbm.at[x], c_ref.at[x], sem.at[4 + rows + x]).wait()
+            coeff = (0.5 * gather_rows(bscr, x, chips, half).astype(F32)).astype(BF16)
+            coeff = jnp.concatenate([coeff, bias], axis=0)
             for k in range(length // chunk):
                 where = pl.ds(k * chunk, chunk)
-                u = u_ref[x, where, :]
-                spec = dot(tt_ref[where, :], coeff)
                 for h in range(2):
                     lanes = slice(h * half, (h + 1) * half)
-                    pre = spec[:, lanes] + dot(u[:, lanes], w_ref[...]) + bias[:, lanes]
-                    inner = pre * (root + (root * 0.044715) * (pre * pre))
-                    th = jnp.tanh(inner)
-                    cdf = 0.5 * th + 0.5
-                    out_ref[x, where, lanes] = (pre * cdf).astype(BF16)
-                    slope = 6.0 * inner - (4.0 * root) * pre
-                    grad = cdf + (cdf - cdf * cdf) * slope
-                    dpre_ref[x, where, lanes] = (c_ref[x, where, lanes].astype(F32) * grad).astype(BF16)
+                    left = jnp.concatenate([u_ref[x, where, lanes], tt_ref[where, :]], axis=1)
+                    right = jnp.concatenate([weight, coeff[:, lanes]], axis=0)
+                    halved = dot(left, right)
+                    for at in range(0, chunk, sub):
+                        place = pl.ds(k * chunk + at, sub)
+                        p = halved[at : at + sub]
+                        inner = p * (2.0 * root + (8.0 * root * 0.044715) * (p * p))
+                        th = jnp.tanh(inner)
+                        twice = 1.0 + th
+                        out_ref[x, place, lanes] = (p * twice).astype(BF16)
+                        slope = 1.5 * inner - (2.0 * root) * p
+                        grad = twice * (0.5 + (1.0 - th) * slope)
+                        dpre_ref[x, place, lanes] = (c_ref[x, place, lanes].astype(F32) * grad).astype(BF16)
             pltpu.make_async_copy(out_ref.at[x], out_hbm.at[x], out_sem.at[x]).start()
             pltpu.make_async_copy(dpre_ref.at[x], dpre_hbm.at[x], out_sem.at[rows + x]).start()
             scatter_rows(dscr, dot(t_ref[...], dpre_ref[x]), x, chips, half)
 
-        pl.loop(0, rows)(one_row)
+        for x in range(rows):
+            one_row(x)
         join_lanes(send_ref, dscr)
         pltpu.make_async_copy(send_ref, send_hbm, out_sem.at[2 * rows]).start()
         for x in range(rows):
@@ -539,7 +584,7 @@
             pltpu.VMEM(pencil.shape, BF16),
             pltpu.VMEM(cut_shape(pencil.shape), F32),
             pltpu.VMEM(cut_shape(pencil.shape), F32),
-            pltpu.SemaphoreType.DMA((5 + 2 * rows,)),
+            pltpu.SemaphoreType.DMA((4 + 2 * rows,)),
             pltpu.SemaphoreType.DMA((2 * rows + 1,)),
         ],
         compiler_params=params(),
@@ -608,7 +653,7 @@
     )(*in_hbm(field, dpre))
 
 
-def weight_sums(me, spectrum, grads, chans):
+def weight_sums(spectrum, pencil, forward, chans):
     modes_x = spectrum.shape[0] // 2
     tiles = spectrum.shape[1] // LANES
     groups = LANES // chans
@@ -616,12 +661,15 @@
     full = chans * chans
     parts = full // step
 
-    def kernel(me_ref, u_ref, d_ref, own_ref, keep_ref, send_ref):
+    def kernel(u_ref, p_ref, f_hbm, d_ref, own_ref, shared_ref, f_ref, sem):
+        copy = start_all([(f_hbm, f_ref)], sem)[0]
+
         def stack(ref):
             return jnp.concatenate([ref[:, k * LANES : (k + 1) * LANES] for k in range(tiles)], axis=0)
 
-        first = me_ref[0] % 2 == 0
         left = stack(u_ref)
+        copy.wait()
+        d_ref[...] = dot(f_ref[...], p_ref[...]).astype(BF16)
         repeat = jnp.concatenate(
             [lane_equals(LANES, LANES, lambda l: l % chans, chans * g) for g in range(groups)], axis=1
         )
@@ -644,47 +692,50 @@
                             key = (kind, t, z)
                             sums[key] = term if key not in sums else sums[key] + term
             for t in range(2):
-                own = jnp.concatenate([sums[0, t, 0], sums[0, t, 1]], axis=1)
-                own_ref[:, t * full + a * step : t * full + (a + 1) * step] = own.astype(BF16)
-                shared = jnp.concatenate([sums[1, t, 0], sums[1, t, 1]], axis=1)
-                at = t * (full // 2) + (a % (parts // 2)) * step
-                low = a < parts // 2
-
-                @pl.when(first if low else jnp.logical_not(first))
-                def _():
-                    keep_ref[:, at : at + step] = shared
-
-                @pl.when(jnp.logical_not(first) if low else first)
-                def _():
-                    send_ref[:, at : at + step] = shared
-
-    half_shape = jax.ShapeDtypeStruct((modes_x, full), F32)
+                lanes = slice(t * full + a * step, t * full + (a + 1) * step)
+                own_ref[:, lanes] = jnp.concatenate([sums[0, t, 0], sums[0, t, 1]], axis=1).astype(BF16)
+                shared_ref[:, lanes] = jnp.concatenate([sums[1, t, 0], sums[1, t, 1]], axis=1)
+
     return pl.pallas_call(
         kernel,
-        in_specs=[smem(), vmem(), vmem()],
-        out_shape=(jax.ShapeDtypeStruct((modes_x, 2 * full), BF16), half_shape, half_shape),
+        in_specs=[vmem(), vmem(), hbm()],
+        out_shape=(
+            jax.ShapeDtypeStruct(spectrum.shape, BF16),
+            jax.ShapeDtypeStruct((modes_x, 2 * full), BF16),
+            jax.ShapeDtypeStruct((modes_x, 2 * full), F32),
+        ),
+        scratch_shapes=[pltpu.VMEM(forward.shape, BF16), pltpu.SemaphoreType.DMA((1,))],
         compiler_params=params(),
         cost_estimate=cost(2 * 288 * 128 * 4096, 4 * 1024 * 1024),
         name="weight_sums",
-    )(me, spectrum, grads)
-
-
-def make_shard(own, keep, other, stats):
+    )(spectrum, pencil, *in_hbm(forward))
+
+
+def make_shard(me, own, shared, other, stats):
     rows, full2 = own.shape
-    full = keep.shape[1]
+    full = full2 // 2
+    half = full // 2
     width = full2 + full + stats.shape[1]
 
-    def kernel(o_ref, k_ref, r_ref, s_ref, out_ref):
+    def kernel(me_ref, o_ref, s_ref, r_ref, st_ref, out_ref):
+        first = me_ref[0] % 2 == 0
         out_ref[:, 0:full2] = o_ref[...]
-        out_ref[:, full2 : full2 + full] = (k_ref[...] + r_ref[...]).astype(BF16)
-        out_ref[:, full2 + full :] = s_ref[...]
+        for t in range(2):
+            low = slice(t * full, t * full + half)
+            high = slice(t * full + half, (t + 1) * full)
+            mine = jnp.where(first, s_ref[:, low], s_ref[:, high])
+            theirs = jnp.where(first, r_ref[:, low], r_ref[:, high])
+            out_ref[:, full2 + t * half : full2 + (t + 1) * half] = (mine + theirs).astype(BF16)
+        out_ref[:, full2 + full :] = st_ref[...]
 
     return pl.pallas_call(
         kernel,
+        in_specs=[smem()] + [vmem()] * 4,
         out_shape=jax.ShapeDtypeStruct((rows, width), BF16),
         compiler_params=params(),
+        cost_estimate=cost(100000, 1000000),
         name="make_shard",
-    )(own, keep, other, stats)
+    )(me, own, shared, other, stats)
 
 
 def ring_chip(spot, chips):
@@ -695,15 +746,48 @@
     return jnp.where(chip % 2 == 0, chip // 2, chips - 1 - chip // 2)
 
 
-def assemble(me, shards_all, turns, modes_y, chans, chips):
+def read_sums(ref, full):
+    left = ref[:, 3 * full : 3 * full + LANES].astype(F32)
+    right = ref[:, 3 * full + LANES : 3 * full + 2 * LANES].astype(F32)
+    middle = jnp.concatenate([left[16:24], right[0:8]], axis=0)
+    return left[0:16] + middle + right[8:24]
+
+
+def early_sums(shards_all, chans):
+    count = len(shards_all)
+    shape = (count, 16, LANES)
+
+    def kernel(*refs):
+        ins, (out_hbm, out_ref, sem) = refs[:count], refs[count:]
+        for n in range(count):
+            out_ref[n] = read_sums(ins[n], chans * chans)
+        copy = pltpu.make_async_copy(out_ref, out_hbm, sem)
+        copy.start()
+        copy.wait()
+
+    return pl.pallas_call(
+        kernel,
+        in_specs=[vmem()] * count,
+        out_specs=hbm(),
+        out_shape=pltpu.HBM(shape, F32),
+        scratch_shapes=[pltpu.VMEM(shape, F32), pltpu.SemaphoreType.DMA],
+        compiler_params=params(),
+        cost_estimate=cost(3 * 10**10, 4 * 1024 * 1024),
+        name="early_sums",
+    )(*shards_all)
+
+
+def assemble(me, early, shards_all, turns, modes_y, chans, chips):
     rows = shards_all[0].shape[0]
     full = chans * chans
+    tiles = 2 * full // LANES
+    part = full // 2 // LANES
     count = len(shards_all)
-    step = 2 * LANES
-    blocks = 2 * full // LANES
-
-    def kernel(me_ref, *refs):
-        ins, (g_ref, l_ref, b_ref, scr, stat, out, sem) = refs[:count], refs[count:]
+
+    def kernel(me_ref, e_hbm, *refs):
+        ins, (g_ref, l_ref, b_ref, scr, stat, out, e_ref, sem) = refs[:count], refs[count:]
+        fetch = pltpu.make_async_copy(e_hbm, e_ref, sem.at[tiles // 4])
+        fetch.start()
         spot = ring_spot(me_ref[0] // 2, chips)
         places = []
         for back, swapped in turns:
@@ -711,23 +795,18 @@
             core = me_ref[0] % 2
             places.append((chip, 1 - core if swapped else core))
         copies = []
-        for k in range(blocks):
-            for n in range(count):
-                chip, core = places[n]
+        for k in range(tiles):
+            keeper = k % (2 * part) // part
+            at = tiles + k // (2 * part) * part + k % part
+            for n, (chip, core) in enumerate(places):
                 own = pl.ds(chip + 2 * chips * core, rows, stride=modes_y)
                 scr[k, own, :] = ins[n][:, k * LANES : (k + 1) * LANES].astype(F32)
-            part = k % (blocks // 2)
-            from_core = part // (blocks // 4)
-            at = 2 * full + (k // (blocks // 2)) * (full // 2) + (part % (blocks // 4)) * LANES
-            for n in range(count):
                 if turns[n][1]:
                     continue
-                chip, core = places[n]
                 mate = turns.index((turns[n][0], True))
-                here = ins[n][:, at : at + LANES].astype(F32)
-                there = ins[mate][:, at : at + LANES].astype(F32)
-                where = pl.ds(chip + chips, rows, stride=modes_y)
-                scr[k, where, :] = jnp.where(core == from_core, here, there)
+                lanes = slice(at * LANES, (at + 1) * LANES)
+                shared = pl.ds(chip + chips, rows, stride=modes_y)
+                scr[k, shared, :] = jnp.where(core == keeper, ins[n][:, lanes], ins[mate][:, lanes]).astype(F32)
             lanes = slice(k * LANES, (k + 1) * LANES)
             for j in range(rows):
                 out[j, :, lanes] = scr[k, j * modes_y : (j + 1) * modes_y, :].astype(BF16)
@@ -735,12 +814,9 @@
                 lanes = pl.ds((k - 3) * LANES, 4 * LANES)
                 copies.append(pltpu.make_async_copy(out.at[:, :, lanes], g_ref.at[:, :, lanes], sem.at[k // 4]))
                 copies[-1].start()
-        for n in range(count):
-            chip, core = places[n]
-            left = ins[n][:, 3 * full : 3 * full + LANES].astype(F32)
-            right = ins[n][:, 3 * full + LANES :].astype(F32)
-            middle = jnp.concatenate([left[16:24], right[0:8]], axis=0)
-            stat[2 * chip + core] = left[0:16] + middle + right[8:24]
+        fetch.wait()
+        for n, (chip, core) in enumerate(places):
+            stat[2 * chip + core] = e_ref[n] if n < early.shape[0] else read_sums(ins[n], full)
         total = stat[0]
         for n in range(1, count):
             total = total + stat[n]
@@ -751,27 +827,27 @@
         for copy in copies:
             copy.wait()
 
-    vmem = pl.BlockSpec(memory_space=pltpu.VMEM)
     shape = (rows, modes_y, 2 * full)
     return pl.pallas_call(
         kernel,
-        in_specs=[pl.BlockSpec(memory_space=pltpu.SMEM)] + [vmem] * count,
-        out_specs=(pl.BlockSpec(memory_space=pl.ANY), vmem, vmem),
+        in_specs=[smem(), hbm()] + [vmem()] * count,
+        out_specs=(hbm(), vmem(), vmem()),
         out_shape=(
-            jax.ShapeDtypeStruct(shape, BF16),
+            pltpu.HBM(shape, BF16),
             jax.ShapeDtypeStruct((chans, chans), F32),
             jax.ShapeDtypeStruct((1, chans), F32),
         ),
         scratch_shapes=[
-            pltpu.VMEM((blocks, rows * modes_y, LANES), F32),
+            pltpu.VMEM((tiles, rows * modes_y, LANES), F32),
             pltpu.VMEM((count, 16, LANES), F32),
             pltpu.VMEM(shape, BF16),
-            pltpu.SemaphoreType.DMA((blocks // 4,)),
+            pltpu.VMEM(early.shape, F32),
+            pltpu.SemaphoreType.DMA((tiles // 4 + 1,)),
         ],
         compiler_params=params(),
         cost_estimate=cost(1000000, 8 * 1024 * 1024),
         name="assemble",
-    )(me, *shards_all)
+    )(me, *in_hbm(early), *shards_all)
 
 
 def back_to_field(dpre, pencil, table_t, block_weight, chips, half):
@@ -881,6 +957,9 @@
     table_y = np_ytable(modes_y, length_y, False)
     table_yw = np_ytable(modes_y, length_y, True)
     table_y_t, table_yw_t = (np.ascontiguousarray(t.T) for t in (table_y, table_yw))
+    ones = np.ones((length_y, 3), table_yw_t.dtype)
+    zeros = np.zeros((length_y, -(table_yw_t.shape[1] + 3) % 16), table_yw_t.dtype)
+    table_yw_t = np.concatenate([table_yw_t, ones, zeros], axis=1)
     forward, inverse = np_xtables(modes_x, rows * devices)
     me_id = me.astype(jnp.int32)[None]
 
@@ -889,7 +968,7 @@
     plain, turned, block, block_t, bias_row = prepare(
         me_id, spectral_weight, local_weight, bias[None, :], chips, half
     )
-    spectrum, send = mode_step(pencil, plain, forward, inverse, chans, False)
+    spectrum, send = mode_step(pencil, plain, forward, inverse, chans)
     pencil = exchange(send)
     output_field, dpre, send = pointwise(
         field, cotangent, pencil, table_yw_t, table_yw, block, bias_row, chips, half
@@ -897,26 +976,32 @@
     pencil = exchange(send)
     stats = local_sums(field, dpre, chans, half)
     pencil, stats = lax.optimization_barrier((pencil, stats))
-    grads, send = mode_step(pencil, turned, forward, inverse, chans, True)
+    grads, own, shared = weight_sums(spectrum, pencil, forward, chans)
+    other = lax.ppermute(shared, "xy", [(i, i ^ 1) for i in range(devices)])
+    shard = make_shard(me_id, own, shared, other, stats)
+
+    ring = Ring(shard, chips)
+    grads = ring.tie(grads)
+    ring.hop()
+    send = adjoint_step(grads, turned, inverse, chans)
+    send = ring.tie(send)
+    ring.settle()
+    early = list(ring.parts)
+    ring.hop()
     pencil = exchange(send)
-    own, keep, give = weight_sums(me_id, spectrum, grads, chans)
-    got = lax.ppermute(give, "xy", [(i, i ^ 1) for i in range(devices)])
-    shard = make_shard(own, keep, got, stats)
-
-    ring = Ring(shard, chips)
+    ring.settle()
+    sums = early_sums(early, chans)
+    sums = ring.tie(sums)
     ring.hop()
-    pencil = ring.tie(pencil)
+    pencil, sums = lax.optimization_barrier((pencil, sums))
     ring.settle()
     ring.hop()
     field_grad = back_to_field(dpre, pencil, table_y_t, block_t, chips, half)
-    field_grad = ring.tie(field_grad)
+    field_grad = ring.hold(field_grad)
     ring.settle()
-    ring.hop()
-    ring.settle()
-    ring.hop()
-    ring.settle()
-    parts, turns = ring.parts, ring.turns
-    spectral_grad, local_grad, bias_grad = assemble(me_id, parts, turns, modes_y, chans, chips)
+    spectral_grad, local_grad, bias_grad = assemble(
+        me_id, sums, ring.parts, ring.turns, modes_y, chans, chips
+    )
     return output_field, field_grad, spectral_grad, local_grad, bias_grad.reshape(chans)
 
 

time: 94.8 us -> 90.8 us (0.958)
  starting transfers between devices: 31.8 us -> 27.8 us
    ppermute x3, waiting for transfers between devices: 6.02 us -> 0.02 us  [hop(): self.back = lax.ppermute(self.back, 'xy', self.hops[-1])]
    ppermute x4, waiting for transfers between devices: 0.52 us -> 5.71 us  [hop(): self.ahead = lax.ppermute(self.ahead, 'xy', self.hops[1])]
    ppermute x8, starting transfers between devices: 9.33 us -> 4.24 us  [keep(): self.parts.append(lax.ppermute(piece, 'xy', self.swap))]
    pallas_call x3 -> x5, Pallas kernels: 4.52 us -> 8.77 us  [the longest x1 3.37 us: assemble(): pl.pallas_call(kernel, in_specs=[smem(), hbm()] + [vmem()] * count, out_s...]
    pallas_call x2 -> x1, Pallas kernels: 6.01 us -> 3.01 us  [mode_step(): pl.pallas_call(kernel, in_specs=[vmem()] + [hbm()] * 3, out_specs=(vmem()...]
    ppermute x1, starting transfers between devices: 0.29 us -> 1.24 us  [fast_shards(): other = lax.ppermute(shared, 'xy', [(i, i ^ 1) for i in range(devices)])]
  transfers between devices with their start and end apart: 19 -> 19, of which waited for: 8 -> 5; matrix products, arithmetic and copies ran while one was open for 0% -> 0% of each run, Pallas kernels for 13% -> 16%
where the time goes in v3:
time: 90.8 us; the launch traced here: 89.7 us
  Pallas kernels  31.9 us (35%)
  starting transfers between devices  27.8 us (31%)
  waiting for transfers between devices  17 us (19%)
  blocking collectives  12.1 us (13%)
  between operations  0.98 us (1%)
    all_to_all x3, starting transfers between devices, exchange(): return lax.all_to_all(pencil, 'xy', split_axis=0, concat_axis=0, tiled=True)  16.2 us
    all_to_all x1, blocking collectives, exchange(): return lax.all_to_all(pencil, 'xy', split_axis=0, concat_axis=0, tiled=True)  12.1 us
    all_to_all x3, waiting for transfers between devices, exchange(): return lax.all_to_all(pencil, 'xy', split_axis=0, concat_axis=0, tiled=True)  9.18 us
    pallas_call x1, Pallas kernels, pointwise(): pl.pallas_call(kernel, in_specs=[hbm(), hbm(), vmem()] + [hbm()] * 4, out...  6.4 us
    ppermute x4, waiting for transfers between devices, hop(): self.ahead = lax.ppermute(self.ahead, 'xy', self.hops[1])  5.71 us
    ppermute x8, starting transfers between devices, keep(): self.parts.append(lax.ppermute(piece, 'xy', self.swap))  4.24 us
    pallas_call x1, Pallas kernels, back_to_field(): pl.pallas_call(kernel, in_specs=[hbm(), vmem(), hbm(), hbm()], out_specs=...  3.82 us
    ppermute x4, starting transfers between devices, hop(): self.ahead = lax.ppermute(self.ahead, 'xy', self.hops[1])  3.67 us
  transfers between devices with their start and end apart: 19, of which 5 were waited for; matrix products, arithmetic and copies ran while one was open for 0% of the time, Pallas kernels for 16%

profile of v3, /device:TPU:1, one launch (start us, length us, event | category | flops | bytes accessed | tf_op | source)
XLA Modules:
  0.0 89.7 jit_solution(17793690114530984977)
XLA Ops:
  0.6 0.0 copy-start.1
  0.6 0.0 copy-start
  0.7 2.8 %rows_to_modes.1 = bf16[128,768]{1,0:T(8,128)(2,1)} custom-call(bf16[4,512,512]{2,1,0:T(8,128)(2,1)} %u_hbm.5, bf16[48,512]{1,0:T(8,128)(2,1)} %constant.16.clone.t_hbm), custom_call_target="tpu_custom_call" | custom-call | flops 100663296 | bytes 2097152 | tf_op jit(solution)/shard_map/rows_to_modes/pallas_call | solution.py:296
  3.4 7.4 %all-to-all-start = ((bf16[16,8,768]{2,1,0:T(8,128)(2,1)}), bf16[16,8,768]{2,1,0:T(8,128)(2,1)S(1)}, u32[]{:S(2)}, u32[]{:S(2)}) async-start(bf16[16,8,768]{2,1,0:T(8,128)(2,1)} %bitcast.16), calls=%async_computation | async-start | bytes 393216 | tf_op jit(solution)/shard_map/all_to_all | solution.py:901
  10.8 0.0 copy-done.1
  10.8 0.0 copy-done
  10.8 3.6 %prepare.1 = (bf16[8,96,512]{2,1,0:T(8,128)(2,1)}, bf16[8,96,512]{2,1,0:T(8,128)(2,1)}, bf16[256,256]{1,0:T(8,128)(2,1)}, bf16[256,256]{1,0:T(8,128)(2,1)}, f32[8,512]{1,0:T(8,128)}) custom-call(s32[1]{0:T(128)} %bitcast.2.me_ref, bf16[24,24,2048]{2,1,0:T(8,128)(2,1)} %w_hbm.1, bf16[32,32]{1,0:T(8,128)(2,1)S(1)} %copy-done, f32[1,32]{1,0:T(1,128)S(1)} %bitcast.15), custom_call_target="tpu_custom_call" | custom-call | flops 1000000 | bytes 4194304 | tf_op jit(solution)/shard_map/prepare/pallas_call | solution.py:382
  14.4 4.7 %all-to-all-done = bf16[16,8,768]{2,1,0:T(8,128)(2,1)S(1)} async-done(((bf16[16,8,768]{2,1,0:T(8,128)(2,1)}), bf16[16,8,768]{2,1,0:T(8,128)(2,1)S(1)}, u32[]{:S(2)}, u32[]{:S(2)}) %all-to-all-start) | async-done | bytes 196640 | tf_op jit(solution)/shard_map/all_to_all | solution.py:901
  19.1 3.0 %mode_step.1 = (bf16[48,768]{1,0:T(8,128)(2,1)S(1)}, bf16[128,768]{1,0:T(8,128)(2,1)}) custom-call(bf16[128,768]{1,0:T(8,128)(2,1)S(1)} %bitcast.13, bf16[8,96,512]{2,1,0:T(8,128)(2,1)} %get-tuple-element.36.w_hbm, bf16[48,128]{1,0:T(8,128)(2,1)} %constant.17.clone.f_hbm, bf16[128,48]{1,0:T(8,128)(2,1)} %constant.18.clone.i_hbm), custom_call_target="tpu_custom_call" | custom-call | flops 301989888 | bytes 1572864 | tf_op jit(solution)/shard_map/mode_step/pallas_call | solution.py:451
  22.1 12.1 %all_to_all.46 = bf16[16,8,768]{2,1,0:T(8,128)(2,1)S(1)} all-to-all(bf16[16,8,768]{2,1,0:T(8,128)(2,1)} %bitcast.19), channel_id=1, replica_groups=mesh['groups'=2,'xy'=16] {'xy'}, dimensions={0} | all-to-all | bytes 393216 | tf_op jit(solution)/shard_map/all_to_all | solution.py:901
  34.2 6.4 %pointwise.1 = (bf16[4,512,512]{2,1,0:T(8,128)(2,1)}, bf16[4,512,512]{2,1,0:T(8,128)(2,1)}, bf16[128,768]{1,0:T(8,128)(2,1)}) custom-call(bf16[4,512,512]{2,1,0:T(8,128)(2,1)} %u_hbm.5, bf16[4,512,512]{2,1,0:T(8,128)(2,1)} %c_hbm.1, bf16[128,768]{1,0:T(8,128)(2,1)S(1)} %bitcast.12, bf16[512,64]{1,0:T(8,128)(2,1)} %constant.19.clone.tt_hbm, ...), custom_call_target="tpu_custom_call" | custom-call | flops 1048576000 | bytes 8388608 | tf_op jit(solution)/shard_map/pointwise/pallas_call | solution.py:566
  40.6 4.5 %all-to-all-start.2 = ((bf16[16,8,768]{2,1,0:T(8,128)(2,1)}), bf16[16,8,768]{2,1,0:T(8,128)(2,1)S(1)}, u32[]{:S(2)}, u32[]{:S(2)}) async-start(bf16[16,8,768]{2,1,0:T(8,128)(2,1)} %bitcast.18), calls=%async_computation.2 | async-start | bytes 393216 | tf_op jit(solution)/shard_map/all_to_all | solution.py:901
  45.1 3.5 %local_sums.1.st_ref = bf16[24,256]{1,0:T(8,128)(2,1)S(1)} custom-call(bf16[4,512,512]{2,1,0:T(8,128)(2,1)} %u_hbm.5, bf16[4,512,512]{2,1,0:T(8,128)(2,1)} %get-tuple-element.43.d_hbm), custom_call_target="tpu_custom_call" | custom-call | flops 1048576000 | bytes 4194304 | tf_op jit(solution)/shard_map/local_sums/pallas_call | solution.py:640
  48.6 4.5 %all-to-all-done.2 = bf16[16,8,768]{2,1,0:T(8,128)(2,1)S(1)} async-done(((bf16[16,8,768]{2,1,0:T(8,128)(2,1)}), bf16[16,8,768]{2,1,0:T(8,128)(2,1)S(1)}, u32[]{:S(2)}, u32[]{:S(2)}) %all-to-all-start.2) | async-done | bytes 196640 | tf_op jit(solution)/shard_map/all_to_all | solution.py:901
  53.1 1.8 %weight_sums.1 = (bf16[48,768]{1,0:T(8,128)(2,1)S(1)}, bf16[24,2048]{1,0:T(8,128)(2,1)S(1)}, f32[24,2048]{1,0:T(8,128)S(1)}) custom-call(bf16[48,768]{1,0:T(8,128)(2,1)S(1)} %get-tuple-element.41.u_ref, bf16[128,768]{1,0:T(8,128)(2,1)S(1)} %bitcast.14, bf16[48,128]{1,0:T(8,128)(2,1)} %constant.17.clone.f_hbm), custom_call_target="tpu_custom_call" | custom-call | flops 301989888 | bytes 4194304 | tf_op jit(solution)/shard_map/weight_sums/pallas_call | solution.py:699
  54.9 1.2 %collective-permute-start = (f32[24,2048]{1,0:T(8,128)S(1)}, f32[24,2048]{1,0:T(8,128)S(1)}, u32[]{:S(2)}, u32[]{:S(2)}) collective-permute-start(f32[24,2048]{1,0:T(8,128)S(1)} %get-tuple-element.46.s_ref), channel_id=1, source_target_pairs={{0,1},{1,0},{2,3},{3,2},{4,5},{5,4},{6,7},{7,6},{8,9},{9,8},{10,11... | collective-permute-start | bytes 589832 | tf_op jit(solution)/shard_map/ppermute | solution.py:980
  56.1 1.1 %collective-permute-done.r_ref = f32[24,2048]{1,0:T(8,128)S(1)} collective-permute-done((f32[24,2048]{1,0:T(8,128)S(1)}, f32[24,2048]{1,0:T(8,128)S(1)}, u32[]{:S(2)}, u32[]{:S(2)}) %collective-permute-start) | collective-permute-done | bytes 196640 | tf_op jit(solution)/shard_map/ppermute | solution.py:980
  57.3 0.1 collective-permute-start.1
  57.3 1.5 %collective-permute-start.2 = (bf16[24,3328]{1,0:T(8,128)(2,1)S(1)}, bf16[24,3328]{1,0:T(8,128)(2,1)S(1)}, u32[]{:S(2)}, u32[]{:S(2)}) collective-permute-start(bf16[24,3328]{1,0:T(8,128)(2,1)S(1)} %make_shard.1.refs_0_), channel_id=1, source_target_pairs={{0,2},{1,3},{4,0},{5,1},{8,4},{9,5},{12,8},{13,9},{14,12},{15,13},... | collective-permute-start | bytes 479240 | tf_op jit(solution)/shard_map/ppermute | solution.py:928
  58.8 0.9 %collective-permute-start.5 = (bf16[24,3328]{1,0:T(8,128)(2,1)S(1)}, bf16[24,3328]{1,0:T(8,128)(2,1)S(1)}, u32[]{:S(2)}, u32[]{:S(2)}) collective-permute-start(bf16[24,3328]{1,0:T(8,128)(2,1)S(1)} %make_shard.1.refs_0_), channel_id=1, source_target_pairs={{0,1},{1,0},{2,3},{3,2},{4,5},{5,4},{6,7},{7,6},{8,9},{9,8},{10,11... | collective-permute-start | bytes 479240 | tf_op jit(solution)/shard_map/ppermute | solution.py:921
  59.7 3.0 %adjoint_step.1 = bf16[128,768]{1,0:T(8,128)(2,1)} custom-call(bf16[48,768]{1,0:T(8,128)(2,1)S(1)} %get-tuple-element.51.g_ref, bf16[8,96,512]{2,1,0:T(8,128)(2,1)} %get-tuple-element.52.w_hbm, bf16[128,48]{1,0:T(8,128)(2,1)} %constant.18.clone.i_hbm), custom_call_target="tpu_custom_call" | custom-call | flops 301989888 | bytes 1572864 | tf_op jit(solution)/shard_map/adjoint_step/pallas_call | solution.py:486
  62.7 0.0 collective-permute-done.1.refs_2_
  62.7 0.0 collective-permute-done.2.refs_4_
  62.7 1.2 %collective-permute-start.6 = (bf16[24,3328]{1,0:T(8,128)(2,1)S(1)}, bf16[24,3328]{1,0:T(8,128)(2,1)S(1)}, u32[]{:S(2)}, u32[]{:S(2)}) collective-permute-start(bf16[24,3328]{1,0:T(8,128)(2,1)S(1)} %collective-permute-done.1.refs_2_), channel_id=1, source_target_pairs={{0,1},{1,0},{2,3},{3,2},{4,5},{5,4},{6,7},{7,6},{8,9},{9,8},{10,11... | collective-permute-start | bytes 479240 | tf_op jit(solution)/shard_map/ppermute | solution.py:921
  63.9 0.0 collective-permute-start.7
  63.9 0.6 collective-permute-start.3
  64.5 0.9 collective-permute-start.4
  65.4 4.4 %all-to-all-start.3 = ((bf16[16,8,768]{2,1,0:T(8,128)(2,1)}), bf16[16,8,768]{2,1,0:T(8,128)(2,1)S(1)}, u32[]{:S(2)}, u32[]{:S(2)}) async-start(bf16[16,8,768]{2,1,0:T(8,128)(2,1)} %bitcast.17), calls=%async_computation.3 | async-start | bytes 393216 | tf_op jit(solution)/shard_map/all_to_all | solution.py:901
  69.7 0.0 collective-permute-done.5.refs_1_
  69.8 0.0 collective-permute-done.6.refs_3_
  69.8 0.0 collective-permute-done.7.refs_5_
  69.8 0.6 early_sums.1.e_hbm
  70.4 0.0 collective-permute-done.3.refs_6_
  70.4 0.0 collective-permute-done.4.refs_8_
  70.4 1.5 %collective-permute-start.8 = (bf16[24,3328]{1,0:T(8,128)(2,1)S(1)}, bf16[24,3328]{1,0:T(8,128)(2,1)S(1)}, u32[]{:S(2)}, u32[]{:S(2)}) collective-permute-start(bf16[24,3328]{1,0:T(8,128)(2,1)S(1)} %collective-permute-done.3.refs_6_), channel_id=1, source_target_pairs={{0,4},{1,5},{4,8},{5,9},{8,12},{9,13},{12,14},{13,15},{14,10},{15,... | collective-permute-start | bytes 479240 | tf_op jit(solution)/shard_map/ppermute | solution.py:926
  71.9 0.1 collective-permute-start.13
  72.0 5.7 %collective-permute-done.8.refs_10_ = bf16[24,3328]{1,0:T(8,128)(2,1)S(1)} collective-permute-done((bf16[24,3328]{1,0:T(8,128)(2,1)S(1)}, bf16[24,3328]{1,0:T(8,128)(2,1)S(1)}, u32[]{:S(2)}, u32[]{:S(2)}) %collective-permute-start.8) | collective-permute-done | bytes 159776 | tf_op jit(solution)/shard_map/ppermute | solution.py:926
  77.7 1.6 %collective-permute-start.9 = (bf16[24,3328]{1,0:T(8,128)(2,1)S(1)}, bf16[24,3328]{1,0:T(8,128)(2,1)S(1)}, u32[]{:S(2)}, u32[]{:S(2)}) collective-permute-start(bf16[24,3328]{1,0:T(8,128)(2,1)S(1)} %collective-permute-done.8.refs_10_), channel_id=1, source_target_pairs={{0,4},{1,5},{4,8},{5,9},{8,12},{9,13},{12,14},{13,15},{14,10},{15,... | collective-permute-start | bytes 479240 | tf_op jit(solution)/shard_map/ppermute | solution.py:926
  79.2 1.0 %collective-permute-start.10 = (bf16[24,3328]{1,0:T(8,128)(2,1)S(1)}, bf16[24,3328]{1,0:T(8,128)(2,1)S(1)}, u32[]{:S(2)}, u32[]{:S(2)}) collective-permute-start(bf16[24,3328]{1,0:T(8,128)(2,1)S(1)} %collective-permute-done.3.refs_6_), channel_id=1, source_target_pairs={{0,1},{1,0},{2,3},{3,2},{4,5},{5,4},{6,7},{7,6},{8,9},{9,8},{10,11... | collective-permute-start | bytes 479240 | tf_op jit(solution)/shard_map/ppermute | solution.py:921
  80.2 0.0 collective-permute-start.11
  80.2 0.5 collective-permute-start.12
  80.7 0.0 collective-permute-done.13.refs_12_
  80.7 0.0 collective-permute-start.14
  80.7 0.0 all-to-all-done.3
  80.7 3.8 %back_to_field.1 = bf16[4,512,512]{2,1,0:T(8,128)(2,1)} custom-call(bf16[4,512,512]{2,1,0:T(8,128)(2,1)} %get-tuple-element.43.d_hbm, bf16[128,768]{1,0:T(8,128)(2,1)S(1)} %bitcast.11, bf16[512,48]{1,0:T(8,128)(2,1)} %constant.21.clone.tt_hbm, bf16[256,256]{1,0:T(8,128)(2,1)} %get-tuple-element.59.w_hbm), custom_call_target="tpu_custom_call" | custom-call | flops 524288000 | bytes 4194304 | tf_op jit(solution)/shard_map/back_to_field/pallas_call | solution.py:880
  84.5 0.0 collective-permute-done.9.refs_14_
  84.5 0.6 collective-permute-start.15
  85.2 0.0 collective-permute-done.10.refs_7_
  85.2 0.0 collective-permute-done.11.refs_9_
  85.2 0.0 collective-permute-done.12.refs_11_
  85.2 0.0 collective-permute-done.14.refs_13_
  85.2 1.0 %collective-permute-done.15.refs_15_ = bf16[24,3328]{1,0:T(8,128)(2,1)S(1)} collective-permute-done((bf16[24,3328]{1,0:T(8,128)(2,1)S(1)}, bf16[24,3328]{1,0:T(8,128)(2,1)S(1)}, u32[]{:S(2)}, u32[]{:S(2)}) %collective-permute-start.15) | collective-permute-done | bytes 159776 | tf_op jit(solution)/shard_map/ppermute | solution.py:921
  86.2 3.4 %assemble.1 = (bf16[24,24,2048]{2,1,0:T(8,128)(2,1)}, f32[32,32]{1,0:T(8,128)}, f32[1,32]{1,0:T(1,128)}) custom-call(s32[1]{0:T(128)} %bitcast.2.me_ref, f32[6,16,128]{2,1,0:T(8,128)} %early_sums.1.e_hbm, bf16[24,3328]{1,0:T(8,128)(2,1)S(1)} %make_shard.1.refs_0_, bf16[24,3328]{1,0:T(8,128)(2,1)S(1)} %collective-permute-done.5.refs_1_, ...), custom_call_target="tpu_custom_call" | custom-call | flops 1000000 | bytes 8388608 | tf_op jit(solution)/shard_map/assemble/pallas_call | solution.py:831
  (1 shorter events, 0.0 us)
Async XLA Ops:
  0.6 10.2 %copy-start.1 = (f32[32]{0:T(128)S(1)}, f32[32]{0:T(128)}, u32[]{:S(2)}) copy-start(f32[32]{0:T(128)} %param.14) | copy-start | bytes 388
  0.6 10.2 %copy-start = (bf16[32,32]{1,0:T(8,128)(2,1)S(1)}, bf16[32,32]{1,0:T(8,128)(2,1)}, u32[]{:S(2)}) copy-start(bf16[32,32]{1,0:T(8,128)(2,1)} %l_ref.1) | copy-start | bytes 6148
  3.4 15.7 %all-to-all-start = ((bf16[16,8,768]{2,1,0:T(8,128)(2,1)}), bf16[16,8,768]{2,1,0:T(8,128)(2,1)S(1)}, u32[]{:S(2)}, u32[]{:S(2)}) async-start(bf16[16,8,768]{2,1,0:T(8,128)(2,1)} %bitcast.16), calls=%async_computation | async-start | bytes 393216 | tf_op jit(solution)/shard_map/all_to_all | solution.py:901
  40.6 12.5 %all-to-all-start.2 = ((bf16[16,8,768]{2,1,0:T(8,128)(2,1)}), bf16[16,8,768]{2,1,0:T(8,128)(2,1)S(1)}, u32[]{:S(2)}, u32[]{:S(2)}) async-start(bf16[16,8,768]{2,1,0:T(8,128)(2,1)} %bitcast.18), calls=%async_computation.2 | async-start | bytes 393216 | tf_op jit(solution)/shard_map/all_to_all | solution.py:901
  54.9 2.3 %collective-permute-start = (f32[24,2048]{1,0:T(8,128)S(1)}, f32[24,2048]{1,0:T(8,128)S(1)}, u32[]{:S(2)}, u32[]{:S(2)}) collective-permute-start(f32[24,2048]{1,0:T(8,128)S(1)} %get-tuple-element.46.s_ref), channel_id=1, source_target_pairs={{0,1},{1,0},{2,3},{3,2},{4,5},{5,4},{6,7},{7,6},{8,9},{9,8},{10,11... | collective-permute-start | bytes 589832 | tf_op jit(solution)/shard_map/ppermute | solution.py:980
  57.3 5.4 %collective-permute-start.1 = (bf16[24,3328]{1,0:T(8,128)(2,1)S(1)}, bf16[24,3328]{1,0:T(8,128)(2,1)S(1)}, u32[]{:S(2)}, u32[]{:S(2)}) collective-permute-start(bf16[24,3328]{1,0:T(8,128)(2,1)S(1)} %make_shard.1.refs_0_), channel_id=1, source_target_pairs={{0,4},{1,5},{4,8},{5,9},{8,12},{9,13},{12,14},{13,15},{14,10},{15,... | collective-permute-start | bytes 479240 | tf_op jit(solution)/shard_map/ppermute | solution.py:926
  57.3 5.4 %collective-permute-start.2 = (bf16[24,3328]{1,0:T(8,128)(2,1)S(1)}, bf16[24,3328]{1,0:T(8,128)(2,1)S(1)}, u32[]{:S(2)}, u32[]{:S(2)}) collective-permute-start(bf16[24,3328]{1,0:T(8,128)(2,1)S(1)} %make_shard.1.refs_0_), channel_id=1, source_target_pairs={{0,2},{1,3},{4,0},{5,1},{8,4},{9,5},{12,8},{13,9},{14,12},{15,13},... | collective-permute-start | bytes 479240 | tf_op jit(solution)/shard_map/ppermute | solution.py:928
  58.8 11.0 %collective-permute-start.5 = (bf16[24,3328]{1,0:T(8,128)(2,1)S(1)}, bf16[24,3328]{1,0:T(8,128)(2,1)S(1)}, u32[]{:S(2)}, u32[]{:S(2)}) collective-permute-start(bf16[24,3328]{1,0:T(8,128)(2,1)S(1)} %make_shard.1.refs_0_), channel_id=1, source_target_pairs={{0,1},{1,0},{2,3},{3,2},{4,5},{5,4},{6,7},{7,6},{8,9},{9,8},{10,11... | collective-permute-start | bytes 479240 | tf_op jit(solution)/shard_map/ppermute | solution.py:921
  62.7 7.1 %collective-permute-start.6 = (bf16[24,3328]{1,0:T(8,128)(2,1)S(1)}, bf16[24,3328]{1,0:T(8,128)(2,1)S(1)}, u32[]{:S(2)}, u32[]{:S(2)}) collective-permute-start(bf16[24,3328]{1,0:T(8,128)(2,1)S(1)} %collective-permute-done.1.refs_2_), channel_id=1, source_target_pairs={{0,1},{1,0},{2,3},{3,2},{4,5},{5,4},{6,7},{7,6},{8,9},{9,8},{10,11... | collective-permute-start | bytes 479240 | tf_op jit(solution)/shard_map/ppermute | solution.py:921
  63.9 5.9 %collective-permute-start.7 = (bf16[24,3328]{1,0:T(8,128)(2,1)S(1)}, bf16[24,3328]{1,0:T(8,128)(2,1)S(1)}, u32[]{:S(2)}, u32[]{:S(2)}) collective-permute-start(bf16[24,3328]{1,0:T(8,128)(2,1)S(1)} %collective-permute-done.2.refs_4_), channel_id=1, source_target_pairs={{0,1},{1,0},{2,3},{3,2},{4,5},{5,4},{6,7},{7,6},{8,9},{9,8},{10,11... | collective-permute-start | bytes 479240 | tf_op jit(solution)/shard_map/ppermute | solution.py:921
  63.9 6.5 %collective-permute-start.3 = (bf16[24,3328]{1,0:T(8,128)(2,1)S(1)}, bf16[24,3328]{1,0:T(8,128)(2,1)S(1)}, u32[]{:S(2)}, u32[]{:S(2)}) collective-permute-start(bf16[24,3328]{1,0:T(8,128)(2,1)S(1)} %collective-permute-done.1.refs_2_), channel_id=1, source_target_pairs={{0,4},{1,5},{4,8},{5,9},{8,12},{9,13},{12,14},{13,15},{14,10},{15,... | collective-permute-start | bytes 479240 | tf_op jit(solution)/shard_map/ppermute | solution.py:926
  64.5 5.9 %collective-permute-start.4 = (bf16[24,3328]{1,0:T(8,128)(2,1)S(1)}, bf16[24,3328]{1,0:T(8,128)(2,1)S(1)}, u32[]{:S(2)}, u32[]{:S(2)}) collective-permute-start(bf16[24,3328]{1,0:T(8,128)(2,1)S(1)} %collective-permute-done.2.refs_4_), channel_id=1, source_target_pairs={{0,2},{1,3},{4,0},{5,1},{8,4},{9,5},{12,8},{13,9},{14,12},{15,13},... | collective-permute-start | bytes 479240 | tf_op jit(solution)/shard_map/ppermute | solution.py:928
  65.4 15.3 %all-to-all-start.3 = ((bf16[16,8,768]{2,1,0:T(8,128)(2,1)}), bf16[16,8,768]{2,1,0:T(8,128)(2,1)S(1)}, u32[]{:S(2)}, u32[]{:S(2)}) async-start(bf16[16,8,768]{2,1,0:T(8,128)(2,1)} %bitcast.17), calls=%async_computation.3 | async-start | bytes 393216 | tf_op jit(solution)/shard_map/all_to_all | solution.py:901
  70.4 7.2 %collective-permute-start.8 = (bf16[24,3328]{1,0:T(8,128)(2,1)S(1)}, bf16[24,3328]{1,0:T(8,128)(2,1)S(1)}, u32[]{:S(2)}, u32[]{:S(2)}) collective-permute-start(bf16[24,3328]{1,0:T(8,128)(2,1)S(1)} %collective-permute-done.3.refs_6_), channel_id=1, source_target_pairs={{0,4},{1,5},{4,8},{5,9},{8,12},{9,13},{12,14},{13,15},{14,10},{15,... | collective-permute-start | bytes 479240 | tf_op jit(solution)/shard_map/ppermute | solution.py:926
  71.9 8.8 %collective-permute-start.13 = (bf16[24,3328]{1,0:T(8,128)(2,1)S(1)}, bf16[24,3328]{1,0:T(8,128)(2,1)S(1)}, u32[]{:S(2)}, u32[]{:S(2)}) collective-permute-start(bf16[24,3328]{1,0:T(8,128)(2,1)S(1)} %collective-permute-done.4.refs_8_), channel_id=1, source_target_pairs={{0,2},{1,3},{4,0},{5,1},{8,4},{9,5},{12,8},{13,9},{14,12},{15,13},... | collective-permute-start | bytes 479240 | tf_op jit(solution)/shard_map/ppermute | solution.py:928
  77.7 6.9 %collective-permute-start.9 = (bf16[24,3328]{1,0:T(8,128)(2,1)S(1)}, bf16[24,3328]{1,0:T(8,128)(2,1)S(1)}, u32[]{:S(2)}, u32[]{:S(2)}) collective-permute-start(bf16[24,3328]{1,0:T(8,128)(2,1)S(1)} %collective-permute-done.8.refs_10_), channel_id=1, source_target_pairs={{0,4},{1,5},{4,8},{5,9},{8,12},{9,13},{12,14},{13,15},{14,10},{15,... | collective-permute-start | bytes 479240 | tf_op jit(solution)/shard_map/ppermute | solution.py:926
  79.2 6.0 %collective-permute-start.10 = (bf16[24,3328]{1,0:T(8,128)(2,1)S(1)}, bf16[24,3328]{1,0:T(8,128)(2,1)S(1)}, u32[]{:S(2)}, u32[]{:S(2)}) collective-permute-start(bf16[24,3328]{1,0:T(8,128)(2,1)S(1)} %collective-permute-done.3.refs_6_), channel_id=1, source_target_pairs={{0,1},{1,0},{2,3},{3,2},{4,5},{5,4},{6,7},{7,6},{8,9},{9,8},{10,11... | collective-permute-start | bytes 479240 | tf_op jit(solution)/shard_map/ppermute | solution.py:921
  80.2 5.0 %collective-permute-start.11 = (bf16[24,3328]{1,0:T(8,128)(2,1)S(1)}, bf16[24,3328]{1,0:T(8,128)(2,1)S(1)}, u32[]{:S(2)}, u32[]{:S(2)}) collective-permute-start(bf16[24,3328]{1,0:T(8,128)(2,1)S(1)} %collective-permute-done.4.refs_8_), channel_id=1, source_target_pairs={{0,1},{1,0},{2,3},{3,2},{4,5},{5,4},{6,7},{7,6},{8,9},{9,8},{10,11... | collective-permute-start | bytes 479240 | tf_op jit(solution)/shard_map/ppermute | solution.py:921
  80.2 5.0 %collective-permute-start.12 = (bf16[24,3328]{1,0:T(8,128)(2,1)S(1)}, bf16[24,3328]{1,0:T(8,128)(2,1)S(1)}, u32[]{:S(2)}, u32[]{:S(2)}) collective-permute-start(bf16[24,3328]{1,0:T(8,128)(2,1)S(1)} %collective-permute-done.8.refs_10_), channel_id=1, source_target_pairs={{0,1},{1,0},{2,3},{3,2},{4,5},{5,4},{6,7},{7,6},{8,9},{9,8},{10,11... | collective-permute-start | bytes 479240 | tf_op jit(solution)/shard_map/ppermute | solution.py:921
  80.7 4.5 %collective-permute-start.14 = (bf16[24,3328]{1,0:T(8,128)(2,1)S(1)}, bf16[24,3328]{1,0:T(8,128)(2,1)S(1)}, u32[]{:S(2)}, u32[]{:S(2)}) collective-permute-start(bf16[24,3328]{1,0:T(8,128)(2,1)S(1)} %collective-permute-done.13.refs_12_), channel_id=1, source_target_pairs={{0,1},{1,0},{2,3},{3,2},{4,5},{5,4},{6,7},{7,6},{8,9},{9,8},{10,11... | collective-permute-start | bytes 479240 | tf_op jit(solution)/shard_map/ppermute | solution.py:921
  84.5 1.7 %collective-permute-start.15 = (bf16[24,3328]{1,0:T(8,128)(2,1)S(1)}, bf16[24,3328]{1,0:T(8,128)(2,1)S(1)}, u32[]{:S(2)}, u32[]{:S(2)}) collective-permute-start(bf16[24,3328]{1,0:T(8,128)(2,1)S(1)} %collective-permute-done.9.refs_14_), channel_id=1, source_target_pairs={{0,1},{1,0},{2,3},{3,2},{4,5},{5,4},{6,7},{7,6},{8,9},{9,8},{10,11... | collective-permute-start | bytes 479240 | tf_op jit(solution)/shard_map/ppermute | solution.py:921

commit v4 on v3

--- a/solution.py
+++ b/solution.py
@@ -312,7 +312,7 @@
     )(*in_hbm(field, table))
 
 
-def prepare(me, weights, local_weight, bias, chips, half):
+def prepare(me, weights, local_weight, bias, tables, chips, half):
     modes_x, modes_y, full2 = weights.shape
     chans = local_weight.shape[0]
     tiles = full2 // LANES
@@ -320,10 +320,12 @@
     groups = full2 // 2 // LANES
     batch = 6
 
-    def kernel(
-        me_ref, w_hbm, l_ref, b_ref, plain_hbm, turned_hbm, block_hbm, block_t_hbm, bias_hbm,
-        w_ref, scr, pick, one, two, plain_ref, turned_ref, block_ref, block_t_ref, bias_ref, sem, out_sem,
-    ):
+    count = len(tables)
+
+    def kernel(me_ref, w_hbm, l_ref, b_ref, *refs):
+        tables_hbm, (plain_ref, turned_ref, block_ref, block_t_ref, bias_ref) = refs[:count], refs[count : count + 5]
+        tables_ref, (w_ref, scr, pick, one, two, sem, table_sem) = refs[count + 5 : 2 * count + 5], refs[2 * count + 5 :]
+        table_copies = start_all(list(zip(tables_hbm, tables_ref)), table_sem)
         cuts = [pl.ds(j, batch) for j in range(0, modes_x, batch)]
         copies = start_all([(w_hbm.at[cut], w_ref.at[cut]) for cut in cuts], sem)
 
@@ -341,9 +343,6 @@
         low = (value - high.astype(F32) - mid.astype(F32)).astype(BF16)
         wide = dot(high, spread) + dot(mid, spread) + dot(low, spread)
         bias_ref[...] = jnp.concatenate([wide, wide], axis=1)
-        out_copies = start_all(
-            [(block_ref, block_hbm), (block_t_ref, block_t_hbm), (bias_ref, bias_hbm)], out_sem
-        )
 
         for n, first in enumerate(range(0, modes_x, batch)):
             copies[n].wait()
@@ -364,44 +363,36 @@
         for g in range(groups):
             plain_ref[g] = dot(pick[g].astype(BF16), repeat).astype(BF16)
             one[g * LANES : (g + 1) * LANES, :] = jnp.transpose(jnp.concatenate([pick[g], pad]))
-        out_copies.append(pltpu.make_async_copy(plain_ref, plain_hbm, out_sem.at[3]))
-        out_copies[-1].start()
         for b in range(chans):
             two[b * chans : (b + 1) * chans, :] = one[pl.ds(b, chans, stride=chans), :]
         for g in range(groups):
             part = jnp.transpose(two[g * LANES : (g + 1) * LANES, :])[0:rows]
             turned_ref[g] = dot(part.astype(BF16), repeat).astype(BF16)
-        out_copies.append(pltpu.make_async_copy(turned_ref, turned_hbm, out_sem.at[4]))
-        out_copies[-1].start()
-        for copy in out_copies:
+        for copy in table_copies:
             copy.wait()
 
     shape = (groups, rows, LANES * LANES // chans)
-    wide = pltpu.HBM(shape, BF16)
-    block = pltpu.HBM((half, half), BF16)
-    return pl.pallas_call(
-        kernel,
-        in_specs=[smem(), hbm(), vmem(), vmem()],
-        out_specs=(hbm(),) * 5,
-        out_shape=(wide, wide, block, block, pltpu.HBM((8, 2 * half), F32)),
+    wide = jax.ShapeDtypeStruct(shape, BF16)
+    block = jax.ShapeDtypeStruct((half, half), BF16)
+    held = tuple(jax.ShapeDtypeStruct(t.shape, t.dtype) for t in tables)
+    return pl.pallas_call(
+        kernel,
+        in_specs=[smem(), hbm(), vmem(), vmem()] + [hbm()] * count,
+        out_specs=(vmem(),) * (5 + count),
+        out_shape=(wide, wide, block, block, jax.ShapeDtypeStruct((8, 2 * half), F32)) + held,
         scratch_shapes=[
             pltpu.VMEM(weights.shape, BF16),
             pltpu.VMEM((tiles, modes_x * modes_y, LANES), F32),
             pltpu.VMEM((groups, rows, LANES), F32),
             pltpu.VMEM((full2 // 2, LANES), F32),
             pltpu.VMEM((full2 // 2, LANES), F32),
-            pltpu.VMEM(shape, BF16),
-            pltpu.VMEM(shape, BF16),
-            pltpu.VMEM((half, half), BF16),
-            pltpu.VMEM((half, half), BF16),
-            pltpu.VMEM((8, 2 * half), F32),
             pltpu.SemaphoreType.DMA((modes_x // batch,)),
-            pltpu.SemaphoreType.DMA((5,)),
+            pltpu.SemaphoreType.DMA((count,)),
         ],
         compiler_params=params(),
         cost_estimate=cost(1000000, 4 * 1024 * 1024),
         name="prepare",
-    )(me, *in_hbm(weights), local_weight, bias)
+    )(me, *in_hbm(weights), local_weight, bias, *in_hbm(*tables))
 
 
 def weigh(spec, w_ref, chans, modes_x, adjoint):
@@ -432,51 +423,40 @@
     return jnp.concatenate([jnp.concatenate(real, axis=1), jnp.concatenate(imag, axis=1)], axis=0).astype(BF16)
 
 
-def mode_step(pencil, spread_w, forward, inverse, chans):
+def mode_step(pencil, spread_w, forward, inverse, field, cotangent, chans):
     modes_x = forward.shape[0] // 2
 
-    def kernel(p_ref, w_hbm, f_hbm, i_hbm, spec_ref, out_hbm, w_ref, f_ref, i_ref, out_ref, sem, out_sem):
-        copies = start_all([(f_hbm, f_ref), (w_hbm, w_ref), (i_hbm, i_ref)], sem)
-        copies[0].wait()
+    def kernel(p_ref, w_ref, f_ref, i_ref, u_hbm, c_hbm, spec_ref, out_ref, u_ref, c_ref, sem):
+        copies = start_all([(u_hbm.at[0], u_ref), (c_hbm.at[0], c_ref)], sem)
         spec = dot(f_ref[...], p_ref[...]).astype(BF16)
         spec_ref[...] = spec
-        copies[1].wait()
-        copies[2].wait()
         mixed = weigh(spec, w_ref, chans, modes_x, False)
         out_ref[...] = dot(i_ref[...], mixed).astype(BF16)
-        copy = pltpu.make_async_copy(out_ref, out_hbm, out_sem)
-        copy.start()
-        copy.wait()
-
-    return pl.pallas_call(
-        kernel,
-        in_specs=[vmem()] + [hbm()] * 3,
-        out_specs=(vmem(), hbm()),
+        for copy in copies:
+            copy.wait()
+
+    return pl.pallas_call(
+        kernel,
+        in_specs=[vmem()] * 4 + [hbm()] * 2,
+        out_specs=(vmem(),) * 4,
         out_shape=(
             jax.ShapeDtypeStruct((2 * modes_x, pencil.shape[1]), BF16),
-            pltpu.HBM(pencil.shape, BF16),
+            jax.ShapeDtypeStruct(pencil.shape, BF16),
+            jax.ShapeDtypeStruct(field.shape[1:], BF16),
+            jax.ShapeDtypeStruct(field.shape[1:], BF16),
         ),
-        scratch_shapes=[
-            pltpu.VMEM(spread_w.shape, BF16),
-            pltpu.VMEM(forward.shape, BF16),
-            pltpu.VMEM(inverse.shape, BF16),
-            pltpu.VMEM(pencil.shape, BF16),
-            pltpu.SemaphoreType.DMA((3,)),
-            pltpu.SemaphoreType.DMA,
-        ],
+        scratch_shapes=[pltpu.SemaphoreType.DMA((2,))],
         compiler_params=params(),
         cost_estimate=cost(2 * 48 * 6 * 128 * 4096, spread_w.size * 4),
         name="mode_step",
-    )(pencil, *in_hbm(spread_w, forward, inverse))
+    )(pencil, spread_w, forward, inverse, *in_hbm(field, cotangent))
 
 
 def adjoint_step(grads, spread_w, inverse, chans):
     modes_x = grads.shape[0] // 2
     shape = (inverse.shape[0], grads.shape[1])
 
-    def kernel(g_ref, w_hbm, i_hbm, out_hbm, w_ref, i_ref, out_ref, sem, out_sem):
-        for copy in start_all([(w_hbm, w_ref), (i_hbm, i_ref)], sem):
-            copy.wait()
+    def kernel(g_ref, w_ref, i_ref, out_hbm, out_ref, out_sem):
         mixed = weigh(g_ref[...], w_ref, chans, modes_x, True)
         out_ref[...] = dot(i_ref[...], mixed).astype(BF16)
         copy = pltpu.make_async_copy(out_ref, out_hbm, out_sem)
@@ -485,38 +465,30 @@
 
     return pl.pallas_call(
         kernel,
-        in_specs=[vmem(), hbm(), hbm()],
+        in_specs=[vmem()] * 3,
         out_specs=hbm(),
         out_shape=pltpu.HBM(shape, BF16),
-        scratch_shapes=[
-            pltpu.VMEM(spread_w.shape, BF16),
-            pltpu.VMEM(inverse.shape, BF16),
-            pltpu.VMEM(shape, BF16),
-            pltpu.SemaphoreType.DMA((2,)),
-            pltpu.SemaphoreType.DMA,
-        ],
+        scratch_shapes=[pltpu.VMEM(shape, BF16), pltpu.SemaphoreType.DMA],
         compiler_params=params(),
         cost_estimate=cost(2 * 48 * 6 * 128 * 4096, spread_w.size * 4),
         name="adjoint_step",
-    )(grads, *in_hbm(spread_w, inverse))
-
-
-def pointwise(field, cotangent, pencil, table_t, table, block_weight, bias_row, chips, half):
+    )(grads, spread_w, inverse)
+
+
+def pointwise(field, cotangent, first_rows, pencil, table_t, table, block_weight, bias_row, chips, half):
     rows, length, width = field.shape
     chunk, sub = 128, 16
     modes = table.shape[0]
     depth = table_t.shape[1]
 
     def kernel(
-        u_hbm, c_hbm, p_ref, tt_hbm, t_hbm, w_hbm, b_hbm, out_hbm, dpre_hbm, send_hbm,
-        u_ref, c_ref, tt_ref, t_ref, w_ref, b_ref, out_ref, dpre_ref, send_ref, bscr, dscr, sem, out_sem,
+        u_hbm, c_hbm, u_first, c_first, p_ref, tt_ref, t_ref, w_ref, b_ref, out_hbm, dpre_hbm, send_hbm,
+        u_rest, c_rest, out_ref, dpre_ref, send_ref, bscr, dscr, sem, out_sem,
     ):
-        copies = start_all([(tt_hbm, tt_ref), (w_hbm, w_ref), (b_hbm, b_ref), (t_hbm, t_ref)], sem)
-        for x in range(rows):
-            pltpu.make_async_copy(u_hbm.at[x], u_ref.at[x], sem.at[4 + x]).start()
-            pltpu.make_async_copy(c_hbm.at[x], c_ref.at[x], sem.at[4 + rows + x]).start()
-        for copy in copies:
-            copy.wait()
+        copies = []
+        for x in range(1, rows):
+            pairs = [(u_hbm.at[x], u_rest.at[x - 1]), (c_hbm.at[x], c_rest.at[x - 1])]
+            copies.append(start_all(pairs, sem.at[x - 1]))
         cut_lanes(bscr, p_ref)
         root = math.sqrt(2.0 / math.pi)
         bias = b_ref[0:1, :]
@@ -529,15 +501,18 @@
         weight = (0.5 * w_ref[...].astype(F32)).astype(BF16)
 
         def one_row(x):
-            pltpu.make_async_copy(u_hbm.at[x], u_ref.at[x], sem.at[4 + x]).wait()
-            pltpu.make_async_copy(c_hbm.at[x], c_ref.at[x], sem.at[4 + rows + x]).wait()
+            if x > 0:
+                for copy in copies[x - 1]:
+                    copy.wait()
+            u_ref = u_rest.at[x - 1] if x > 0 else u_first
+            c_ref = c_rest.at[x - 1] if x > 0 else c_first
             coeff = (0.5 * gather_rows(bscr, x, chips, half).astype(F32)).astype(BF16)
             coeff = jnp.concatenate([coeff, bias], axis=0)
             for k in range(length // chunk):
                 where = pl.ds(k * chunk, chunk)
                 for h in range(2):
                     lanes = slice(h * half, (h + 1) * half)
-                    left = jnp.concatenate([u_ref[x, where, lanes], tt_ref[where, :]], axis=1)
+                    left = jnp.concatenate([u_ref[where, lanes], tt_ref[where, :]], axis=1)
                     right = jnp.concatenate([weight, coeff[:, lanes]], axis=0)
                     halved = dot(left, right)
                     for at in range(0, chunk, sub):
@@ -549,7 +524,7 @@
                         out_ref[x, place, lanes] = (p * twice).astype(BF16)
                         slope = 1.5 * inner - (2.0 * root) * p
                         grad = twice * (0.5 + (1.0 - th) * slope)
-                        dpre_ref[x, place, lanes] = (c_ref[x, place, lanes].astype(F32) * grad).astype(BF16)
+                        dpre_ref[x, place, lanes] = (c_ref[place, lanes].astype(F32) * grad).astype(BF16)
             pltpu.make_async_copy(out_ref.at[x], out_hbm.at[x], out_sem.at[x]).start()
             pltpu.make_async_copy(dpre_ref.at[x], dpre_hbm.at[x], out_sem.at[rows + x]).start()
             scatter_rows(dscr, dot(t_ref[...], dpre_ref[x]), x, chips, half)
@@ -565,7 +540,7 @@
 
     return pl.pallas_call(
         kernel,
-        in_specs=[hbm(), hbm(), vmem()] + [hbm()] * 4,
+        in_specs=[hbm(), hbm()] + [vmem()] * 7,
         out_specs=(hbm(), hbm(), hbm()),
         out_shape=(
             pltpu.HBM(field.shape, BF16),
@@ -573,24 +548,20 @@
             pltpu.HBM(pencil.shape, BF16),
         ),
         scratch_shapes=[
-            pltpu.VMEM(field.shape, BF16),
-            pltpu.VMEM(field.shape, BF16),
-            pltpu.VMEM(table_t.shape, BF16),
-            pltpu.VMEM(table.shape, BF16),
-            pltpu.VMEM(block_weight.shape, BF16),
-            pltpu.VMEM(bias_row.shape, F32),
+            pltpu.VMEM((rows - 1, length, width), BF16),
+            pltpu.VMEM((rows - 1, length, width), BF16),
             pltpu.VMEM(field.shape, BF16),
             pltpu.VMEM(field.shape, BF16),
             pltpu.VMEM(pencil.shape, BF16),
             pltpu.VMEM(cut_shape(pencil.shape), F32),
             pltpu.VMEM(cut_shape(pencil.shape), F32),
-            pltpu.SemaphoreType.DMA((4 + 2 * rows,)),
+            pltpu.SemaphoreType.DMA((rows - 1, 2)),
             pltpu.SemaphoreType.DMA((2 * rows + 1,)),
         ],
         compiler_params=params(),
         cost_estimate=cost(field.size * 1000, field.size * 8),
         name="pointwise",
-    )(*in_hbm(field, cotangent), pencil, *in_hbm(table_t, table, block_weight, bias_row))
+    )(*in_hbm(field, cotangent), *first_rows, pencil, table_t, table, block_weight, bias_row)
 
 
 def local_sums(field, dpre, chans, half):
@@ -661,14 +632,11 @@
     full = chans * chans
     parts = full // step
 
-    def kernel(u_ref, p_ref, f_hbm, d_ref, own_ref, shared_ref, f_ref, sem):
-        copy = start_all([(f_hbm, f_ref)], sem)[0]
-
+    def kernel(u_ref, p_ref, f_ref, d_ref, own_ref, shared_ref):
         def stack(ref):
             return jnp.concatenate([ref[:, k * LANES : (k + 1) * LANES] for k in range(tiles)], axis=0)
 
         left = stack(u_ref)
-        copy.wait()
         d_ref[...] = dot(f_ref[...], p_ref[...]).astype(BF16)
         repeat = jnp.concatenate(
             [lane_equals(LANES, LANES, lambda l: l % chans, chans * g) for g in range(groups)], axis=1
@@ -698,17 +666,16 @@
 
     return pl.pallas_call(
         kernel,
-        in_specs=[vmem(), vmem(), hbm()],
+        in_specs=[vmem()] * 3,
         out_shape=(
             jax.ShapeDtypeStruct(spectrum.shape, BF16),
             jax.ShapeDtypeStruct((modes_x, 2 * full), BF16),
             jax.ShapeDtypeStruct((modes_x, 2 * full), F32),
         ),
-        scratch_shapes=[pltpu.VMEM(forward.shape, BF16), pltpu.SemaphoreType.DMA((1,))],
         compiler_params=params(),
         cost_estimate=cost(2 * 288 * 128 * 4096, 4 * 1024 * 1024),
         name="weight_sums",
-    )(spectrum, pencil, *in_hbm(forward))
+    )(spectrum, pencil, forward)
 
 
 def make_shard(me, own, shared, other, stats):
@@ -777,36 +744,74 @@
     )(*shards_all)
 
 
-def assemble(me, early, shards_all, turns, modes_y, chans, chips):
+def shard_places(me, turns, chips):
+    spot = ring_spot(me // 2, chips)
+    core = me % 2
+    return [
+        (ring_chip((spot + chips - back) % chips, chips), 1 - core if swapped else core) for back, swapped in turns
+    ]
+
+
+def place_tile(scr, refs, places, turns, k, modes_y, tiles):
+    rows = scr.shape[1] // modes_y
+    part = tiles // 4
+    chips = modes_y // 3
+    keeper = k % (2 * part) // part
+    at = tiles + k // (2 * part) * part + k % part
+    for n, (chip, core) in enumerate(places):
+        own = pl.ds(chip + 2 * chips * core, rows, stride=modes_y)
+        scr[k, own, :] = refs[n][:, k * LANES : (k + 1) * LANES].astype(F32)
+        if turns[n][1]:
+            continue
+        mate = turns.index((turns[n][0], True))
+        lanes = slice(at * LANES, (at + 1) * LANES)
+        shared = pl.ds(chip + chips, rows, stride=modes_y)
+        scr[k, shared, :] = jnp.where(core == keeper, refs[n][:, lanes], refs[mate][:, lanes]).astype(F32)
+
+
+def assemble_first(me, shards_all, known, turns, modes_y, chans, chips):
+    rows = shards_all[0].shape[0]
+    count = len(shards_all)
+    tiles = 2 * chans * chans // LANES
+
+    def kernel(me_ref, *refs):
+        places = shard_places(me_ref[0], turns, chips)
+        for k in range(tiles):
+            place_tile(refs[count], refs[:count], places, turns, k, modes_y, tiles)
+        for n in range(known, count):
+            refs[count + 1][n - known] = read_sums(refs[n], chans * chans)
+
+    return pl.pallas_call(
+        kernel,
+        in_specs=[smem()] + [vmem()] * count,
+        out_specs=(vmem(), vmem()),
+        out_shape=(
+            jax.ShapeDtypeStruct((tiles, rows * modes_y, LANES), F32),
+            jax.ShapeDtypeStruct((count - known, 16, LANES), F32),
+        ),
+        compiler_params=params(),
+        cost_estimate=cost(1000000, 4 * 1024 * 1024),
+        name="assemble_first",
+    )(me, *shards_all)
+
+
+def assemble(me, scr, early, more, shards_all, turns, modes_y, chans, chips):
     rows = shards_all[0].shape[0]
     full = chans * chans
     tiles = 2 * full // LANES
-    part = full // 2 // LANES
     count = len(shards_all)
-
-    def kernel(me_ref, e_hbm, *refs):
-        ins, (g_ref, l_ref, b_ref, scr, stat, out, e_ref, sem) = refs[:count], refs[count:]
+    total_count = len(turns)
+    before = total_count - count
+    known = early.shape[0]
+
+    def kernel(me_ref, scr_in, e_hbm, m_ref, *refs):
+        ins, (scr, g_ref, l_ref, b_ref, stat, out, e_ref, sem) = refs[:count], refs[count:]
         fetch = pltpu.make_async_copy(e_hbm, e_ref, sem.at[tiles // 4])
         fetch.start()
-        spot = ring_spot(me_ref[0] // 2, chips)
-        places = []
-        for back, swapped in turns:
-            chip = ring_chip((spot + chips - back) % chips, chips)
-            core = me_ref[0] % 2
-            places.append((chip, 1 - core if swapped else core))
+        places = shard_places(me_ref[0], turns, chips)
         copies = []
         for k in range(tiles):
-            keeper = k % (2 * part) // part
-            at = tiles + k // (2 * part) * part + k % part
-            for n, (chip, core) in enumerate(places):
-                own = pl.ds(chip + 2 * chips * core, rows, stride=modes_y)
-                scr[k, own, :] = ins[n][:, k * LANES : (k + 1) * LANES].astype(F32)
-                if turns[n][1]:
-                    continue
-                mate = turns.index((turns[n][0], True))
-                lanes = slice(at * LANES, (at + 1) * LANES)
-                shared = pl.ds(chip + chips, rows, stride=modes_y)
-                scr[k, shared, :] = jnp.where(core == keeper, ins[n][:, lanes], ins[mate][:, lanes]).astype(F32)
+            place_tile(scr, ins, places[before:], turns[before:], k, modes_y, tiles)
             lanes = slice(k * LANES, (k + 1) * LANES)
             for j in range(rows):
                 out[j, :, lanes] = scr[k, j * modes_y : (j + 1) * modes_y, :].astype(BF16)
@@ -816,9 +821,14 @@
                 copies[-1].start()
         fetch.wait()
         for n, (chip, core) in enumerate(places):
-            stat[2 * chip + core] = e_ref[n] if n < early.shape[0] else read_sums(ins[n], full)
+            if n < known:
+                stat[2 * chip + core] = e_ref[n]
+            elif n < before:
+                stat[2 * chip + core] = m_ref[n - known]
+            else:
+                stat[2 * chip + core] = read_sums(ins[n - before], full)
         total = stat[0]
-        for n in range(1, count):
+        for n in range(1, total_count):
             total = total + stat[n]
         for k in range(chans // 8):
             piece = total[0:8] if k == 0 else pltpu.roll(total[0:8], LANES - k * chans, 1)
@@ -830,16 +840,17 @@
     shape = (rows, modes_y, 2 * full)
     return pl.pallas_call(
         kernel,
-        in_specs=[smem(), hbm()] + [vmem()] * count,
-        out_specs=(hbm(), vmem(), vmem()),
+        in_specs=[smem(), vmem(), hbm(), vmem()] + [vmem()] * count,
+        out_specs=(vmem(), hbm(), vmem(), vmem()),
         out_shape=(
+            jax.ShapeDtypeStruct(scr.shape, F32),
             pltpu.HBM(shape, BF16),
             jax.ShapeDtypeStruct((chans, chans), F32),
             jax.ShapeDtypeStruct((1, chans), F32),
         ),
+        input_output_aliases={1: 0},
         scratch_shapes=[
-            pltpu.VMEM((tiles, rows * modes_y, LANES), F32),
-            pltpu.VMEM((count, 16, LANES), F32),
+            pltpu.VMEM((total_count, 16, LANES), F32),
             pltpu.VMEM(shape, BF16),
             pltpu.VMEM(early.shape, F32),
             pltpu.SemaphoreType.DMA((tiles // 4 + 1,)),
@@ -847,23 +858,19 @@
         compiler_params=params(),
         cost_estimate=cost(1000000, 8 * 1024 * 1024),
         name="assemble",
-    )(me, *in_hbm(early), *shards_all)
+    )(me, scr, *in_hbm(early), more, *shards_all)[1:]
 
 
 def back_to_field(dpre, pencil, table_t, block_weight, chips, half):
     rows, length, width = dpre.shape
     chunk = 128
 
-    def kernel(d_hbm, p_ref, tt_hbm, w_hbm, out_hbm, d_ref, tt_ref, w_ref, out_ref, bscr, sem, out_sem):
-        copies = start_all(
-            [(tt_hbm, tt_ref), (w_hbm, w_ref)] + [(d_hbm.at[x], d_ref.at[x]) for x in range(rows)], sem
-        )
-        for copy in copies[0:2]:
-            copy.wait()
+    def kernel(d_hbm, p_ref, tt_ref, w_ref, out_hbm, d_ref, out_ref, bscr, sem, out_sem):
+        copies = start_all([(d_hbm.at[x], d_ref.at[x]) for x in range(rows)], sem)
         cut_lanes(bscr, p_ref)
         out_copies = []
         for x in range(rows):
-            copies[2 + x].wait()
+            copies[x].wait()
             coeff = gather_rows(bscr, x, chips, half)
             for k in range(length // chunk):
                 where = pl.ds(k * chunk, chunk)
@@ -879,22 +886,20 @@
 
     return pl.pallas_call(
         kernel,
-        in_specs=[hbm(), vmem(), hbm(), hbm()],
+        in_specs=[hbm()] + [vmem()] * 3,
         out_specs=hbm(),
         out_shape=pltpu.HBM(dpre.shape, BF16),
         scratch_shapes=[
             pltpu.VMEM(dpre.shape, BF16),
-            pltpu.VMEM(table_t.shape, BF16),
-            pltpu.VMEM(block_weight.shape, BF16),
             pltpu.VMEM(dpre.shape, BF16),
             pltpu.VMEM(cut_shape(pencil.shape), F32),
-            pltpu.SemaphoreType.DMA((2 + rows,)),
+            pltpu.SemaphoreType.DMA((rows,)),
             pltpu.SemaphoreType.DMA((rows,)),
         ],
         compiler_params=params(),
         cost_estimate=cost(dpre.size * 500, dpre.size * 4),
         name="back_to_field",
-    )(*in_hbm(dpre), pencil, *in_hbm(table_t, block_weight))
+    )(*in_hbm(dpre), pencil, table_t, block_weight)
 
 
 def exchange(pencil):
@@ -965,13 +970,15 @@
 
     send = rows_to_modes(field, table_y, chips, half)
     pencil = exchange(send)
-    plain, turned, block, block_t, bias_row = prepare(
-        me_id, spectral_weight, local_weight, bias[None, :], chips, half
-    )
-    spectrum, send = mode_step(pencil, plain, forward, inverse, chans)
+    tables = [jnp.asarray(t) for t in (forward, inverse, table_yw_t, table_yw, table_y_t)]
+    plain, turned, block, block_t, bias_row, *tables = prepare(
+        me_id, spectral_weight, local_weight, bias[None, :], tables, chips, half
+    )
+    forward, inverse, table_yw_t, table_yw, table_y_t = tables
+    spectrum, send, *first_rows = mode_step(pencil, plain, forward, inverse, field, cotangent, chans)
     pencil = exchange(send)
     output_field, dpre, send = pointwise(
-        field, cotangent, pencil, table_yw_t, table_yw, block, bias_row, chips, half
+        field, cotangent, first_rows, pencil, table_yw_t, table_yw, block, bias_row, chips, half
     )
     pencil = exchange(send)
     stats = local_sums(field, dpre, chans, half)
@@ -986,21 +993,25 @@
     send = adjoint_step(grads, turned, inverse, chans)
     send = ring.tie(send)
     ring.settle()
-    early = list(ring.parts)
+    first = list(ring.parts)
     ring.hop()
     pencil = exchange(send)
     ring.settle()
-    sums = early_sums(early, chans)
+    early, turns = list(ring.parts), list(ring.turns)
+    sums = early_sums(first, chans)
     sums = ring.tie(sums)
     ring.hop()
     pencil, sums = lax.optimization_barrier((pencil, sums))
     ring.settle()
     ring.hop()
     field_grad = back_to_field(dpre, pencil, table_y_t, block_t, chips, half)
-    field_grad = ring.hold(field_grad)
+    early[0], field_grad = lax.optimization_barrier((early[0], field_grad))
+    scr, more = assemble_first(me_id, early, len(first), turns, modes_y, chans, chips)
+    scr = ring.hold(scr)
     ring.settle()
+    late = ring.parts[len(early) :]
     spectral_grad, local_grad, bias_grad = assemble(
-        me_id, sums, ring.parts, ring.turns, modes_y, chans, chips
+        me_id, scr, sums, more, late, ring.turns, modes_y, chans, chips
     )
     return output_field, field_grad, spectral_grad, local_grad, bias_grad.reshape(chans)
 

time: 90.8 us -> 85.7 us (0.944)
  Pallas kernels: 31.9 us -> 26.4 us
  waiting for transfers between devices: 17 us -> 18 us
    pallas_call x7 -> x8, Pallas kernels: 24.9 us -> 19.5 us  [the longest x1 5.48 us: pointwise(): pl.pallas_call(kernel, in_specs=[hbm(), hbm()] + [vmem()] * 7, out_specs=...]
  transfers between devices with their start and end apart: 19 -> 19, of which waited for: 5 -> 7; matrix products, arithmetic and copies ran while one was open for 0% -> 0% of each run, Pallas kernels for 16% -> 15%
where the time goes in v4:
time: 85.7 us; the launch traced here: 84.9 us
  starting transfers between devices  28.3 us (33%)
  Pallas kernels  26.4 us (31%)
  waiting for transfers between devices  18 us (21%)
  blocking collectives  11.2 us (13%)
  between operations  0.98 us (1%)
    all_to_all x3, starting transfers between devices, exchange(): return lax.all_to_all(pencil, 'xy', split_axis=0, concat_axis=0, tiled=True)  16.2 us
    all_to_all x1, blocking collectives, exchange(): return lax.all_to_all(pencil, 'xy', split_axis=0, concat_axis=0, tiled=True)  11.2 us
    all_to_all x3, waiting for transfers between devices, exchange(): return lax.all_to_all(pencil, 'xy', split_axis=0, concat_axis=0, tiled=True)  10.1 us
    ppermute x4, waiting for transfers between devices, hop(): self.ahead = lax.ppermute(self.ahead, 'xy', self.hops[1])  5.71 us
    pallas_call x1, Pallas kernels, pointwise(): pl.pallas_call(kernel, in_specs=[hbm(), hbm()] + [vmem()] * 7, out_specs=...  5.48 us
    ppermute x8, starting transfers between devices, keep(): self.parts.append(lax.ppermute(piece, 'xy', self.swap))  4.76 us
    pallas_call x1, Pallas kernels, back_to_field(): pl.pallas_call(kernel, in_specs=[hbm()] + [vmem()] * 3, out_specs=hbm(),...  3.67 us
    ppermute x4, starting transfers between devices, hop(): self.ahead = lax.ppermute(self.ahead, 'xy', self.hops[1])  3.67 us
  transfers between devices with their start and end apart: 19, of which 7 were waited for; matrix products, arithmetic and copies ran while one was open for 0% of the time, Pallas kernels for 15%

profile of v4, /device:TPU:1, one launch (start us, length us, event | category | flops | bytes accessed | tf_op | source)
XLA Modules:
  0.0 84.9 jit_solution(8845301094009810610)
XLA Ops:
  0.6 0.0 copy-start.1
  0.6 0.0 copy-start
  0.7 2.8 %rows_to_modes.1 = bf16[128,768]{1,0:T(8,128)(2,1)} custom-call(bf16[4,512,512]{2,1,0:T(8,128)(2,1)} %u_hbm.7, bf16[48,512]{1,0:T(8,128)(2,1)} %constant.16.clone.t_hbm), custom_call_target="tpu_custom_call" | custom-call | flops 100663296 | bytes 2097152 | tf_op jit(solution)/shard_map/rows_to_modes/pallas_call | solution.py:296
  3.4 7.4 %all-to-all-start = ((bf16[16,8,768]{2,1,0:T(8,128)(2,1)}), bf16[16,8,768]{2,1,0:T(8,128)(2,1)S(1)}, u32[]{:S(2)}, u32[]{:S(2)}) async-start(bf16[16,8,768]{2,1,0:T(8,128)(2,1)} %bitcast.17), calls=%async_computation | async-start | bytes 393216 | tf_op jit(solution)/shard_map/all_to_all | solution.py:906
  10.8 0.0 copy-done.1
  10.8 0.0 copy-done
  10.8 2.7 %prepare.1 = (bf16[8,96,512]{2,1,0:T(8,128)(2,1)S(1)}, bf16[8,96,512]{2,1,0:T(8,128)(2,1)S(1)}, bf16[256,256]{1,0:T(8,128)(2,1)S(1)}, bf16[256,256]{1,0:T(8,128)...) custom-call(s32[1]{0:T(128)} %bitcast.2.me_ref, ...), custom_call_target="tpu_custom_call" | custom-call | flops 1000000 | bytes 4194304 | tf_op jit(solution)/shard_map/prepare/pallas_call | solution.py:378
  13.5 5.6 %all-to-all-done = bf16[16,8,768]{2,1,0:T(8,128)(2,1)S(1)} async-done(((bf16[16,8,768]{2,1,0:T(8,128)(2,1)}), bf16[16,8,768]{2,1,0:T(8,128)(2,1)S(1)}, u32[]{:S(2)}, u32[]{:S(2)}) %all-to-all-start) | async-done | bytes 196640 | tf_op jit(solution)/shard_map/all_to_all | solution.py:906
  19.1 1.3 %mode_step.1 = (bf16[48,768]{1,0:T(8,128)(2,1)S(1)}, bf16[128,768]{1,0:T(8,128)(2,1)S(1)}, bf16[512,512]{1,0:T(8,128)(2,1)S(1)}, bf16[512,512]{1,0:T(8,128)(2,1)S(1)}) custom-call(bf16[128,768]{1,0:T(8,128)(2,1)S(1)} %bitcast.12, bf16[8,96,512]{2,1,0:T(8,128)(2,1)S(1)} %get-tuple-element.47.w_ref, bf16[48,128]{1,0:T(8,128)(2,1)S(1)} %get-tuple-element.48.f_ref, ...), custom_call_target="tpu_custom_call" | custom-call | flops 301989888 | bytes 1572864 | tf_op jit(solution)/shard_map/mode_step/pallas_call | solution.py:438
  20.4 11.2 %all_to_all.46 = bf16[16,8,768]{2,1,0:T(8,128)(2,1)S(1)} all-to-all(bf16[16,8,768]{2,1,0:T(8,128)(2,1)S(1)} %bitcast.15), channel_id=1, replica_groups=mesh['groups'=2,'xy'=16] {'xy'}, dimensions={0} | all-to-all | bytes 393216 | tf_op jit(solution)/shard_map/all_to_all | solution.py:906
  31.6 5.5 %pointwise.1 = (bf16[4,512,512]{2,1,0:T(8,128)(2,1)}, bf16[4,512,512]{2,1,0:T(8,128)(2,1)}, bf16[128,768]{1,0:T(8,128)(2,1)}) custom-call(bf16[4,512,512]{2,1,0:T(8,128)(2,1)} %u_hbm.7, bf16[4,512,512]{2,1,0:T(8,128)(2,1)} %c_hbm.3, bf16[512,512]{1,0:T(8,128)(2,1)S(1)} %get-tuple-element.50.u_first, bf16[512,512]{1,0:T(8,128)(2,1)S(1)} %get-tuple-element.51.c_first, ...), custom_call_target="tpu_custom_call" | custom-call | flops 1048576000 | bytes 8388608 | tf_op jit(solution)/shard_map/pointwise/pallas_call | solution.py:541
  37.1 4.5 %all-to-all-start.2 = ((bf16[16,8,768]{2,1,0:T(8,128)(2,1)}), bf16[16,8,768]{2,1,0:T(8,128)(2,1)S(1)}, u32[]{:S(2)}, u32[]{:S(2)}) async-start(bf16[16,8,768]{2,1,0:T(8,128)(2,1)} %bitcast.19), calls=%async_computation.2 | async-start | bytes 393216 | tf_op jit(solution)/shard_map/all_to_all | solution.py:906
  41.6 3.5 %local_sums.1.st_ref = bf16[24,256]{1,0:T(8,128)(2,1)S(1)} custom-call(bf16[4,512,512]{2,1,0:T(8,128)(2,1)} %u_hbm.7, bf16[4,512,512]{2,1,0:T(8,128)(2,1)} %get-tuple-element.60.d_hbm), custom_call_target="tpu_custom_call" | custom-call | flops 1048576000 | bytes 4194304 | tf_op jit(solution)/shard_map/local_sums/pallas_call | solution.py:611
  45.1 4.5 %all-to-all-done.2 = bf16[16,8,768]{2,1,0:T(8,128)(2,1)S(1)} async-done(((bf16[16,8,768]{2,1,0:T(8,128)(2,1)}), bf16[16,8,768]{2,1,0:T(8,128)(2,1)S(1)}, u32[]{:S(2)}, u32[]{:S(2)}) %all-to-all-start.2) | async-done | bytes 196640 | tf_op jit(solution)/shard_map/all_to_all | solution.py:906
  49.6 1.1 %weight_sums.1 = (bf16[48,768]{1,0:T(8,128)(2,1)S(1)}, bf16[24,2048]{1,0:T(8,128)(2,1)S(1)}, f32[24,2048]{1,0:T(8,128)S(1)}) custom-call(bf16[48,768]{1,0:T(8,128)(2,1)S(1)} %get-tuple-element.58.u_ref, bf16[128,768]{1,0:T(8,128)(2,1)S(1)} %bitcast.14, bf16[48,128]{1,0:T(8,128)(2,1)S(1)} %get-tuple-element.48.f_ref), custom_call_target="tpu_custom_call" | custom-call | flops 301989888 | bytes 4194304 | tf_op jit(solution)/shard_map/weight_sums/pallas_call | solution.py:667
  50.7 1.2 %collective-permute-start = (f32[24,2048]{1,0:T(8,128)S(1)}, f32[24,2048]{1,0:T(8,128)S(1)}, u32[]{:S(2)}, u32[]{:S(2)}) collective-permute-start(f32[24,2048]{1,0:T(8,128)S(1)} %get-tuple-element.63.s_ref), channel_id=1, source_target_pairs={{0,1},{1,0},{2,3},{3,2},{4,5},{5,4},{6,7},{7,6},{8,9},{9,8},{10,11... | collective-permute-start | bytes 589832 | tf_op jit(solution)/shard_map/ppermute | solution.py:987
  51.9 1.1 %collective-permute-done.r_ref = f32[24,2048]{1,0:T(8,128)S(1)} collective-permute-done((f32[24,2048]{1,0:T(8,128)S(1)}, f32[24,2048]{1,0:T(8,128)S(1)}, u32[]{:S(2)}, u32[]{:S(2)}) %collective-permute-start) | collective-permute-done | bytes 196640 | tf_op jit(solution)/shard_map/ppermute | solution.py:987
  53.0 0.1 collective-permute-start.1
  53.1 1.5 %collective-permute-start.2 = (bf16[24,3328]{1,0:T(8,128)(2,1)S(1)}, bf16[24,3328]{1,0:T(8,128)(2,1)S(1)}, u32[]{:S(2)}, u32[]{:S(2)}) collective-permute-start(bf16[24,3328]{1,0:T(8,128)(2,1)S(1)} %make_shard.1.refs_0_), channel_id=1, source_target_pairs={{0,2},{1,3},{4,0},{5,1},{8,4},{9,5},{12,8},{13,9},{14,12},{15,13},... | collective-permute-start | bytes 479240 | tf_op jit(solution)/shard_map/ppermute | solution.py:933
  54.6 0.9 %collective-permute-start.5 = (bf16[24,3328]{1,0:T(8,128)(2,1)S(1)}, bf16[24,3328]{1,0:T(8,128)(2,1)S(1)}, u32[]{:S(2)}, u32[]{:S(2)}) collective-permute-start(bf16[24,3328]{1,0:T(8,128)(2,1)S(1)} %make_shard.1.refs_0_), channel_id=1, source_target_pairs={{0,1},{1,0},{2,3},{3,2},{4,5},{5,4},{6,7},{7,6},{8,9},{9,8},{10,11... | collective-permute-start | bytes 479240 | tf_op jit(solution)/shard_map/ppermute | solution.py:926
  55.5 1.8 %adjoint_step.1 = bf16[128,768]{1,0:T(8,128)(2,1)} custom-call(bf16[48,768]{1,0:T(8,128)(2,1)S(1)} %get-tuple-element.68.g_ref, bf16[8,96,512]{2,1,0:T(8,128)(2,1)S(1)} %get-tuple-element.69.w_ref, bf16[128,48]{1,0:T(8,128)(2,1)S(1)} %get-tuple-element.49.i_ref), custom_call_target="tpu_custom_call" | custom-call | flops 301989888 | bytes 1572864 | tf_op jit(solution)/shard_map/adjoint_step/pallas_call | solution.py:466
  57.3 1.1 %collective-permute-done.1.refs_2_ = bf16[24,3328]{1,0:T(8,128)(2,1)S(1)} collective-permute-done((bf16[24,3328]{1,0:T(8,128)(2,1)S(1)}, bf16[24,3328]{1,0:T(8,128)(2,1)S(1)}, u32[]{:S(2)}, u32[]{:S(2)}) %collective-permute-start.1) | collective-permute-done | bytes 159776 | tf_op jit(solution)/shard_map/ppermute | solution.py:931
  58.4 0.1 collective-permute-done.2.refs_4_
  58.5 1.2 %collective-permute-start.6 = (bf16[24,3328]{1,0:T(8,128)(2,1)S(1)}, bf16[24,3328]{1,0:T(8,128)(2,1)S(1)}, u32[]{:S(2)}, u32[]{:S(2)}) collective-permute-start(bf16[24,3328]{1,0:T(8,128)(2,1)S(1)} %collective-permute-done.1.refs_2_), channel_id=1, source_target_pairs={{0,1},{1,0},{2,3},{3,2},{4,5},{5,4},{6,7},{7,6},{8,9},{9,8},{10,11... | collective-permute-start | bytes 479240 | tf_op jit(solution)/shard_map/ppermute | solution.py:926
  59.7 0.0 collective-permute-start.7
  59.7 0.6 collective-permute-start.3
  60.3 0.9 %collective-permute-start.4 = (bf16[24,3328]{1,0:T(8,128)(2,1)S(1)}, bf16[24,3328]{1,0:T(8,128)(2,1)S(1)}, u32[]{:S(2)}, u32[]{:S(2)}) collective-permute-start(bf16[24,3328]{1,0:T(8,128)(2,1)S(1)} %collective-permute-done.2.refs_4_), channel_id=1, source_target_pairs={{0,2},{1,3},{4,0},{5,1},{8,4},{9,5},{12,8},{13,9},{14,12},{15,13},... | collective-permute-start | bytes 479240 | tf_op jit(solution)/shard_map/ppermute | solution.py:933
  61.1 4.4 %all-to-all-start.3 = ((bf16[16,8,768]{2,1,0:T(8,128)(2,1)}), bf16[16,8,768]{2,1,0:T(8,128)(2,1)S(1)}, u32[]{:S(2)}, u32[]{:S(2)}) async-start(bf16[16,8,768]{2,1,0:T(8,128)(2,1)} %bitcast.18), calls=%async_computation.3 | async-start | bytes 393216 | tf_op jit(solution)/shard_map/all_to_all | solution.py:906
  65.5 0.0 collective-permute-done.5.refs_1_
  65.5 0.0 collective-permute-done.6.refs_3_
  65.5 0.0 collective-permute-done.7.refs_5_
  65.6 0.6 early_sums.1.e_hbm
  66.2 0.0 collective-permute-done.3.refs_6_
  66.2 0.0 collective-permute-done.4.refs_8_
  66.2 1.5 %collective-permute-start.8 = (bf16[24,3328]{1,0:T(8,128)(2,1)S(1)}, bf16[24,3328]{1,0:T(8,128)(2,1)S(1)}, u32[]{:S(2)}, u32[]{:S(2)}) collective-permute-start(bf16[24,3328]{1,0:T(8,128)(2,1)S(1)} %collective-permute-done.3.refs_6_), channel_id=1, source_target_pairs={{0,4},{1,5},{4,8},{5,9},{8,12},{9,13},{12,14},{13,15},{14,10},{15,... | collective-permute-start | bytes 479240 | tf_op jit(solution)/shard_map/ppermute | solution.py:931
  67.7 0.1 collective-permute-start.13
  67.7 1.1 %collective-permute-start.10 = (bf16[24,3328]{1,0:T(8,128)(2,1)S(1)}, bf16[24,3328]{1,0:T(8,128)(2,1)S(1)}, u32[]{:S(2)}, u32[]{:S(2)}) collective-permute-start(bf16[24,3328]{1,0:T(8,128)(2,1)S(1)} %collective-permute-done.3.refs_6_), channel_id=1, source_target_pairs={{0,1},{1,0},{2,3},{3,2},{4,5},{5,4},{6,7},{7,6},{8,9},{9,8},{10,11... | collective-permute-start | bytes 479240 | tf_op jit(solution)/shard_map/ppermute | solution.py:926
  68.8 0.0 collective-permute-start.11
  68.8 4.6 %collective-permute-done.8.refs_0_ = bf16[24,3328]{1,0:T(8,128)(2,1)S(1)} collective-permute-done((bf16[24,3328]{1,0:T(8,128)(2,1)S(1)}, bf16[24,3328]{1,0:T(8,128)(2,1)S(1)}, u32[]{:S(2)}, u32[]{:S(2)}) %collective-permute-start.8) | collective-permute-done | bytes 159776 | tf_op jit(solution)/shard_map/ppermute | solution.py:931
  73.4 1.6 %collective-permute-start.9 = (bf16[24,3328]{1,0:T(8,128)(2,1)S(1)}, bf16[24,3328]{1,0:T(8,128)(2,1)S(1)}, u32[]{:S(2)}, u32[]{:S(2)}) collective-permute-start(bf16[24,3328]{1,0:T(8,128)(2,1)S(1)} %collective-permute-done.8.refs_0_), channel_id=1, source_target_pairs={{0,4},{1,5},{4,8},{5,9},{8,12},{9,13},{12,14},{13,15},{14,10},{15,... | collective-permute-start | bytes 479240 | tf_op jit(solution)/shard_map/ppermute | solution.py:931
  75.0 1.0 %collective-permute-start.12 = (bf16[24,3328]{1,0:T(8,128)(2,1)S(1)}, bf16[24,3328]{1,0:T(8,128)(2,1)S(1)}, u32[]{:S(2)}, u32[]{:S(2)}) collective-permute-start(bf16[24,3328]{1,0:T(8,128)(2,1)S(1)} %collective-permute-done.8.refs_0_), channel_id=1, source_target_pairs={{0,1},{1,0},{2,3},{3,2},{4,5},{5,4},{6,7},{7,6},{8,9},{9,8},{10,11... | collective-permute-start | bytes 479240 | tf_op jit(solution)/shard_map/ppermute | solution.py:926
  76.0 0.0 collective-permute-done.13.refs_2_
  76.0 0.0 collective-permute-start.14
  76.0 0.0 all-to-all-done.3
  76.0 3.7 %back_to_field.1 = bf16[4,512,512]{2,1,0:T(8,128)(2,1)} custom-call(bf16[4,512,512]{2,1,0:T(8,128)(2,1)} %get-tuple-element.60.d_hbm, bf16[128,768]{1,0:T(8,128)(2,1)S(1)} %bitcast.11, bf16[512,48]{1,0:T(8,128)(2,1)S(1)} %get-tuple-element.75.tt_ref, bf16[256,256]{1,0:T(8,128)(2,1)S(1)} %get-tuple-element.76.w_ref), custom_call_target="tpu_custom_call" | custom-call | flops 524288000 | bytes 4194304 | tf_op jit(solution)/shard_map/back_to_field/pallas_call | solution.py:887
  79.6 0.0 collective-permute-done.10.refs_7_
  79.7 0.0 collective-permute-done.11.refs_9_
  79.7 0.8 assemble_first.1
  80.5 0.0 collective-permute-done.9.refs_4_
  80.5 0.6 collective-permute-start.15
  81.1 0.0 collective-permute-done.12.refs_1_
  81.1 0.0 collective-permute-done.14.refs_3_
  81.1 1.0 %collective-permute-done.15.refs_5_ = bf16[24,3328]{1,0:T(8,128)(2,1)S(1)} collective-permute-done((bf16[24,3328]{1,0:T(8,128)(2,1)S(1)}, bf16[24,3328]{1,0:T(8,128)(2,1)S(1)}, u32[]{:S(2)}, u32[]{:S(2)}) %collective-permute-start.15) | collective-permute-done | bytes 159776 | tf_op jit(solution)/shard_map/ppermute | solution.py:926
  82.1 2.6 %assemble.1 = (f32[16,576,128]{2,1,0:T(8,128)S(1)}, bf16[24,24,2048]{2,1,0:T(8,128)(2,1)}, f32[32,32]{1,0:T(8,128)}, f32[1,32]{1,0:T(1,128)}) custom-call(s32[1]{0:T(128)} %bitcast.2.me_ref, f32[16,576,128]{2,1,0:T(8,128)S(1)} %get-tuple-element.81.scr_in, f32[6,16,128]{2,1,0:T(8,128)} %early_sums.1.e_hbm, ...), custom_call_target="tpu_custom_call", output_to_operand_aliasing={{0}: (1, {})} | custom-call | flops 1000000 | bytes 8388608 | tf_op jit(solution)/shard_map/assemble/pallas_call | solution.py:841
  (1 shorter events, 0.0 us)
Async XLA Ops:
  0.6 10.2 %copy-start.1 = (f32[32]{0:T(128)S(1)}, f32[32]{0:T(128)}, u32[]{:S(2)}) copy-start(f32[32]{0:T(128)} %param.14) | copy-start | bytes 388
  0.6 10.2 %copy-start = (bf16[32,32]{1,0:T(8,128)(2,1)S(1)}, bf16[32,32]{1,0:T(8,128)(2,1)}, u32[]{:S(2)}) copy-start(bf16[32,32]{1,0:T(8,128)(2,1)} %l_ref.1) | copy-start | bytes 6148
  3.4 15.7 %all-to-all-start = ((bf16[16,8,768]{2,1,0:T(8,128)(2,1)}), bf16[16,8,768]{2,1,0:T(8,128)(2,1)S(1)}, u32[]{:S(2)}, u32[]{:S(2)}) async-start(bf16[16,8,768]{2,1,0:T(8,128)(2,1)} %bitcast.17), calls=%async_computation | async-start | bytes 393216 | tf_op jit(solution)/shard_map/all_to_all | solution.py:906
  37.1 12.5 %all-to-all-start.2 = ((bf16[16,8,768]{2,1,0:T(8,128)(2,1)}), bf16[16,8,768]{2,1,0:T(8,128)(2,1)S(1)}, u32[]{:S(2)}, u32[]{:S(2)}) async-start(bf16[16,8,768]{2,1,0:T(8,128)(2,1)} %bitcast.19), calls=%async_computation.2 | async-start | bytes 393216 | tf_op jit(solution)/shard_map/all_to_all | solution.py:906
  50.7 2.3 %collective-permute-start = (f32[24,2048]{1,0:T(8,128)S(1)}, f32[24,2048]{1,0:T(8,128)S(1)}, u32[]{:S(2)}, u32[]{:S(2)}) collective-permute-start(f32[24,2048]{1,0:T(8,128)S(1)} %get-tuple-element.63.s_ref), channel_id=1, source_target_pairs={{0,1},{1,0},{2,3},{3,2},{4,5},{5,4},{6,7},{7,6},{8,9},{9,8},{10,11... | collective-permute-start | bytes 589832 | tf_op jit(solution)/shard_map/ppermute | solution.py:987
  53.0 5.4 %collective-permute-start.1 = (bf16[24,3328]{1,0:T(8,128)(2,1)S(1)}, bf16[24,3328]{1,0:T(8,128)(2,1)S(1)}, u32[]{:S(2)}, u32[]{:S(2)}) collective-permute-start(bf16[24,3328]{1,0:T(8,128)(2,1)S(1)} %make_shard.1.refs_0_), channel_id=1, source_target_pairs={{0,4},{1,5},{4,8},{5,9},{8,12},{9,13},{12,14},{13,15},{14,10},{15,... | collective-permute-start | bytes 479240 | tf_op jit(solution)/shard_map/ppermute | solution.py:931
  53.1 5.4 %collective-permute-start.2 = (bf16[24,3328]{1,0:T(8,128)(2,1)S(1)}, bf16[24,3328]{1,0:T(8,128)(2,1)S(1)}, u32[]{:S(2)}, u32[]{:S(2)}) collective-permute-start(bf16[24,3328]{1,0:T(8,128)(2,1)S(1)} %make_shard.1.refs_0_), channel_id=1, source_target_pairs={{0,2},{1,3},{4,0},{5,1},{8,4},{9,5},{12,8},{13,9},{14,12},{15,13},... | collective-permute-start | bytes 479240 | tf_op jit(solution)/shard_map/ppermute | solution.py:933
  54.6 11.0 %collective-permute-start.5 = (bf16[24,3328]{1,0:T(8,128)(2,1)S(1)}, bf16[24,3328]{1,0:T(8,128)(2,1)S(1)}, u32[]{:S(2)}, u32[]{:S(2)}) collective-permute-start(bf16[24,3328]{1,0:T(8,128)(2,1)S(1)} %make_shard.1.refs_0_), channel_id=1, source_target_pairs={{0,1},{1,0},{2,3},{3,2},{4,5},{5,4},{6,7},{7,6},{8,9},{9,8},{10,11... | collective-permute-start | bytes 479240 | tf_op jit(solution)/shard_map/ppermute | solution.py:926
  58.5 7.1 %collective-permute-start.6 = (bf16[24,3328]{1,0:T(8,128)(2,1)S(1)}, bf16[24,3328]{1,0:T(8,128)(2,1)S(1)}, u32[]{:S(2)}, u32[]{:S(2)}) collective-permute-start(bf16[24,3328]{1,0:T(8,128)(2,1)S(1)} %collective-permute-done.1.refs_2_), channel_id=1, source_target_pairs={{0,1},{1,0},{2,3},{3,2},{4,5},{5,4},{6,7},{7,6},{8,9},{9,8},{10,11... | collective-permute-start | bytes 479240 | tf_op jit(solution)/shard_map/ppermute | solution.py:926
  59.7 5.9 %collective-permute-start.7 = (bf16[24,3328]{1,0:T(8,128)(2,1)S(1)}, bf16[24,3328]{1,0:T(8,128)(2,1)S(1)}, u32[]{:S(2)}, u32[]{:S(2)}) collective-permute-start(bf16[24,3328]{1,0:T(8,128)(2,1)S(1)} %collective-permute-done.2.refs_4_), channel_id=1, source_target_pairs={{0,1},{1,0},{2,3},{3,2},{4,5},{5,4},{6,7},{7,6},{8,9},{9,8},{10,11... | collective-permute-start | bytes 479240 | tf_op jit(solution)/shard_map/ppermute | solution.py:926
  59.7 6.5 %collective-permute-start.3 = (bf16[24,3328]{1,0:T(8,128)(2,1)S(1)}, bf16[24,3328]{1,0:T(8,128)(2,1)S(1)}, u32[]{:S(2)}, u32[]{:S(2)}) collective-permute-start(bf16[24,3328]{1,0:T(8,128)(2,1)S(1)} %collective-permute-done.1.refs_2_), channel_id=1, source_target_pairs={{0,4},{1,5},{4,8},{5,9},{8,12},{9,13},{12,14},{13,15},{14,10},{15,... | collective-permute-start | bytes 479240 | tf_op jit(solution)/shard_map/ppermute | solution.py:931
  60.3 5.9 %collective-permute-start.4 = (bf16[24,3328]{1,0:T(8,128)(2,1)S(1)}, bf16[24,3328]{1,0:T(8,128)(2,1)S(1)}, u32[]{:S(2)}, u32[]{:S(2)}) collective-permute-start(bf16[24,3328]{1,0:T(8,128)(2,1)S(1)} %collective-permute-done.2.refs_4_), channel_id=1, source_target_pairs={{0,2},{1,3},{4,0},{5,1},{8,4},{9,5},{12,8},{13,9},{14,12},{15,13},... | collective-permute-start | bytes 479240 | tf_op jit(solution)/shard_map/ppermute | solution.py:933
  61.1 14.8 %all-to-all-start.3 = ((bf16[16,8,768]{2,1,0:T(8,128)(2,1)}), bf16[16,8,768]{2,1,0:T(8,128)(2,1)S(1)}, u32[]{:S(2)}, u32[]{:S(2)}) async-start(bf16[16,8,768]{2,1,0:T(8,128)(2,1)} %bitcast.18), calls=%async_computation.3 | async-start | bytes 393216 | tf_op jit(solution)/shard_map/all_to_all | solution.py:906
  66.2 7.2 %collective-permute-start.8 = (bf16[24,3328]{1,0:T(8,128)(2,1)S(1)}, bf16[24,3328]{1,0:T(8,128)(2,1)S(1)}, u32[]{:S(2)}, u32[]{:S(2)}) collective-permute-start(bf16[24,3328]{1,0:T(8,128)(2,1)S(1)} %collective-permute-done.3.refs_6_), channel_id=1, source_target_pairs={{0,4},{1,5},{4,8},{5,9},{8,12},{9,13},{12,14},{13,15},{14,10},{15,... | collective-permute-start | bytes 479240 | tf_op jit(solution)/shard_map/ppermute | solution.py:931
  67.7 8.3 %collective-permute-start.13 = (bf16[24,3328]{1,0:T(8,128)(2,1)S(1)}, bf16[24,3328]{1,0:T(8,128)(2,1)S(1)}, u32[]{:S(2)}, u32[]{:S(2)}) collective-permute-start(bf16[24,3328]{1,0:T(8,128)(2,1)S(1)} %collective-permute-done.4.refs_8_), channel_id=1, source_target_pairs={{0,2},{1,3},{4,0},{5,1},{8,4},{9,5},{12,8},{13,9},{14,12},{15,13},... | collective-permute-start | bytes 479240 | tf_op jit(solution)/shard_map/ppermute | solution.py:933
  67.7 11.9 %collective-permute-start.10 = (bf16[24,3328]{1,0:T(8,128)(2,1)S(1)}, bf16[24,3328]{1,0:T(8,128)(2,1)S(1)}, u32[]{:S(2)}, u32[]{:S(2)}) collective-permute-start(bf16[24,3328]{1,0:T(8,128)(2,1)S(1)} %collective-permute-done.3.refs_6_), channel_id=1, source_target_pairs={{0,1},{1,0},{2,3},{3,2},{4,5},{5,4},{6,7},{7,6},{8,9},{9,8},{10,11... | collective-permute-start | bytes 479240 | tf_op jit(solution)/shard_map/ppermute | solution.py:926
  68.8 10.8 %collective-permute-start.11 = (bf16[24,3328]{1,0:T(8,128)(2,1)S(1)}, bf16[24,3328]{1,0:T(8,128)(2,1)S(1)}, u32[]{:S(2)}, u32[]{:S(2)}) collective-permute-start(bf16[24,3328]{1,0:T(8,128)(2,1)S(1)} %collective-permute-done.4.refs_8_), channel_id=1, source_target_pairs={{0,1},{1,0},{2,3},{3,2},{4,5},{5,4},{6,7},{7,6},{8,9},{9,8},{10,11... | collective-permute-start | bytes 479240 | tf_op jit(solution)/shard_map/ppermute | solution.py:926
  73.4 7.0 %collective-permute-start.9 = (bf16[24,3328]{1,0:T(8,128)(2,1)S(1)}, bf16[24,3328]{1,0:T(8,128)(2,1)S(1)}, u32[]{:S(2)}, u32[]{:S(2)}) collective-permute-start(bf16[24,3328]{1,0:T(8,128)(2,1)S(1)} %collective-permute-done.8.refs_0_), channel_id=1, source_target_pairs={{0,4},{1,5},{4,8},{5,9},{8,12},{9,13},{12,14},{13,15},{14,10},{15,... | collective-permute-start | bytes 479240 | tf_op jit(solution)/shard_map/ppermute | solution.py:931
  75.0 6.1 %collective-permute-start.12 = (bf16[24,3328]{1,0:T(8,128)(2,1)S(1)}, bf16[24,3328]{1,0:T(8,128)(2,1)S(1)}, u32[]{:S(2)}, u32[]{:S(2)}) collective-permute-start(bf16[24,3328]{1,0:T(8,128)(2,1)S(1)} %collective-permute-done.8.refs_0_), channel_id=1, source_target_pairs={{0,1},{1,0},{2,3},{3,2},{4,5},{5,4},{6,7},{7,6},{8,9},{9,8},{10,11... | collective-permute-start | bytes 479240 | tf_op jit(solution)/shard_map/ppermute | solution.py:926
  76.0 5.1 %collective-permute-start.14 = (bf16[24,3328]{1,0:T(8,128)(2,1)S(1)}, bf16[24,3328]{1,0:T(8,128)(2,1)S(1)}, u32[]{:S(2)}, u32[]{:S(2)}) collective-permute-start(bf16[24,3328]{1,0:T(8,128)(2,1)S(1)} %collective-permute-done.13.refs_2_), channel_id=1, source_target_pairs={{0,1},{1,0},{2,3},{3,2},{4,5},{5,4},{6,7},{7,6},{8,9},{9,8},{10,11... | collective-permute-start | bytes 479240 | tf_op jit(solution)/shard_map/ppermute | solution.py:926
  80.5 1.6 %collective-permute-start.15 = (bf16[24,3328]{1,0:T(8,128)(2,1)S(1)}, bf16[24,3328]{1,0:T(8,128)(2,1)S(1)}, u32[]{:S(2)}, u32[]{:S(2)}) collective-permute-start(bf16[24,3328]{1,0:T(8,128)(2,1)S(1)} %collective-permute-done.9.refs_4_), channel_id=1, source_target_pairs={{0,1},{1,0},{2,3},{3,2},{4,5},{5,4},{6,7},{7,6},{8,9},{9,8},{10,11... | collective-permute-start | bytes 479240 | tf_op jit(solution)/shard_map/ppermute | solution.py:926

commit v5 on v4

--- a/solution.py
+++ b/solution.py
@@ -600,19 +600,20 @@
         folded = jnp.zeros((8, LANES), F32)
         for k in range(chans // 8):
             folded = jnp.where(group8 == k, total[8 * k : 8 * k + 8], folded)
-        value = jnp.concatenate([folded, bias], axis=0)
-        high = value.astype(BF16).astype(F32)
-        mid = (value - high).astype(BF16).astype(F32)
-        low = value - high - mid
-        left = jnp.concatenate([high, mid[0:8]], axis=0)
-        right = jnp.concatenate([mid[8:16], low], axis=0)
-        out_ref[...] = jnp.concatenate([left, right], axis=1).astype(BF16)
+        high = folded.astype(BF16).astype(F32)
+        rest = (folded - high).astype(BF16).astype(F32)
+        bias_high = bias.astype(BF16).astype(F32)
+        bias_mid = (bias - bias_high).astype(BF16).astype(F32)
+        bias_low = bias - bias_high - bias_mid
+        row = lax.broadcasted_iota(jnp.int32, (8, LANES), 0)
+        terms = jnp.where(row == 0, bias_high, jnp.where(row == 1, bias_mid, jnp.where(row == 2, bias_low, 0.0)))
+        out_ref[...] = jnp.concatenate([high, rest, terms], axis=0).astype(BF16)
 
     return pl.pallas_call(
         kernel,
         in_specs=[hbm(), hbm()],
         out_specs=vmem(),
-        out_shape=jax.ShapeDtypeStruct((24, 2 * LANES), BF16),
+        out_shape=jax.ShapeDtypeStruct((24, LANES), BF16),
         scratch_shapes=[
             pltpu.VMEM(field.shape, BF16),
             pltpu.VMEM(field.shape, BF16),
@@ -714,30 +715,22 @@
 
 
 def read_sums(ref, full):
-    left = ref[:, 3 * full : 3 * full + LANES].astype(F32)
-    right = ref[:, 3 * full + LANES : 3 * full + 2 * LANES].astype(F32)
-    middle = jnp.concatenate([left[16:24], right[0:8]], axis=0)
-    return left[0:16] + middle + right[8:24]
+    sums = ref[:, 3 * full : 3 * full + LANES].astype(F32)
+    return jnp.concatenate([sums[0:8] + sums[8:16], sums[16:24]], axis=0)
 
 
 def early_sums(shards_all, chans):
     count = len(shards_all)
-    shape = (count, 16, LANES)
 
     def kernel(*refs):
-        ins, (out_hbm, out_ref, sem) = refs[:count], refs[count:]
         for n in range(count):
-            out_ref[n] = read_sums(ins[n], chans * chans)
-        copy = pltpu.make_async_copy(out_ref, out_hbm, sem)
-        copy.start()
-        copy.wait()
+            refs[count][n] = read_sums(refs[n], chans * chans)
 
     return pl.pallas_call(
         kernel,
         in_specs=[vmem()] * count,
-        out_specs=hbm(),
-        out_shape=pltpu.HBM(shape, F32),
-        scratch_shapes=[pltpu.VMEM(shape, F32), pltpu.SemaphoreType.DMA],
+        out_specs=vmem(),
+        out_shape=jax.ShapeDtypeStruct((count, 16, LANES), F32),
         compiler_params=params(),
         cost_estimate=cost(3 * 10**10, 4 * 1024 * 1024),
         name="early_sums",
@@ -804,10 +797,8 @@
     before = total_count - count
     known = early.shape[0]
 
-    def kernel(me_ref, scr_in, e_hbm, m_ref, *refs):
-        ins, (scr, g_ref, l_ref, b_ref, stat, out, e_ref, sem) = refs[:count], refs[count:]
-        fetch = pltpu.make_async_copy(e_hbm, e_ref, sem.at[tiles // 4])
-        fetch.start()
+    def kernel(me_ref, scr_in, e_ref, m_ref, *refs):
+        ins, (scr, g_ref, l_ref, b_ref, stat, out, sem) = refs[:count], refs[count:]
         places = shard_places(me_ref[0], turns, chips)
         copies = []
         for k in range(tiles):
@@ -819,7 +810,6 @@
                 lanes = pl.ds((k - 3) * LANES, 4 * LANES)
                 copies.append(pltpu.make_async_copy(out.at[:, :, lanes], g_ref.at[:, :, lanes], sem.at[k // 4]))
                 copies[-1].start()
-        fetch.wait()
         for n, (chip, core) in enumerate(places):
             if n < known:
                 stat[2 * chip + core] = e_ref[n]
@@ -833,14 +823,14 @@
         for k in range(chans // 8):
             piece = total[0:8] if k == 0 else pltpu.roll(total[0:8], LANES - k * chans, 1)
             l_ref[8 * k : 8 * k + 8, :] = piece[:, 0:chans]
-        b_ref[...] = total[8:9, 0:chans]
+        b_ref[...] = jnp.sum(total[8:16], axis=0, keepdims=True)[:, 0:chans]
         for copy in copies:
             copy.wait()
 
     shape = (rows, modes_y, 2 * full)
     return pl.pallas_call(
         kernel,
-        in_specs=[smem(), vmem(), hbm(), vmem()] + [vmem()] * count,
+        in_specs=[smem()] + [vmem()] * (3 + count),
         out_specs=(vmem(), hbm(), vmem(), vmem()),
         out_shape=(
             jax.ShapeDtypeStruct(scr.shape, F32),
@@ -852,13 +842,12 @@
         scratch_shapes=[
             pltpu.VMEM((total_count, 16, LANES), F32),
             pltpu.VMEM(shape, BF16),
-            pltpu.VMEM(early.shape, F32),
-            pltpu.SemaphoreType.DMA((tiles // 4 + 1,)),
+            pltpu.SemaphoreType.DMA((tiles // 4,)),
         ],
         compiler_params=params(),
         cost_estimate=cost(1000000, 8 * 1024 * 1024),
         name="assemble",
-    )(me, scr, *in_hbm(early), more, *shards_all)[1:]
+    )(me, scr, early, more, *shards_all)[1:]
 
 
 def back_to_field(dpre, pencil, table_t, block_weight, chips, half):

time: 85.7 us -> 85.4 us (level)
  starting transfers between devices: 28.3 us -> 29.6 us
  waiting for transfers between devices: 18 us -> 17 us
    ppermute x4, waiting for transfers between devices: 5.71 us -> 4.78 us  [hop(): self.ahead = lax.ppermute(self.ahead, 'xy', self.hops[1])]
where the time goes in v5:
time: 85.4 us; the launch traced here: 84.6 us
  starting transfers between devices  29.6 us (35%)
  Pallas kernels  25.8 us (30%)
  waiting for transfers between devices  17 us (20%)
  blocking collectives  11.2 us (13%)
  between operations  0.98 us (1%)
    all_to_all x3, starting transfers between devices, exchange(): return lax.all_to_all(pencil, 'xy', split_axis=0, concat_axis=0, tiled=True)  16.2 us
    all_to_all x1, blocking collectives, exchange(): return lax.all_to_all(pencil, 'xy', split_axis=0, concat_axis=0, tiled=True)  11.2 us
    all_to_all x3, waiting for transfers between devices, exchange(): return lax.all_to_all(pencil, 'xy', split_axis=0, concat_axis=0, tiled=True)  10.1 us
    pallas_call x1, Pallas kernels, pointwise(): pl.pallas_call(kernel, in_specs=[hbm(), hbm()] + [vmem()] * 7, out_specs=...  5.47 us
    ppermute x8, starting transfers between devices, keep(): self.parts.append(lax.ppermute(piece, 'xy', self.swap))  5.25 us
    ppermute x4, waiting for transfers between devices, hop(): self.ahead = lax.ppermute(self.ahead, 'xy', self.hops[1])  4.78 us
    ppermute x4, starting transfers between devices, hop(): self.ahead = lax.ppermute(self.ahead, 'xy', self.hops[1])  4.48 us
    pallas_call x1, Pallas kernels, back_to_field(): pl.pallas_call(kernel, in_specs=[hbm()] + [vmem()] * 3, out_specs=hbm(),...  3.67 us
  transfers between devices with their start and end apart: 19, of which 7 were waited for; matrix products, arithmetic and copies ran while one was open for 0% of the time, Pallas kernels for 15%

profile of v5, /device:TPU:1, one launch (start us, length us, event | category | flops | bytes accessed | tf_op | source)
XLA Modules:
  0.0 84.6 jit_solution(1300532277007740044)
XLA Ops:
  0.6 0.0 copy-start.1
  0.6 0.0 copy-start
  0.7 2.8 %rows_to_modes.1 = bf16[128,768]{1,0:T(8,128)(2,1)} custom-call(bf16[4,512,512]{2,1,0:T(8,128)(2,1)} %u_hbm.7, bf16[48,512]{1,0:T(8,128)(2,1)} %constant.16.clone.t_hbm), custom_call_target="tpu_custom_call" | custom-call | flops 100663296 | bytes 2097152 | tf_op jit(solution)/shard_map/rows_to_modes/pallas_call | solution.py:296
  3.4 7.4 %all-to-all-start = ((bf16[16,8,768]{2,1,0:T(8,128)(2,1)}), bf16[16,8,768]{2,1,0:T(8,128)(2,1)S(1)}, u32[]{:S(2)}, u32[]{:S(2)}) async-start(bf16[16,8,768]{2,1,0:T(8,128)(2,1)} %bitcast.17), calls=%async_computation | async-start | bytes 393216 | tf_op jit(solution)/shard_map/all_to_all | solution.py:895
  10.8 0.0 copy-done.1
  10.8 0.0 copy-done
  10.8 2.7 %prepare.1 = (bf16[8,96,512]{2,1,0:T(8,128)(2,1)S(1)}, bf16[8,96,512]{2,1,0:T(8,128)(2,1)S(1)}, bf16[256,256]{1,0:T(8,128)(2,1)S(1)}, bf16[256,256]{1,0:T(8,128)...) custom-call(s32[1]{0:T(128)} %bitcast.2.me_ref, ...), custom_call_target="tpu_custom_call" | custom-call | flops 1000000 | bytes 4194304 | tf_op jit(solution)/shard_map/prepare/pallas_call | solution.py:378
  13.5 5.6 %all-to-all-done = bf16[16,8,768]{2,1,0:T(8,128)(2,1)S(1)} async-done(((bf16[16,8,768]{2,1,0:T(8,128)(2,1)}), bf16[16,8,768]{2,1,0:T(8,128)(2,1)S(1)}, u32[]{:S(2)}, u32[]{:S(2)}) %all-to-all-start) | async-done | bytes 196640 | tf_op jit(solution)/shard_map/all_to_all | solution.py:895
  19.1 1.3 %mode_step.1 = (bf16[48,768]{1,0:T(8,128)(2,1)S(1)}, bf16[128,768]{1,0:T(8,128)(2,1)S(1)}, bf16[512,512]{1,0:T(8,128)(2,1)S(1)}, bf16[512,512]{1,0:T(8,128)(2,1)S(1)}) custom-call(bf16[128,768]{1,0:T(8,128)(2,1)S(1)} %bitcast.12, bf16[8,96,512]{2,1,0:T(8,128)(2,1)S(1)} %get-tuple-element.47.w_ref, bf16[48,128]{1,0:T(8,128)(2,1)S(1)} %get-tuple-element.48.f_ref, ...), custom_call_target="tpu_custom_call" | custom-call | flops 301989888 | bytes 1572864 | tf_op jit(solution)/shard_map/mode_step/pallas_call | solution.py:438
  20.4 11.2 %all_to_all.46 = bf16[16,8,768]{2,1,0:T(8,128)(2,1)S(1)} all-to-all(bf16[16,8,768]{2,1,0:T(8,128)(2,1)S(1)} %bitcast.15), channel_id=1, replica_groups=mesh['groups'=2,'xy'=16] {'xy'}, dimensions={0} | all-to-all | bytes 393216 | tf_op jit(solution)/shard_map/all_to_all | solution.py:895
  31.6 5.5 %pointwise.1 = (bf16[4,512,512]{2,1,0:T(8,128)(2,1)}, bf16[4,512,512]{2,1,0:T(8,128)(2,1)}, bf16[128,768]{1,0:T(8,128)(2,1)}) custom-call(bf16[4,512,512]{2,1,0:T(8,128)(2,1)} %u_hbm.7, bf16[4,512,512]{2,1,0:T(8,128)(2,1)} %c_hbm.3, bf16[512,512]{1,0:T(8,128)(2,1)S(1)} %get-tuple-element.50.u_first, bf16[512,512]{1,0:T(8,128)(2,1)S(1)} %get-tuple-element.51.c_first, ...), custom_call_target="tpu_custom_call" | custom-call | flops 1048576000 | bytes 8388608 | tf_op jit(solution)/shard_map/pointwise/pallas_call | solution.py:541
  37.1 4.5 %all-to-all-start.2 = ((bf16[16,8,768]{2,1,0:T(8,128)(2,1)}), bf16[16,8,768]{2,1,0:T(8,128)(2,1)S(1)}, u32[]{:S(2)}, u32[]{:S(2)}) async-start(bf16[16,8,768]{2,1,0:T(8,128)(2,1)} %bitcast.19), calls=%async_computation.2 | async-start | bytes 393216 | tf_op jit(solution)/shard_map/all_to_all | solution.py:895
  41.6 3.5 %local_sums.1.st_ref = bf16[24,128]{1,0:T(8,128)(2,1)S(1)} custom-call(bf16[4,512,512]{2,1,0:T(8,128)(2,1)} %u_hbm.7, bf16[4,512,512]{2,1,0:T(8,128)(2,1)} %get-tuple-element.60.d_hbm), custom_call_target="tpu_custom_call" | custom-call | flops 1048576000 | bytes 4194304 | tf_op jit(solution)/shard_map/local_sums/pallas_call | solution.py:612
  45.1 4.5 %all-to-all-done.2 = bf16[16,8,768]{2,1,0:T(8,128)(2,1)S(1)} async-done(((bf16[16,8,768]{2,1,0:T(8,128)(2,1)}), bf16[16,8,768]{2,1,0:T(8,128)(2,1)S(1)}, u32[]{:S(2)}, u32[]{:S(2)}) %all-to-all-start.2) | async-done | bytes 196640 | tf_op jit(solution)/shard_map/all_to_all | solution.py:895
  49.6 1.1 %weight_sums.1 = (bf16[48,768]{1,0:T(8,128)(2,1)S(1)}, bf16[24,2048]{1,0:T(8,128)(2,1)S(1)}, f32[24,2048]{1,0:T(8,128)S(1)}) custom-call(bf16[48,768]{1,0:T(8,128)(2,1)S(1)} %get-tuple-element.58.u_ref, bf16[128,768]{1,0:T(8,128)(2,1)S(1)} %bitcast.14, bf16[48,128]{1,0:T(8,128)(2,1)S(1)} %get-tuple-element.48.f_ref), custom_call_target="tpu_custom_call" | custom-call | flops 301989888 | bytes 4194304 | tf_op jit(solution)/shard_map/weight_sums/pallas_call | solution.py:668
  50.7 1.2 %collective-permute-start = (f32[24,2048]{1,0:T(8,128)S(1)}, f32[24,2048]{1,0:T(8,128)S(1)}, u32[]{:S(2)}, u32[]{:S(2)}) collective-permute-start(f32[24,2048]{1,0:T(8,128)S(1)} %get-tuple-element.63.s_ref), channel_id=1, source_target_pairs={{0,1},{1,0},{2,3},{3,2},{4,5},{5,4},{6,7},{7,6},{8,9},{9,8},{10,11... | collective-permute-start | bytes 589832 | tf_op jit(solution)/shard_map/ppermute | solution.py:976
  51.9 1.1 %collective-permute-done.r_ref = f32[24,2048]{1,0:T(8,128)S(1)} collective-permute-done((f32[24,2048]{1,0:T(8,128)S(1)}, f32[24,2048]{1,0:T(8,128)S(1)}, u32[]{:S(2)}, u32[]{:S(2)}) %collective-permute-start) | collective-permute-done | bytes 196640 | tf_op jit(solution)/shard_map/ppermute | solution.py:976
  53.0 0.1 collective-permute-start.1
  53.1 1.5 %collective-permute-start.2 = (bf16[24,3200]{1,0:T(8,128)(2,1)S(1)}, bf16[24,3200]{1,0:T(8,128)(2,1)S(1)}, u32[]{:S(2)}, u32[]{:S(2)}) collective-permute-start(bf16[24,3200]{1,0:T(8,128)(2,1)S(1)} %make_shard.1.refs_0_), channel_id=1, source_target_pairs={{0,2},{1,3},{4,0},{5,1},{8,4},{9,5},{12,8},{13,9},{14,12},{15,13},... | collective-permute-start | bytes 460808 | tf_op jit(solution)/shard_map/ppermute | solution.py:922
  54.5 0.9 %collective-permute-start.5 = (bf16[24,3200]{1,0:T(8,128)(2,1)S(1)}, bf16[24,3200]{1,0:T(8,128)(2,1)S(1)}, u32[]{:S(2)}, u32[]{:S(2)}) collective-permute-start(bf16[24,3200]{1,0:T(8,128)(2,1)S(1)} %make_shard.1.refs_0_), channel_id=1, source_target_pairs={{0,1},{1,0},{2,3},{3,2},{4,5},{5,4},{6,7},{7,6},{8,9},{9,8},{10,11... | collective-permute-start | bytes 460808 | tf_op jit(solution)/shard_map/ppermute | solution.py:915
  55.5 1.8 %adjoint_step.1 = bf16[128,768]{1,0:T(8,128)(2,1)} custom-call(bf16[48,768]{1,0:T(8,128)(2,1)S(1)} %get-tuple-element.68.g_ref, bf16[8,96,512]{2,1,0:T(8,128)(2,1)S(1)} %get-tuple-element.69.w_ref, bf16[128,48]{1,0:T(8,128)(2,1)S(1)} %get-tuple-element.49.i_ref), custom_call_target="tpu_custom_call" | custom-call | flops 301989888 | bytes 1572864 | tf_op jit(solution)/shard_map/adjoint_step/pallas_call | solution.py:466
  57.3 1.0 %collective-permute-done.1.refs_2_ = bf16[24,3200]{1,0:T(8,128)(2,1)S(1)} collective-permute-done((bf16[24,3200]{1,0:T(8,128)(2,1)S(1)}, bf16[24,3200]{1,0:T(8,128)(2,1)S(1)}, u32[]{:S(2)}, u32[]{:S(2)}) %collective-permute-start.1) | collective-permute-done | bytes 153632 | tf_op jit(solution)/shard_map/ppermute | solution.py:920
  58.3 0.1 collective-permute-done.2.refs_4_
  58.3 1.2 %collective-permute-start.6 = (bf16[24,3200]{1,0:T(8,128)(2,1)S(1)}, bf16[24,3200]{1,0:T(8,128)(2,1)S(1)}, u32[]{:S(2)}, u32[]{:S(2)}) collective-permute-start(bf16[24,3200]{1,0:T(8,128)(2,1)S(1)} %collective-permute-done.1.refs_2_), channel_id=1, source_target_pairs={{0,1},{1,0},{2,3},{3,2},{4,5},{5,4},{6,7},{7,6},{8,9},{9,8},{10,11... | collective-permute-start | bytes 460808 | tf_op jit(solution)/shard_map/ppermute | solution.py:915
  59.5 0.0 collective-permute-start.7
  59.5 0.6 collective-permute-start.3
  60.1 0.9 %collective-permute-start.4 = (bf16[24,3200]{1,0:T(8,128)(2,1)S(1)}, bf16[24,3200]{1,0:T(8,128)(2,1)S(1)}, u32[]{:S(2)}, u32[]{:S(2)}) collective-permute-start(bf16[24,3200]{1,0:T(8,128)(2,1)S(1)} %collective-permute-done.2.refs_4_), channel_id=1, source_target_pairs={{0,2},{1,3},{4,0},{5,1},{8,4},{9,5},{12,8},{13,9},{14,12},{15,13},... | collective-permute-start | bytes 460808 | tf_op jit(solution)/shard_map/ppermute | solution.py:922
  61.0 4.4 %all-to-all-start.3 = ((bf16[16,8,768]{2,1,0:T(8,128)(2,1)}), bf16[16,8,768]{2,1,0:T(8,128)(2,1)S(1)}, u32[]{:S(2)}, u32[]{:S(2)}) async-start(bf16[16,8,768]{2,1,0:T(8,128)(2,1)} %bitcast.18), calls=%async_computation.3 | async-start | bytes 393216 | tf_op jit(solution)/shard_map/all_to_all | solution.py:895
  65.4 0.0 collective-permute-done.5.refs_1_
  65.4 0.0 collective-permute-done.6.refs_3_
  65.4 0.0 collective-permute-done.7.refs_5_
  65.4 0.0 collective-permute-done.3.refs_6_
  65.4 0.0 collective-permute-done.4.refs_8_
  65.5 1.5 %collective-permute-start.8 = (bf16[24,3200]{1,0:T(8,128)(2,1)S(1)}, bf16[24,3200]{1,0:T(8,128)(2,1)S(1)}, u32[]{:S(2)}, u32[]{:S(2)}) collective-permute-start(bf16[24,3200]{1,0:T(8,128)(2,1)S(1)} %collective-permute-done.3.refs_6_), channel_id=1, source_target_pairs={{0,4},{1,5},{4,8},{5,9},{8,12},{9,13},{12,14},{13,15},{14,10},{15,... | collective-permute-start | bytes 460808 | tf_op jit(solution)/shard_map/ppermute | solution.py:920
  66.9 0.1 collective-permute-start.13
  67.0 1.6 %collective-permute-start.10 = (bf16[24,3200]{1,0:T(8,128)(2,1)S(1)}, bf16[24,3200]{1,0:T(8,128)(2,1)S(1)}, u32[]{:S(2)}, u32[]{:S(2)}) collective-permute-start(bf16[24,3200]{1,0:T(8,128)(2,1)S(1)} %collective-permute-done.3.refs_6_), channel_id=1, source_target_pairs={{0,1},{1,0},{2,3},{3,2},{4,5},{5,4},{6,7},{7,6},{8,9},{9,8},{10,11... | collective-permute-start | bytes 460808 | tf_op jit(solution)/shard_map/ppermute | solution.py:915
  68.6 0.0 collective-permute-start.11
  68.6 3.8 %collective-permute-done.8.refs_0_ = bf16[24,3200]{1,0:T(8,128)(2,1)S(1)} collective-permute-done((bf16[24,3200]{1,0:T(8,128)(2,1)S(1)}, bf16[24,3200]{1,0:T(8,128)(2,1)S(1)}, u32[]{:S(2)}, u32[]{:S(2)}) %collective-permute-start.8) | collective-permute-done | bytes 153632 | tf_op jit(solution)/shard_map/ppermute | solution.py:920
  72.4 2.4 %collective-permute-start.9 = (bf16[24,3200]{1,0:T(8,128)(2,1)S(1)}, bf16[24,3200]{1,0:T(8,128)(2,1)S(1)}, u32[]{:S(2)}, u32[]{:S(2)}) collective-permute-start(bf16[24,3200]{1,0:T(8,128)(2,1)S(1)} %collective-permute-done.8.refs_0_), channel_id=1, source_target_pairs={{0,4},{1,5},{4,8},{5,9},{8,12},{9,13},{12,14},{13,15},{14,10},{15,... | collective-permute-start | bytes 460808 | tf_op jit(solution)/shard_map/ppermute | solution.py:920
  74.7 1.0 %collective-permute-start.12 = (bf16[24,3200]{1,0:T(8,128)(2,1)S(1)}, bf16[24,3200]{1,0:T(8,128)(2,1)S(1)}, u32[]{:S(2)}, u32[]{:S(2)}) collective-permute-start(bf16[24,3200]{1,0:T(8,128)(2,1)S(1)} %collective-permute-done.8.refs_0_), channel_id=1, source_target_pairs={{0,1},{1,0},{2,3},{3,2},{4,5},{5,4},{6,7},{7,6},{8,9},{9,8},{10,11... | collective-permute-start | bytes 460808 | tf_op jit(solution)/shard_map/ppermute | solution.py:915
  75.7 0.0 collective-permute-done.13.refs_2_
  75.7 0.0 collective-permute-start.14
  75.7 0.0 all-to-all-done.3
  75.7 3.7 %back_to_field.1 = bf16[4,512,512]{2,1,0:T(8,128)(2,1)} custom-call(bf16[4,512,512]{2,1,0:T(8,128)(2,1)} %get-tuple-element.60.d_hbm, bf16[128,768]{1,0:T(8,128)(2,1)S(1)} %bitcast.11, bf16[512,48]{1,0:T(8,128)(2,1)S(1)} %get-tuple-element.75.tt_ref, bf16[256,256]{1,0:T(8,128)(2,1)S(1)} %get-tuple-element.76.w_ref), custom_call_target="tpu_custom_call" | custom-call | flops 524288000 | bytes 4194304 | tf_op jit(solution)/shard_map/back_to_field/pallas_call | solution.py:876
  79.4 0.0 collective-permute-done.10.refs_7_
  79.4 0.0 collective-permute-done.11.refs_9_
  79.4 0.8 assemble_first.1
  80.2 0.0 collective-permute-done.9.refs_4_
  80.2 0.6 collective-permute-start.15
  80.7 0.0 collective-permute-done.12.refs_1_
  80.7 0.0 collective-permute-done.14.refs_3_
  80.8 1.0 %collective-permute-done.15.refs_5_ = bf16[24,3200]{1,0:T(8,128)(2,1)S(1)} collective-permute-done((bf16[24,3200]{1,0:T(8,128)(2,1)S(1)}, bf16[24,3200]{1,0:T(8,128)(2,1)S(1)}, u32[]{:S(2)}, u32[]{:S(2)}) %collective-permute-start.15) | collective-permute-done | bytes 153632 | tf_op jit(solution)/shard_map/ppermute | solution.py:915
  81.8 2.6 %assemble.1 = (f32[16,576,128]{2,1,0:T(8,128)S(1)}, bf16[24,24,2048]{2,1,0:T(8,128)(2,1)}, f32[32,32]{1,0:T(8,128)}, f32[1,32]{1,0:T(1,128)}) custom-call(s32[1]{0:T(128)} %bitcast.2.me_ref, f32[16,576,128]{2,1,0:T(8,128)S(1)} %get-tuple-element.81.scr_in, f32[6,16,128]{2,1,0:T(8,128)S(1)} %early_sums.1.e_ref, ...), custom_call_target="tpu_custom_call", output_to_operand_aliasing={{0}: (1, {})} | custom-call | flops 1000000 | bytes 8388608 | tf_op jit(solution)/shard_map/assemble/pallas_call | solution.py:831
  (2 shorter events, 0.1 us)
Async XLA Ops:
  0.6 10.2 %copy-start.1 = (f32[32]{0:T(128)S(1)}, f32[32]{0:T(128)}, u32[]{:S(2)}) copy-start(f32[32]{0:T(128)} %param.14) | copy-start | bytes 388
  0.6 10.2 %copy-start = (bf16[32,32]{1,0:T(8,128)(2,1)S(1)}, bf16[32,32]{1,0:T(8,128)(2,1)}, u32[]{:S(2)}) copy-start(bf16[32,32]{1,0:T(8,128)(2,1)} %l_ref.1) | copy-start | bytes 6148
  3.4 15.7 %all-to-all-start = ((bf16[16,8,768]{2,1,0:T(8,128)(2,1)}), bf16[16,8,768]{2,1,0:T(8,128)(2,1)S(1)}, u32[]{:S(2)}, u32[]{:S(2)}) async-start(bf16[16,8,768]{2,1,0:T(8,128)(2,1)} %bitcast.17), calls=%async_computation | async-start | bytes 393216 | tf_op jit(solution)/shard_map/all_to_all | solution.py:895
  37.1 12.5 %all-to-all-start.2 = ((bf16[16,8,768]{2,1,0:T(8,128)(2,1)}), bf16[16,8,768]{2,1,0:T(8,128)(2,1)S(1)}, u32[]{:S(2)}, u32[]{:S(2)}) async-start(bf16[16,8,768]{2,1,0:T(8,128)(2,1)} %bitcast.19), calls=%async_computation.2 | async-start | bytes 393216 | tf_op jit(solution)/shard_map/all_to_all | solution.py:895
  50.7 2.3 %collective-permute-start = (f32[24,2048]{1,0:T(8,128)S(1)}, f32[24,2048]{1,0:T(8,128)S(1)}, u32[]{:S(2)}, u32[]{:S(2)}) collective-permute-start(f32[24,2048]{1,0:T(8,128)S(1)} %get-tuple-element.63.s_ref), channel_id=1, source_target_pairs={{0,1},{1,0},{2,3},{3,2},{4,5},{5,4},{6,7},{7,6},{8,9},{9,8},{10,11... | collective-permute-start | bytes 589832 | tf_op jit(solution)/shard_map/ppermute | solution.py:976
  53.0 5.2 %collective-permute-start.1 = (bf16[24,3200]{1,0:T(8,128)(2,1)S(1)}, bf16[24,3200]{1,0:T(8,128)(2,1)S(1)}, u32[]{:S(2)}, u32[]{:S(2)}) collective-permute-start(bf16[24,3200]{1,0:T(8,128)(2,1)S(1)} %make_shard.1.refs_0_), channel_id=1, source_target_pairs={{0,4},{1,5},{4,8},{5,9},{8,12},{9,13},{12,14},{13,15},{14,10},{15,... | collective-permute-start | bytes 460808 | tf_op jit(solution)/shard_map/ppermute | solution.py:920
  53.1 5.2 %collective-permute-start.2 = (bf16[24,3200]{1,0:T(8,128)(2,1)S(1)}, bf16[24,3200]{1,0:T(8,128)(2,1)S(1)}, u32[]{:S(2)}, u32[]{:S(2)}) collective-permute-start(bf16[24,3200]{1,0:T(8,128)(2,1)S(1)} %make_shard.1.refs_0_), channel_id=1, source_target_pairs={{0,2},{1,3},{4,0},{5,1},{8,4},{9,5},{12,8},{13,9},{14,12},{15,13},... | collective-permute-start | bytes 460808 | tf_op jit(solution)/shard_map/ppermute | solution.py:922
  54.5 10.8 %collective-permute-start.5 = (bf16[24,3200]{1,0:T(8,128)(2,1)S(1)}, bf16[24,3200]{1,0:T(8,128)(2,1)S(1)}, u32[]{:S(2)}, u32[]{:S(2)}) collective-permute-start(bf16[24,3200]{1,0:T(8,128)(2,1)S(1)} %make_shard.1.refs_0_), channel_id=1, source_target_pairs={{0,1},{1,0},{2,3},{3,2},{4,5},{5,4},{6,7},{7,6},{8,9},{9,8},{10,11... | collective-permute-start | bytes 460808 | tf_op jit(solution)/shard_map/ppermute | solution.py:915
  58.3 7.1 %collective-permute-start.6 = (bf16[24,3200]{1,0:T(8,128)(2,1)S(1)}, bf16[24,3200]{1,0:T(8,128)(2,1)S(1)}, u32[]{:S(2)}, u32[]{:S(2)}) collective-permute-start(bf16[24,3200]{1,0:T(8,128)(2,1)S(1)} %collective-permute-done.1.refs_2_), channel_id=1, source_target_pairs={{0,1},{1,0},{2,3},{3,2},{4,5},{5,4},{6,7},{7,6},{8,9},{9,8},{10,11... | collective-permute-start | bytes 460808 | tf_op jit(solution)/shard_map/ppermute | solution.py:915
  59.5 5.9 %collective-permute-start.7 = (bf16[24,3200]{1,0:T(8,128)(2,1)S(1)}, bf16[24,3200]{1,0:T(8,128)(2,1)S(1)}, u32[]{:S(2)}, u32[]{:S(2)}) collective-permute-start(bf16[24,3200]{1,0:T(8,128)(2,1)S(1)} %collective-permute-done.2.refs_4_), channel_id=1, source_target_pairs={{0,1},{1,0},{2,3},{3,2},{4,5},{5,4},{6,7},{7,6},{8,9},{9,8},{10,11... | collective-permute-start | bytes 460808 | tf_op jit(solution)/shard_map/ppermute | solution.py:915
  59.5 5.9 %collective-permute-start.3 = (bf16[24,3200]{1,0:T(8,128)(2,1)S(1)}, bf16[24,3200]{1,0:T(8,128)(2,1)S(1)}, u32[]{:S(2)}, u32[]{:S(2)}) collective-permute-start(bf16[24,3200]{1,0:T(8,128)(2,1)S(1)} %collective-permute-done.1.refs_2_), channel_id=1, source_target_pairs={{0,4},{1,5},{4,8},{5,9},{8,12},{9,13},{12,14},{13,15},{14,10},{15,... | collective-permute-start | bytes 460808 | tf_op jit(solution)/shard_map/ppermute | solution.py:920
  60.1 5.3 %collective-permute-start.4 = (bf16[24,3200]{1,0:T(8,128)(2,1)S(1)}, bf16[24,3200]{1,0:T(8,128)(2,1)S(1)}, u32[]{:S(2)}, u32[]{:S(2)}) collective-permute-start(bf16[24,3200]{1,0:T(8,128)(2,1)S(1)} %collective-permute-done.2.refs_4_), channel_id=1, source_target_pairs={{0,2},{1,3},{4,0},{5,1},{8,4},{9,5},{12,8},{13,9},{14,12},{15,13},... | collective-permute-start | bytes 460808 | tf_op jit(solution)/shard_map/ppermute | solution.py:922
  61.0 14.7 %all-to-all-start.3 = ((bf16[16,8,768]{2,1,0:T(8,128)(2,1)}), bf16[16,8,768]{2,1,0:T(8,128)(2,1)S(1)}, u32[]{:S(2)}, u32[]{:S(2)}) async-start(bf16[16,8,768]{2,1,0:T(8,128)(2,1)} %bitcast.18), calls=%async_computation.3 | async-start | bytes 393216 | tf_op jit(solution)/shard_map/all_to_all | solution.py:895
  65.5 6.9 %collective-permute-start.8 = (bf16[24,3200]{1,0:T(8,128)(2,1)S(1)}, bf16[24,3200]{1,0:T(8,128)(2,1)S(1)}, u32[]{:S(2)}, u32[]{:S(2)}) collective-permute-start(bf16[24,3200]{1,0:T(8,128)(2,1)S(1)} %collective-permute-done.3.refs_6_), channel_id=1, source_target_pairs={{0,4},{1,5},{4,8},{5,9},{8,12},{9,13},{12,14},{13,15},{14,10},{15,... | collective-permute-start | bytes 460808 | tf_op jit(solution)/shard_map/ppermute | solution.py:920
  66.9 8.8 %collective-permute-start.13 = (bf16[24,3200]{1,0:T(8,128)(2,1)S(1)}, bf16[24,3200]{1,0:T(8,128)(2,1)S(1)}, u32[]{:S(2)}, u32[]{:S(2)}) collective-permute-start(bf16[24,3200]{1,0:T(8,128)(2,1)S(1)} %collective-permute-done.4.refs_8_), channel_id=1, source_target_pairs={{0,2},{1,3},{4,0},{5,1},{8,4},{9,5},{12,8},{13,9},{14,12},{15,13},... | collective-permute-start | bytes 460808 | tf_op jit(solution)/shard_map/ppermute | solution.py:922
  67.0 12.4 %collective-permute-start.10 = (bf16[24,3200]{1,0:T(8,128)(2,1)S(1)}, bf16[24,3200]{1,0:T(8,128)(2,1)S(1)}, u32[]{:S(2)}, u32[]{:S(2)}) collective-permute-start(bf16[24,3200]{1,0:T(8,128)(2,1)S(1)} %collective-permute-done.3.refs_6_), channel_id=1, source_target_pairs={{0,1},{1,0},{2,3},{3,2},{4,5},{5,4},{6,7},{7,6},{8,9},{9,8},{10,11... | collective-permute-start | bytes 460808 | tf_op jit(solution)/shard_map/ppermute | solution.py:915
  68.6 10.8 %collective-permute-start.11 = (bf16[24,3200]{1,0:T(8,128)(2,1)S(1)}, bf16[24,3200]{1,0:T(8,128)(2,1)S(1)}, u32[]{:S(2)}, u32[]{:S(2)}) collective-permute-start(bf16[24,3200]{1,0:T(8,128)(2,1)S(1)} %collective-permute-done.4.refs_8_), channel_id=1, source_target_pairs={{0,1},{1,0},{2,3},{3,2},{4,5},{5,4},{6,7},{7,6},{8,9},{9,8},{10,11... | collective-permute-start | bytes 460808 | tf_op jit(solution)/shard_map/ppermute | solution.py:915
  72.4 7.8 %collective-permute-start.9 = (bf16[24,3200]{1,0:T(8,128)(2,1)S(1)}, bf16[24,3200]{1,0:T(8,128)(2,1)S(1)}, u32[]{:S(2)}, u32[]{:S(2)}) collective-permute-start(bf16[24,3200]{1,0:T(8,128)(2,1)S(1)} %collective-permute-done.8.refs_0_), channel_id=1, source_target_pairs={{0,4},{1,5},{4,8},{5,9},{8,12},{9,13},{12,14},{13,15},{14,10},{15,... | collective-permute-start | bytes 460808 | tf_op jit(solution)/shard_map/ppermute | solution.py:920
  74.7 6.0 %collective-permute-start.12 = (bf16[24,3200]{1,0:T(8,128)(2,1)S(1)}, bf16[24,3200]{1,0:T(8,128)(2,1)S(1)}, u32[]{:S(2)}, u32[]{:S(2)}) collective-permute-start(bf16[24,3200]{1,0:T(8,128)(2,1)S(1)} %collective-permute-done.8.refs_0_), channel_id=1, source_target_pairs={{0,1},{1,0},{2,3},{3,2},{4,5},{5,4},{6,7},{7,6},{8,9},{9,8},{10,11... | collective-permute-start | bytes 460808 | tf_op jit(solution)/shard_map/ppermute | solution.py:915
  75.7 5.1 %collective-permute-start.14 = (bf16[24,3200]{1,0:T(8,128)(2,1)S(1)}, bf16[24,3200]{1,0:T(8,128)(2,1)S(1)}, u32[]{:S(2)}, u32[]{:S(2)}) collective-permute-start(bf16[24,3200]{1,0:T(8,128)(2,1)S(1)} %collective-permute-done.13.refs_2_), channel_id=1, source_target_pairs={{0,1},{1,0},{2,3},{3,2},{4,5},{5,4},{6,7},{7,6},{8,9},{9,8},{10,11... | collective-permute-start | bytes 460808 | tf_op jit(solution)/shard_map/ppermute | solution.py:915
  80.2 1.6 %collective-permute-start.15 = (bf16[24,3200]{1,0:T(8,128)(2,1)S(1)}, bf16[24,3200]{1,0:T(8,128)(2,1)S(1)}, u32[]{:S(2)}, u32[]{:S(2)}) collective-permute-start(bf16[24,3200]{1,0:T(8,128)(2,1)S(1)} %collective-permute-done.9.refs_4_), channel_id=1, source_target_pairs={{0,1},{1,0},{2,3},{3,2},{4,5},{5,4},{6,7},{7,6},{8,9},{9,8},{10,11... | collective-permute-start | bytes 460808 | tf_op jit(solution)/shard_map/ppermute | solution.py:915

commit v6 on v5

--- a/solution.py
+++ b/solution.py
@@ -266,16 +266,16 @@
 
 def cut_lanes(dst, src):
     for k in range(dst.shape[0]):
-        dst[k] = src[:, k * LANES : (k + 1) * LANES].astype(F32)
+        dst[k, 0 : src.shape[0], :] = src[:, k * LANES : (k + 1) * LANES].astype(F32)
 
 
 def join_lanes(dst, src):
     for k in range(src.shape[0]):
-        dst[:, k * LANES : (k + 1) * LANES] = src[k].astype(BF16)
+        dst[:, k * LANES : (k + 1) * LANES] = src[k, 0 : dst.shape[0], :].astype(BF16)
 
 
 def cut_shape(shape):
-    return (shape[1] // LANES, shape[0], LANES)
+    return (shape[1] // LANES, shape[0] + 16, LANES)
 
 
 def rows_to_modes(field, table, chips, half):
@@ -382,9 +382,9 @@
         out_shape=(wide, wide, block, block, jax.ShapeDtypeStruct((8, 2 * half), F32)) + held,
         scratch_shapes=[
             pltpu.VMEM(weights.shape, BF16),
-            pltpu.VMEM((tiles, modes_x * modes_y, LANES), F32),
+            pltpu.VMEM((tiles, (modes_x + 1) * modes_y, LANES), F32),
             pltpu.VMEM((groups, rows, LANES), F32),
-            pltpu.VMEM((full2 // 2, LANES), F32),
+            pltpu.VMEM((full2 // 2 + chans, LANES), F32),
             pltpu.VMEM((full2 // 2, LANES), F32),
             pltpu.SemaphoreType.DMA((modes_x // batch,)),
             pltpu.SemaphoreType.DMA((count,)),
@@ -499,6 +499,9 @@
         bias = jnp.concatenate(parts + [jnp.zeros((depth - modes - 3, width), F32)], axis=0)
         bias = (0.5 * bias).astype(BF16)
         weight = (0.5 * w_ref[...].astype(F32)).astype(BF16)
+
+        def transform_row(x):
+            scatter_rows(dscr, dot(t_ref[...], dpre_ref[x]), x, chips, half)
 
         def one_row(x):
             if x > 0:
@@ -527,10 +530,12 @@
                         dpre_ref[x, place, lanes] = (c_ref[place, lanes].astype(F32) * grad).astype(BF16)
             pltpu.make_async_copy(out_ref.at[x], out_hbm.at[x], out_sem.at[x]).start()
             pltpu.make_async_copy(dpre_ref.at[x], dpre_hbm.at[x], out_sem.at[rows + x]).start()
-            scatter_rows(dscr, dot(t_ref[...], dpre_ref[x]), x, chips, half)
+            if x > 0:
+                transform_row(x - 1)
 
         for x in range(rows):
             one_row(x)
+        transform_row(rows - 1)
         join_lanes(send_ref, dscr)
         pltpu.make_async_copy(send_ref, send_hbm, out_sem.at[2 * rows]).start()
         for x in range(rows):
@@ -746,7 +751,7 @@
 
 
 def place_tile(scr, refs, places, turns, k, modes_y, tiles):
-    rows = scr.shape[1] // modes_y
+    rows = refs[0].shape[0]
     part = tiles // 4
     chips = modes_y // 3
     keeper = k % (2 * part) // part
@@ -779,7 +784,7 @@
         in_specs=[smem()] + [vmem()] * count,
         out_specs=(vmem(), vmem()),
         out_shape=(
-            jax.ShapeDtypeStruct((tiles, rows * modes_y, LANES), F32),
+            jax.ShapeDtypeStruct((tiles, (rows + 1) * modes_y, LANES), F32),
             jax.ShapeDtypeStruct((count - known, 16, LANES), F32),
         ),
         compiler_params=params(),

time: 85.4 us -> 84.9 us (level)
  no operation moved by 1% of the time
where the time goes in v6:
time: 84.9 us; the launch traced here: 84.1 us
  starting transfers between devices  29.6 us (35%)
  Pallas kernels  25.3 us (30%)
  waiting for transfers between devices  17 us (20%)
  blocking collectives  11.2 us (13%)
  between operations  0.98 us (1%)
    all_to_all x3, starting transfers between devices, exchange(): return lax.all_to_all(pencil, 'xy', split_axis=0, concat_axis=0, tiled=True)  16.2 us
    all_to_all x1, blocking collectives, exchange(): return lax.all_to_all(pencil, 'xy', split_axis=0, concat_axis=0, tiled=True)  11.2 us
    all_to_all x3, waiting for transfers between devices, exchange(): return lax.all_to_all(pencil, 'xy', split_axis=0, concat_axis=0, tiled=True)  10.1 us
    ppermute x8, starting transfers between devices, keep(): self.parts.append(lax.ppermute(piece, 'xy', self.swap))  5.25 us
    pallas_call x1, Pallas kernels, pointwise(): pl.pallas_call(kernel, in_specs=[hbm(), hbm()] + [vmem()] * 7, out_specs=...  5.01 us
    ppermute x4, waiting for transfers between devices, hop(): self.ahead = lax.ppermute(self.ahead, 'xy', self.hops[1])  4.78 us
    ppermute x4, starting transfers between devices, hop(): self.ahead = lax.ppermute(self.ahead, 'xy', self.hops[1])  4.48 us
    pallas_call x1, Pallas kernels, back_to_field(): pl.pallas_call(kernel, in_specs=[hbm()] + [vmem()] * 3, out_specs=hbm(),...  3.67 us
  transfers between devices with their start and end apart: 19, of which 7 were waited for; matrix products, arithmetic and copies ran while one was open for 0% of the time, Pallas kernels for 15%

profile of v6, /device:TPU:1, one launch (start us, length us, event | category | flops | bytes accessed | tf_op | source)
XLA Modules:
  0.0 84.1 jit_solution(13803935669392539639)
XLA Ops:
  0.6 0.0 copy-start.1
  0.6 0.0 copy-start
  0.7 2.8 %rows_to_modes.1 = bf16[128,768]{1,0:T(8,128)(2,1)} custom-call(bf16[4,512,512]{2,1,0:T(8,128)(2,1)} %u_hbm.7, bf16[48,512]{1,0:T(8,128)(2,1)} %constant.16.clone.t_hbm), custom_call_target="tpu_custom_call" | custom-call | flops 100663296 | bytes 2097152 | tf_op jit(solution)/shard_map/rows_to_modes/pallas_call | solution.py:296
  3.4 7.4 %all-to-all-start = ((bf16[16,8,768]{2,1,0:T(8,128)(2,1)}), bf16[16,8,768]{2,1,0:T(8,128)(2,1)S(1)}, u32[]{:S(2)}, u32[]{:S(2)}) async-start(bf16[16,8,768]{2,1,0:T(8,128)(2,1)} %bitcast.17), calls=%async_computation | async-start | bytes 393216 | tf_op jit(solution)/shard_map/all_to_all | solution.py:900
  10.8 0.0 copy-done.1
  10.8 0.0 copy-done
  10.8 2.7 %prepare.1 = (bf16[8,96,512]{2,1,0:T(8,128)(2,1)S(1)}, bf16[8,96,512]{2,1,0:T(8,128)(2,1)S(1)}, bf16[256,256]{1,0:T(8,128)(2,1)S(1)}, bf16[256,256]{1,0:T(8,128)...) custom-call(s32[1]{0:T(128)} %bitcast.2.me_ref, ...), custom_call_target="tpu_custom_call" | custom-call | flops 1000000 | bytes 4194304 | tf_op jit(solution)/shard_map/prepare/pallas_call | solution.py:378
  13.5 5.6 %all-to-all-done = bf16[16,8,768]{2,1,0:T(8,128)(2,1)S(1)} async-done(((bf16[16,8,768]{2,1,0:T(8,128)(2,1)}), bf16[16,8,768]{2,1,0:T(8,128)(2,1)S(1)}, u32[]{:S(2)}, u32[]{:S(2)}) %all-to-all-start) | async-done | bytes 196640 | tf_op jit(solution)/shard_map/all_to_all | solution.py:900
  19.1 1.3 %mode_step.1 = (bf16[48,768]{1,0:T(8,128)(2,1)S(1)}, bf16[128,768]{1,0:T(8,128)(2,1)S(1)}, bf16[512,512]{1,0:T(8,128)(2,1)S(1)}, bf16[512,512]{1,0:T(8,128)(2,1)S(1)}) custom-call(bf16[128,768]{1,0:T(8,128)(2,1)S(1)} %bitcast.12, bf16[8,96,512]{2,1,0:T(8,128)(2,1)S(1)} %get-tuple-element.47.w_ref, bf16[48,128]{1,0:T(8,128)(2,1)S(1)} %get-tuple-element.48.f_ref, ...), custom_call_target="tpu_custom_call" | custom-call | flops 301989888 | bytes 1572864 | tf_op jit(solution)/shard_map/mode_step/pallas_call | solution.py:438
  20.4 11.2 %all_to_all.46 = bf16[16,8,768]{2,1,0:T(8,128)(2,1)S(1)} all-to-all(bf16[16,8,768]{2,1,0:T(8,128)(2,1)S(1)} %bitcast.15), channel_id=1, replica_groups=mesh['groups'=2,'xy'=16] {'xy'}, dimensions={0} | all-to-all | bytes 393216 | tf_op jit(solution)/shard_map/all_to_all | solution.py:900
  31.6 5.0 %pointwise.1 = (bf16[4,512,512]{2,1,0:T(8,128)(2,1)}, bf16[4,512,512]{2,1,0:T(8,128)(2,1)}, bf16[128,768]{1,0:T(8,128)(2,1)}) custom-call(bf16[4,512,512]{2,1,0:T(8,128)(2,1)} %u_hbm.7, bf16[4,512,512]{2,1,0:T(8,128)(2,1)} %c_hbm.3, bf16[512,512]{1,0:T(8,128)(2,1)S(1)} %get-tuple-element.50.u_first, bf16[512,512]{1,0:T(8,128)(2,1)S(1)} %get-tuple-element.51.c_first, ...), custom_call_target="tpu_custom_call" | custom-call | flops 1048576000 | bytes 8388608 | tf_op jit(solution)/shard_map/pointwise/pallas_call | solution.py:546
  36.6 4.5 %all-to-all-start.2 = ((bf16[16,8,768]{2,1,0:T(8,128)(2,1)}), bf16[16,8,768]{2,1,0:T(8,128)(2,1)S(1)}, u32[]{:S(2)}, u32[]{:S(2)}) async-start(bf16[16,8,768]{2,1,0:T(8,128)(2,1)} %bitcast.19), calls=%async_computation.2 | async-start | bytes 393216 | tf_op jit(solution)/shard_map/all_to_all | solution.py:900
  41.1 3.5 %local_sums.1.st_ref = bf16[24,128]{1,0:T(8,128)(2,1)S(1)} custom-call(bf16[4,512,512]{2,1,0:T(8,128)(2,1)} %u_hbm.7, bf16[4,512,512]{2,1,0:T(8,128)(2,1)} %get-tuple-element.60.d_hbm), custom_call_target="tpu_custom_call" | custom-call | flops 1048576000 | bytes 4194304 | tf_op jit(solution)/shard_map/local_sums/pallas_call | solution.py:617
  44.7 4.5 %all-to-all-done.2 = bf16[16,8,768]{2,1,0:T(8,128)(2,1)S(1)} async-done(((bf16[16,8,768]{2,1,0:T(8,128)(2,1)}), bf16[16,8,768]{2,1,0:T(8,128)(2,1)S(1)}, u32[]{:S(2)}, u32[]{:S(2)}) %all-to-all-start.2) | async-done | bytes 196640 | tf_op jit(solution)/shard_map/all_to_all | solution.py:900
  49.1 1.1 %weight_sums.1 = (bf16[48,768]{1,0:T(8,128)(2,1)S(1)}, bf16[24,2048]{1,0:T(8,128)(2,1)S(1)}, f32[24,2048]{1,0:T(8,128)S(1)}) custom-call(bf16[48,768]{1,0:T(8,128)(2,1)S(1)} %get-tuple-element.58.u_ref, bf16[128,768]{1,0:T(8,128)(2,1)S(1)} %bitcast.14, bf16[48,128]{1,0:T(8,128)(2,1)S(1)} %get-tuple-element.48.f_ref), custom_call_target="tpu_custom_call" | custom-call | flops 301989888 | bytes 4194304 | tf_op jit(solution)/shard_map/weight_sums/pallas_call | solution.py:673
  50.2 1.2 %collective-permute-start = (f32[24,2048]{1,0:T(8,128)S(1)}, f32[24,2048]{1,0:T(8,128)S(1)}, u32[]{:S(2)}, u32[]{:S(2)}) collective-permute-start(f32[24,2048]{1,0:T(8,128)S(1)} %get-tuple-element.63.s_ref), channel_id=1, source_target_pairs={{0,1},{1,0},{2,3},{3,2},{4,5},{5,4},{6,7},{7,6},{8,9},{9,8},{10,11... | collective-permute-start | bytes 589832 | tf_op jit(solution)/shard_map/ppermute | solution.py:981
  51.5 1.1 %collective-permute-done.r_ref = f32[24,2048]{1,0:T(8,128)S(1)} collective-permute-done((f32[24,2048]{1,0:T(8,128)S(1)}, f32[24,2048]{1,0:T(8,128)S(1)}, u32[]{:S(2)}, u32[]{:S(2)}) %collective-permute-start) | collective-permute-done | bytes 196640 | tf_op jit(solution)/shard_map/ppermute | solution.py:981
  52.6 0.1 collective-permute-start.1
  52.6 1.5 %collective-permute-start.2 = (bf16[24,3200]{1,0:T(8,128)(2,1)S(1)}, bf16[24,3200]{1,0:T(8,128)(2,1)S(1)}, u32[]{:S(2)}, u32[]{:S(2)}) collective-permute-start(bf16[24,3200]{1,0:T(8,128)(2,1)S(1)} %make_shard.1.refs_0_), channel_id=1, source_target_pairs={{0,2},{1,3},{4,0},{5,1},{8,4},{9,5},{12,8},{13,9},{14,12},{15,13},... | collective-permute-start | bytes 460808 | tf_op jit(solution)/shard_map/ppermute | solution.py:927
  54.1 0.9 %collective-permute-start.5 = (bf16[24,3200]{1,0:T(8,128)(2,1)S(1)}, bf16[24,3200]{1,0:T(8,128)(2,1)S(1)}, u32[]{:S(2)}, u32[]{:S(2)}) collective-permute-start(bf16[24,3200]{1,0:T(8,128)(2,1)S(1)} %make_shard.1.refs_0_), channel_id=1, source_target_pairs={{0,1},{1,0},{2,3},{3,2},{4,5},{5,4},{6,7},{7,6},{8,9},{9,8},{10,11... | collective-permute-start | bytes 460808 | tf_op jit(solution)/shard_map/ppermute | solution.py:920
  55.0 1.8 %adjoint_step.1 = bf16[128,768]{1,0:T(8,128)(2,1)} custom-call(bf16[48,768]{1,0:T(8,128)(2,1)S(1)} %get-tuple-element.68.g_ref, bf16[8,96,512]{2,1,0:T(8,128)(2,1)S(1)} %get-tuple-element.69.w_ref, bf16[128,48]{1,0:T(8,128)(2,1)S(1)} %get-tuple-element.49.i_ref), custom_call_target="tpu_custom_call" | custom-call | flops 301989888 | bytes 1572864 | tf_op jit(solution)/shard_map/adjoint_step/pallas_call | solution.py:466
  56.8 1.0 %collective-permute-done.1.refs_2_ = bf16[24,3200]{1,0:T(8,128)(2,1)S(1)} collective-permute-done((bf16[24,3200]{1,0:T(8,128)(2,1)S(1)}, bf16[24,3200]{1,0:T(8,128)(2,1)S(1)}, u32[]{:S(2)}, u32[]{:S(2)}) %collective-permute-start.1) | collective-permute-done | bytes 153632 | tf_op jit(solution)/shard_map/ppermute | solution.py:925
  57.8 0.1 collective-permute-done.2.refs_4_
  57.9 1.2 %collective-permute-start.6 = (bf16[24,3200]{1,0:T(8,128)(2,1)S(1)}, bf16[24,3200]{1,0:T(8,128)(2,1)S(1)}, u32[]{:S(2)}, u32[]{:S(2)}) collective-permute-start(bf16[24,3200]{1,0:T(8,128)(2,1)S(1)} %collective-permute-done.1.refs_2_), channel_id=1, source_target_pairs={{0,1},{1,0},{2,3},{3,2},{4,5},{5,4},{6,7},{7,6},{8,9},{9,8},{10,11... | collective-permute-start | bytes 460808 | tf_op jit(solution)/shard_map/ppermute | solution.py:920
  59.1 0.0 collective-permute-start.7
  59.1 0.6 collective-permute-start.3
  59.7 0.9 %collective-permute-start.4 = (bf16[24,3200]{1,0:T(8,128)(2,1)S(1)}, bf16[24,3200]{1,0:T(8,128)(2,1)S(1)}, u32[]{:S(2)}, u32[]{:S(2)}) collective-permute-start(bf16[24,3200]{1,0:T(8,128)(2,1)S(1)} %collective-permute-done.2.refs_4_), channel_id=1, source_target_pairs={{0,2},{1,3},{4,0},{5,1},{8,4},{9,5},{12,8},{13,9},{14,12},{15,13},... | collective-permute-start | bytes 460808 | tf_op jit(solution)/shard_map/ppermute | solution.py:927
  60.6 4.4 %all-to-all-start.3 = ((bf16[16,8,768]{2,1,0:T(8,128)(2,1)}), bf16[16,8,768]{2,1,0:T(8,128)(2,1)S(1)}, u32[]{:S(2)}, u32[]{:S(2)}) async-start(bf16[16,8,768]{2,1,0:T(8,128)(2,1)} %bitcast.18), calls=%async_computation.3 | async-start | bytes 393216 | tf_op jit(solution)/shard_map/all_to_all | solution.py:900
  64.9 0.0 collective-permute-done.5.refs_1_
  64.9 0.0 collective-permute-done.6.refs_3_
  65.0 0.0 collective-permute-done.7.refs_5_
  65.0 0.0 collective-permute-done.3.refs_6_
  65.0 0.0 collective-permute-done.4.refs_8_
  65.0 1.5 %collective-permute-start.8 = (bf16[24,3200]{1,0:T(8,128)(2,1)S(1)}, bf16[24,3200]{1,0:T(8,128)(2,1)S(1)}, u32[]{:S(2)}, u32[]{:S(2)}) collective-permute-start(bf16[24,3200]{1,0:T(8,128)(2,1)S(1)} %collective-permute-done.3.refs_6_), channel_id=1, source_target_pairs={{0,4},{1,5},{4,8},{5,9},{8,12},{9,13},{12,14},{13,15},{14,10},{15,... | collective-permute-start | bytes 460808 | tf_op jit(solution)/shard_map/ppermute | solution.py:925
  66.5 0.1 collective-permute-start.13
  66.5 1.6 %collective-permute-start.10 = (bf16[24,3200]{1,0:T(8,128)(2,1)S(1)}, bf16[24,3200]{1,0:T(8,128)(2,1)S(1)}, u32[]{:S(2)}, u32[]{:S(2)}) collective-permute-start(bf16[24,3200]{1,0:T(8,128)(2,1)S(1)} %collective-permute-done.3.refs_6_), channel_id=1, source_target_pairs={{0,1},{1,0},{2,3},{3,2},{4,5},{5,4},{6,7},{7,6},{8,9},{9,8},{10,11... | collective-permute-start | bytes 460808 | tf_op jit(solution)/shard_map/ppermute | solution.py:920
  68.1 0.0 collective-permute-start.11
  68.1 3.8 %collective-permute-done.8.refs_0_ = bf16[24,3200]{1,0:T(8,128)(2,1)S(1)} collective-permute-done((bf16[24,3200]{1,0:T(8,128)(2,1)S(1)}, bf16[24,3200]{1,0:T(8,128)(2,1)S(1)}, u32[]{:S(2)}, u32[]{:S(2)}) %collective-permute-start.8) | collective-permute-done | bytes 153632 | tf_op jit(solution)/shard_map/ppermute | solution.py:925
  71.9 2.4 %collective-permute-start.9 = (bf16[24,3200]{1,0:T(8,128)(2,1)S(1)}, bf16[24,3200]{1,0:T(8,128)(2,1)S(1)}, u32[]{:S(2)}, u32[]{:S(2)}) collective-permute-start(bf16[24,3200]{1,0:T(8,128)(2,1)S(1)} %collective-permute-done.8.refs_0_), channel_id=1, source_target_pairs={{0,4},{1,5},{4,8},{5,9},{8,12},{9,13},{12,14},{13,15},{14,10},{15,... | collective-permute-start | bytes 460808 | tf_op jit(solution)/shard_map/ppermute | solution.py:925
  74.3 1.0 %collective-permute-start.12 = (bf16[24,3200]{1,0:T(8,128)(2,1)S(1)}, bf16[24,3200]{1,0:T(8,128)(2,1)S(1)}, u32[]{:S(2)}, u32[]{:S(2)}) collective-permute-start(bf16[24,3200]{1,0:T(8,128)(2,1)S(1)} %collective-permute-done.8.refs_0_), channel_id=1, source_target_pairs={{0,1},{1,0},{2,3},{3,2},{4,5},{5,4},{6,7},{7,6},{8,9},{9,8},{10,11... | collective-permute-start | bytes 460808 | tf_op jit(solution)/shard_map/ppermute | solution.py:920
  75.2 0.0 collective-permute-done.13.refs_2_
  75.2 0.0 collective-permute-start.14
  75.2 0.0 all-to-all-done.3
  75.2 3.7 %back_to_field.1 = bf16[4,512,512]{2,1,0:T(8,128)(2,1)} custom-call(bf16[4,512,512]{2,1,0:T(8,128)(2,1)} %get-tuple-element.60.d_hbm, bf16[128,768]{1,0:T(8,128)(2,1)S(1)} %bitcast.11, bf16[512,48]{1,0:T(8,128)(2,1)S(1)} %get-tuple-element.75.tt_ref, bf16[256,256]{1,0:T(8,128)(2,1)S(1)} %get-tuple-element.76.w_ref), custom_call_target="tpu_custom_call" | custom-call | flops 524288000 | bytes 4194304 | tf_op jit(solution)/shard_map/back_to_field/pallas_call | solution.py:881
  78.9 0.0 collective-permute-done.10.refs_7_
  78.9 0.0 collective-permute-done.11.refs_9_
  78.9 0.8 assemble_first.1
  79.7 0.0 collective-permute-done.9.refs_4_
  79.7 0.6 collective-permute-start.15
  80.3 0.0 collective-permute-done.12.refs_1_
  80.3 0.0 collective-permute-done.14.refs_3_
  80.3 1.0 %collective-permute-done.15.refs_5_ = bf16[24,3200]{1,0:T(8,128)(2,1)S(1)} collective-permute-done((bf16[24,3200]{1,0:T(8,128)(2,1)S(1)}, bf16[24,3200]{1,0:T(8,128)(2,1)S(1)}, u32[]{:S(2)}, u32[]{:S(2)}) %collective-permute-start.15) | collective-permute-done | bytes 153632 | tf_op jit(solution)/shard_map/ppermute | solution.py:920
  81.3 2.6 %assemble.1 = (f32[16,600,128]{2,1,0:T(8,128)S(1)}, bf16[24,24,2048]{2,1,0:T(8,128)(2,1)}, f32[32,32]{1,0:T(8,128)}, f32[1,32]{1,0:T(1,128)}) custom-call(s32[1]{0:T(128)} %bitcast.2.me_ref, f32[16,600,128]{2,1,0:T(8,128)S(1)} %get-tuple-element.81.scr_in, f32[6,16,128]{2,1,0:T(8,128)S(1)} %early_sums.1.e_ref, ...), custom_call_target="tpu_custom_call", output_to_operand_aliasing={{0}: (1, {})} | custom-call | flops 1000000 | bytes 8388608 | tf_op jit(solution)/shard_map/assemble/pallas_call | solution.py:836
  (2 shorter events, 0.1 us)
Async XLA Ops:
  0.6 10.2 %copy-start.1 = (f32[32]{0:T(128)S(1)}, f32[32]{0:T(128)}, u32[]{:S(2)}) copy-start(f32[32]{0:T(128)} %param.14) | copy-start | bytes 388
  0.6 10.2 %copy-start = (bf16[32,32]{1,0:T(8,128)(2,1)S(1)}, bf16[32,32]{1,0:T(8,128)(2,1)}, u32[]{:S(2)}) copy-start(bf16[32,32]{1,0:T(8,128)(2,1)} %l_ref.1) | copy-start | bytes 6148
  3.4 15.7 %all-to-all-start = ((bf16[16,8,768]{2,1,0:T(8,128)(2,1)}), bf16[16,8,768]{2,1,0:T(8,128)(2,1)S(1)}, u32[]{:S(2)}, u32[]{:S(2)}) async-start(bf16[16,8,768]{2,1,0:T(8,128)(2,1)} %bitcast.17), calls=%async_computation | async-start | bytes 393216 | tf_op jit(solution)/shard_map/all_to_all | solution.py:900
  36.6 12.5 %all-to-all-start.2 = ((bf16[16,8,768]{2,1,0:T(8,128)(2,1)}), bf16[16,8,768]{2,1,0:T(8,128)(2,1)S(1)}, u32[]{:S(2)}, u32[]{:S(2)}) async-start(bf16[16,8,768]{2,1,0:T(8,128)(2,1)} %bitcast.19), calls=%async_computation.2 | async-start | bytes 393216 | tf_op jit(solution)/shard_map/all_to_all | solution.py:900
  50.2 2.3 %collective-permute-start = (f32[24,2048]{1,0:T(8,128)S(1)}, f32[24,2048]{1,0:T(8,128)S(1)}, u32[]{:S(2)}, u32[]{:S(2)}) collective-permute-start(f32[24,2048]{1,0:T(8,128)S(1)} %get-tuple-element.63.s_ref), channel_id=1, source_target_pairs={{0,1},{1,0},{2,3},{3,2},{4,5},{5,4},{6,7},{7,6},{8,9},{9,8},{10,11... | collective-permute-start | bytes 589832 | tf_op jit(solution)/shard_map/ppermute | solution.py:981
  52.6 5.2 %collective-permute-start.1 = (bf16[24,3200]{1,0:T(8,128)(2,1)S(1)}, bf16[24,3200]{1,0:T(8,128)(2,1)S(1)}, u32[]{:S(2)}, u32[]{:S(2)}) collective-permute-start(bf16[24,3200]{1,0:T(8,128)(2,1)S(1)} %make_shard.1.refs_0_), channel_id=1, source_target_pairs={{0,4},{1,5},{4,8},{5,9},{8,12},{9,13},{12,14},{13,15},{14,10},{15,... | collective-permute-start | bytes 460808 | tf_op jit(solution)/shard_map/ppermute | solution.py:925
  52.6 5.2 %collective-permute-start.2 = (bf16[24,3200]{1,0:T(8,128)(2,1)S(1)}, bf16[24,3200]{1,0:T(8,128)(2,1)S(1)}, u32[]{:S(2)}, u32[]{:S(2)}) collective-permute-start(bf16[24,3200]{1,0:T(8,128)(2,1)S(1)} %make_shard.1.refs_0_), channel_id=1, source_target_pairs={{0,2},{1,3},{4,0},{5,1},{8,4},{9,5},{12,8},{13,9},{14,12},{15,13},... | collective-permute-start | bytes 460808 | tf_op jit(solution)/shard_map/ppermute | solution.py:927
  54.1 10.8 %collective-permute-start.5 = (bf16[24,3200]{1,0:T(8,128)(2,1)S(1)}, bf16[24,3200]{1,0:T(8,128)(2,1)S(1)}, u32[]{:S(2)}, u32[]{:S(2)}) collective-permute-start(bf16[24,3200]{1,0:T(8,128)(2,1)S(1)} %make_shard.1.refs_0_), channel_id=1, source_target_pairs={{0,1},{1,0},{2,3},{3,2},{4,5},{5,4},{6,7},{7,6},{8,9},{9,8},{10,11... | collective-permute-start | bytes 460808 | tf_op jit(solution)/shard_map/ppermute | solution.py:920
  57.9 7.1 %collective-permute-start.6 = (bf16[24,3200]{1,0:T(8,128)(2,1)S(1)}, bf16[24,3200]{1,0:T(8,128)(2,1)S(1)}, u32[]{:S(2)}, u32[]{:S(2)}) collective-permute-start(bf16[24,3200]{1,0:T(8,128)(2,1)S(1)} %collective-permute-done.1.refs_2_), channel_id=1, source_target_pairs={{0,1},{1,0},{2,3},{3,2},{4,5},{5,4},{6,7},{7,6},{8,9},{9,8},{10,11... | collective-permute-start | bytes 460808 | tf_op jit(solution)/shard_map/ppermute | solution.py:920
  59.1 5.9 %collective-permute-start.7 = (bf16[24,3200]{1,0:T(8,128)(2,1)S(1)}, bf16[24,3200]{1,0:T(8,128)(2,1)S(1)}, u32[]{:S(2)}, u32[]{:S(2)}) collective-permute-start(bf16[24,3200]{1,0:T(8,128)(2,1)S(1)} %collective-permute-done.2.refs_4_), channel_id=1, source_target_pairs={{0,1},{1,0},{2,3},{3,2},{4,5},{5,4},{6,7},{7,6},{8,9},{9,8},{10,11... | collective-permute-start | bytes 460808 | tf_op jit(solution)/shard_map/ppermute | solution.py:920
  59.1 5.9 %collective-permute-start.3 = (bf16[24,3200]{1,0:T(8,128)(2,1)S(1)}, bf16[24,3200]{1,0:T(8,128)(2,1)S(1)}, u32[]{:S(2)}, u32[]{:S(2)}) collective-permute-start(bf16[24,3200]{1,0:T(8,128)(2,1)S(1)} %collective-permute-done.1.refs_2_), channel_id=1, source_target_pairs={{0,4},{1,5},{4,8},{5,9},{8,12},{9,13},{12,14},{13,15},{14,10},{15,... | collective-permute-start | bytes 460808 | tf_op jit(solution)/shard_map/ppermute | solution.py:925
  59.7 5.3 %collective-permute-start.4 = (bf16[24,3200]{1,0:T(8,128)(2,1)S(1)}, bf16[24,3200]{1,0:T(8,128)(2,1)S(1)}, u32[]{:S(2)}, u32[]{:S(2)}) collective-permute-start(bf16[24,3200]{1,0:T(8,128)(2,1)S(1)} %collective-permute-done.2.refs_4_), channel_id=1, source_target_pairs={{0,2},{1,3},{4,0},{5,1},{8,4},{9,5},{12,8},{13,9},{14,12},{15,13},... | collective-permute-start | bytes 460808 | tf_op jit(solution)/shard_map/ppermute | solution.py:927
  60.6 14.7 %all-to-all-start.3 = ((bf16[16,8,768]{2,1,0:T(8,128)(2,1)}), bf16[16,8,768]{2,1,0:T(8,128)(2,1)S(1)}, u32[]{:S(2)}, u32[]{:S(2)}) async-start(bf16[16,8,768]{2,1,0:T(8,128)(2,1)} %bitcast.18), calls=%async_computation.3 | async-start | bytes 393216 | tf_op jit(solution)/shard_map/all_to_all | solution.py:900
  65.0 6.9 %collective-permute-start.8 = (bf16[24,3200]{1,0:T(8,128)(2,1)S(1)}, bf16[24,3200]{1,0:T(8,128)(2,1)S(1)}, u32[]{:S(2)}, u32[]{:S(2)}) collective-permute-start(bf16[24,3200]{1,0:T(8,128)(2,1)S(1)} %collective-permute-done.3.refs_6_), channel_id=1, source_target_pairs={{0,4},{1,5},{4,8},{5,9},{8,12},{9,13},{12,14},{13,15},{14,10},{15,... | collective-permute-start | bytes 460808 | tf_op jit(solution)/shard_map/ppermute | solution.py:925
  66.5 8.8 %collective-permute-start.13 = (bf16[24,3200]{1,0:T(8,128)(2,1)S(1)}, bf16[24,3200]{1,0:T(8,128)(2,1)S(1)}, u32[]{:S(2)}, u32[]{:S(2)}) collective-permute-start(bf16[24,3200]{1,0:T(8,128)(2,1)S(1)} %collective-permute-done.4.refs_8_), channel_id=1, source_target_pairs={{0,2},{1,3},{4,0},{5,1},{8,4},{9,5},{12,8},{13,9},{14,12},{15,13},... | collective-permute-start | bytes 460808 | tf_op jit(solution)/shard_map/ppermute | solution.py:927
  66.5 12.4 %collective-permute-start.10 = (bf16[24,3200]{1,0:T(8,128)(2,1)S(1)}, bf16[24,3200]{1,0:T(8,128)(2,1)S(1)}, u32[]{:S(2)}, u32[]{:S(2)}) collective-permute-start(bf16[24,3200]{1,0:T(8,128)(2,1)S(1)} %collective-permute-done.3.refs_6_), channel_id=1, source_target_pairs={{0,1},{1,0},{2,3},{3,2},{4,5},{5,4},{6,7},{7,6},{8,9},{9,8},{10,11... | collective-permute-start | bytes 460808 | tf_op jit(solution)/shard_map/ppermute | solution.py:920
  68.1 10.8 %collective-permute-start.11 = (bf16[24,3200]{1,0:T(8,128)(2,1)S(1)}, bf16[24,3200]{1,0:T(8,128)(2,1)S(1)}, u32[]{:S(2)}, u32[]{:S(2)}) collective-permute-start(bf16[24,3200]{1,0:T(8,128)(2,1)S(1)} %collective-permute-done.4.refs_8_), channel_id=1, source_target_pairs={{0,1},{1,0},{2,3},{3,2},{4,5},{5,4},{6,7},{7,6},{8,9},{9,8},{10,11... | collective-permute-start | bytes 460808 | tf_op jit(solution)/shard_map/ppermute | solution.py:920
  71.9 7.8 %collective-permute-start.9 = (bf16[24,3200]{1,0:T(8,128)(2,1)S(1)}, bf16[24,3200]{1,0:T(8,128)(2,1)S(1)}, u32[]{:S(2)}, u32[]{:S(2)}) collective-permute-start(bf16[24,3200]{1,0:T(8,128)(2,1)S(1)} %collective-permute-done.8.refs_0_), channel_id=1, source_target_pairs={{0,4},{1,5},{4,8},{5,9},{8,12},{9,13},{12,14},{13,15},{14,10},{15,... | collective-permute-start | bytes 460808 | tf_op jit(solution)/shard_map/ppermute | solution.py:925
  74.3 6.0 %collective-permute-start.12 = (bf16[24,3200]{1,0:T(8,128)(2,1)S(1)}, bf16[24,3200]{1,0:T(8,128)(2,1)S(1)}, u32[]{:S(2)}, u32[]{:S(2)}) collective-permute-start(bf16[24,3200]{1,0:T(8,128)(2,1)S(1)} %collective-permute-done.8.refs_0_), channel_id=1, source_target_pairs={{0,1},{1,0},{2,3},{3,2},{4,5},{5,4},{6,7},{7,6},{8,9},{9,8},{10,11... | collective-permute-start | bytes 460808 | tf_op jit(solution)/shard_map/ppermute | solution.py:920
  75.2 5.1 %collective-permute-start.14 = (bf16[24,3200]{1,0:T(8,128)(2,1)S(1)}, bf16[24,3200]{1,0:T(8,128)(2,1)S(1)}, u32[]{:S(2)}, u32[]{:S(2)}) collective-permute-start(bf16[24,3200]{1,0:T(8,128)(2,1)S(1)} %collective-permute-done.13.refs_2_), channel_id=1, source_target_pairs={{0,1},{1,0},{2,3},{3,2},{4,5},{5,4},{6,7},{7,6},{8,9},{9,8},{10,11... | collective-permute-start | bytes 460808 | tf_op jit(solution)/shard_map/ppermute | solution.py:920
  79.7 1.6 %collective-permute-start.15 = (bf16[24,3200]{1,0:T(8,128)(2,1)S(1)}, bf16[24,3200]{1,0:T(8,128)(2,1)S(1)}, u32[]{:S(2)}, u32[]{:S(2)}) collective-permute-start(bf16[24,3200]{1,0:T(8,128)(2,1)S(1)} %collective-permute-done.9.refs_4_), channel_id=1, source_target_pairs={{0,1},{1,0},{2,3},{3,2},{4,5},{5,4},{6,7},{7,6},{8,9},{9,8},{10,11... | collective-permute-start | bytes 460808 | tf_op jit(solution)/shard_map/ppermute | solution.py:920

commit v7 on v6

--- a/solution.py
+++ b/solution.py
@@ -985,7 +985,7 @@
     grads = ring.tie(grads)
     ring.hop()
     send = adjoint_step(grads, turned, inverse, chans)
-    send = ring.tie(send)
+    send = ring.hold(send)
     ring.settle()
     first = list(ring.parts)
     ring.hop()
@@ -993,7 +993,7 @@
     ring.settle()
     early, turns = list(ring.parts), list(ring.turns)
     sums = early_sums(first, chans)
-    sums = ring.tie(sums)
+    sums = ring.hold(sums)
     ring.hop()
     pencil, sums = lax.optimization_barrier((pencil, sums))
     ring.settle()

time: 84.9 us -> 88.8 us (1.046)
  waiting for transfers between devices: 17 us -> 22.4 us
  starting transfers between devices: 29.6 us -> 28.4 us
    ppermute x3, waiting for transfers between devices: 0.07 us -> 8.85 us  [hop(): self.back = lax.ppermute(self.back, 'xy', self.hops[-1])]
    ppermute x4, waiting for transfers between devices: 4.78 us -> 0.99 us  [hop(): self.ahead = lax.ppermute(self.ahead, 'xy', self.hops[1])]
    ppermute x4, starting transfers between devices: 4.48 us -> 3.23 us  [hop(): self.ahead = lax.ppermute(self.ahead, 'xy', self.hops[1])]
  transfers between devices with their start and end apart: 19 -> 19, of which waited for: 7 -> 7; matrix products, arithmetic and copies ran while one was open for 0% -> 0% of each run, Pallas kernels for 15% -> 14%
where the time goes in v7:
time: 88.8 us; the launch traced here: 88.2 us
  starting transfers between devices  28.4 us (32%)
  Pallas kernels  25.3 us (28%)
  waiting for transfers between devices  22.4 us (25%)
  blocking collectives  11.2 us (13%)
  between operations  0.98 us (1%)
    all_to_all x3, starting transfers between devices, exchange(): return lax.all_to_all(pencil, 'xy', split_axis=0, concat_axis=0, tiled=True)  15.7 us
    all_to_all x1, blocking collectives, exchange(): return lax.all_to_all(pencil, 'xy', split_axis=0, concat_axis=0, tiled=True)  11.2 us
    all_to_all x3, waiting for transfers between devices, exchange(): return lax.all_to_all(pencil, 'xy', split_axis=0, concat_axis=0, tiled=True)  10.1 us
    ppermute x3, waiting for transfers between devices, hop(): self.back = lax.ppermute(self.back, 'xy', self.hops[-1])  8.85 us
    ppermute x8, starting transfers between devices, keep(): self.parts.append(lax.ppermute(piece, 'xy', self.swap))  5.38 us
    pallas_call x1, Pallas kernels, pointwise(): pl.pallas_call(kernel, in_specs=[hbm(), hbm()] + [vmem()] * 7, out_specs=...  5.01 us
    pallas_call x1, Pallas kernels, back_to_field(): pl.pallas_call(kernel, in_specs=[hbm()] + [vmem()] * 3, out_specs=hbm(),...  3.67 us
    pallas_call x1, Pallas kernels, local_sums(): pl.pallas_call(kernel, in_specs=[hbm(), hbm()], out_specs=vmem(), out_sha...  3.52 us
  transfers between devices with their start and end apart: 19, of which 7 were waited for; matrix products, arithmetic and copies ran while one was open for 0% of the time, Pallas kernels for 14%

profile of v7, /device:TPU:1, one launch (start us, length us, event | category | flops | bytes accessed | tf_op | source)
XLA Modules:
  0.0 88.2 jit_solution(5558097181554838890)
XLA Ops:
  0.6 0.0 copy-start.1
  0.6 0.0 copy-start
  0.7 2.8 %rows_to_modes.1 = bf16[128,768]{1,0:T(8,128)(2,1)} custom-call(bf16[4,512,512]{2,1,0:T(8,128)(2,1)} %u_hbm.7, bf16[48,512]{1,0:T(8,128)(2,1)} %constant.16.clone.t_hbm), custom_call_target="tpu_custom_call" | custom-call | flops 100663296 | bytes 2097152 | tf_op jit(solution)/shard_map/rows_to_modes/pallas_call | solution.py:296
  3.4 7.4 %all-to-all-start = ((bf16[16,8,768]{2,1,0:T(8,128)(2,1)}), bf16[16,8,768]{2,1,0:T(8,128)(2,1)S(1)}, u32[]{:S(2)}, u32[]{:S(2)}) async-start(bf16[16,8,768]{2,1,0:T(8,128)(2,1)} %bitcast.17), calls=%async_computation | async-start | bytes 393216 | tf_op jit(solution)/shard_map/all_to_all | solution.py:900
  10.8 0.0 copy-done.1
  10.8 0.0 copy-done
  10.8 2.7 %prepare.1 = (bf16[8,96,512]{2,1,0:T(8,128)(2,1)S(1)}, bf16[8,96,512]{2,1,0:T(8,128)(2,1)S(1)}, bf16[256,256]{1,0:T(8,128)(2,1)S(1)}, bf16[256,256]{1,0:T(8,128)...) custom-call(s32[1]{0:T(128)} %bitcast.2.me_ref, ...), custom_call_target="tpu_custom_call" | custom-call | flops 1000000 | bytes 4194304 | tf_op jit(solution)/shard_map/prepare/pallas_call | solution.py:378
  13.5 5.6 %all-to-all-done = bf16[16,8,768]{2,1,0:T(8,128)(2,1)S(1)} async-done(((bf16[16,8,768]{2,1,0:T(8,128)(2,1)}), bf16[16,8,768]{2,1,0:T(8,128)(2,1)S(1)}, u32[]{:S(2)}, u32[]{:S(2)}) %all-to-all-start) | async-done | bytes 196640 | tf_op jit(solution)/shard_map/all_to_all | solution.py:900
  19.1 1.3 %mode_step.1 = (bf16[48,768]{1,0:T(8,128)(2,1)S(1)}, bf16[128,768]{1,0:T(8,128)(2,1)S(1)}, bf16[512,512]{1,0:T(8,128)(2,1)S(1)}, bf16[512,512]{1,0:T(8,128)(2,1)S(1)}) custom-call(bf16[128,768]{1,0:T(8,128)(2,1)S(1)} %bitcast.12, bf16[8,96,512]{2,1,0:T(8,128)(2,1)S(1)} %get-tuple-element.45.w_ref, bf16[48,128]{1,0:T(8,128)(2,1)S(1)} %get-tuple-element.46.f_ref, ...), custom_call_target="tpu_custom_call" | custom-call | flops 301989888 | bytes 1572864 | tf_op jit(solution)/shard_map/mode_step/pallas_call | solution.py:438
  20.4 11.2 %all_to_all.46 = bf16[16,8,768]{2,1,0:T(8,128)(2,1)S(1)} all-to-all(bf16[16,8,768]{2,1,0:T(8,128)(2,1)S(1)} %bitcast.15), channel_id=1, replica_groups=mesh['groups'=2,'xy'=16] {'xy'}, dimensions={0} | all-to-all | bytes 393216 | tf_op jit(solution)/shard_map/all_to_all | solution.py:900
  31.6 5.0 %pointwise.1 = (bf16[4,512,512]{2,1,0:T(8,128)(2,1)}, bf16[4,512,512]{2,1,0:T(8,128)(2,1)}, bf16[128,768]{1,0:T(8,128)(2,1)}) custom-call(bf16[4,512,512]{2,1,0:T(8,128)(2,1)} %u_hbm.7, bf16[4,512,512]{2,1,0:T(8,128)(2,1)} %c_hbm.3, bf16[512,512]{1,0:T(8,128)(2,1)S(1)} %get-tuple-element.48.u_first, bf16[512,512]{1,0:T(8,128)(2,1)S(1)} %get-tuple-element.49.c_first, ...), custom_call_target="tpu_custom_call" | custom-call | flops 1048576000 | bytes 8388608 | tf_op jit(solution)/shard_map/pointwise/pallas_call | solution.py:546
  36.6 4.5 %all-to-all-start.2 = ((bf16[16,8,768]{2,1,0:T(8,128)(2,1)}), bf16[16,8,768]{2,1,0:T(8,128)(2,1)S(1)}, u32[]{:S(2)}, u32[]{:S(2)}) async-start(bf16[16,8,768]{2,1,0:T(8,128)(2,1)} %bitcast.19), calls=%async_computation.2 | async-start | bytes 393216 | tf_op jit(solution)/shard_map/all_to_all | solution.py:900
  41.1 3.5 %local_sums.1.st_ref = bf16[24,128]{1,0:T(8,128)(2,1)S(1)} custom-call(bf16[4,512,512]{2,1,0:T(8,128)(2,1)} %u_hbm.7, bf16[4,512,512]{2,1,0:T(8,128)(2,1)} %get-tuple-element.58.d_hbm), custom_call_target="tpu_custom_call" | custom-call | flops 1048576000 | bytes 4194304 | tf_op jit(solution)/shard_map/local_sums/pallas_call | solution.py:617
  44.7 4.5 %all-to-all-done.2 = bf16[16,8,768]{2,1,0:T(8,128)(2,1)S(1)} async-done(((bf16[16,8,768]{2,1,0:T(8,128)(2,1)}), bf16[16,8,768]{2,1,0:T(8,128)(2,1)S(1)}, u32[]{:S(2)}, u32[]{:S(2)}) %all-to-all-start.2) | async-done | bytes 196640 | tf_op jit(solution)/shard_map/all_to_all | solution.py:900
  49.1 1.1 %weight_sums.1 = (bf16[48,768]{1,0:T(8,128)(2,1)S(1)}, bf16[24,2048]{1,0:T(8,128)(2,1)S(1)}, f32[24,2048]{1,0:T(8,128)S(1)}) custom-call(bf16[48,768]{1,0:T(8,128)(2,1)S(1)} %get-tuple-element.56.u_ref, bf16[128,768]{1,0:T(8,128)(2,1)S(1)} %bitcast.14, bf16[48,128]{1,0:T(8,128)(2,1)S(1)} %get-tuple-element.46.f_ref), custom_call_target="tpu_custom_call" | custom-call | flops 301989888 | bytes 4194304 | tf_op jit(solution)/shard_map/weight_sums/pallas_call | solution.py:673
  50.2 1.2 %collective-permute-start = (f32[24,2048]{1,0:T(8,128)S(1)}, f32[24,2048]{1,0:T(8,128)S(1)}, u32[]{:S(2)}, u32[]{:S(2)}) collective-permute-start(f32[24,2048]{1,0:T(8,128)S(1)} %get-tuple-element.61.s_ref), channel_id=1, source_target_pairs={{0,1},{1,0},{2,3},{3,2},{4,5},{5,4},{6,7},{7,6},{8,9},{9,8},{10,11... | collective-permute-start | bytes 589832 | tf_op jit(solution)/shard_map/ppermute | solution.py:981
  51.5 1.1 %collective-permute-done.r_ref = f32[24,2048]{1,0:T(8,128)S(1)} collective-permute-done((f32[24,2048]{1,0:T(8,128)S(1)}, f32[24,2048]{1,0:T(8,128)S(1)}, u32[]{:S(2)}, u32[]{:S(2)}) %collective-permute-start) | collective-permute-done | bytes 196640 | tf_op jit(solution)/shard_map/ppermute | solution.py:981
  52.6 0.1 collective-permute-start.1
  52.6 1.5 %collective-permute-start.5 = (bf16[24,3200]{1,0:T(8,128)(2,1)S(1)}, bf16[24,3200]{1,0:T(8,128)(2,1)S(1)}, u32[]{:S(2)}, u32[]{:S(2)}) collective-permute-start(bf16[24,3200]{1,0:T(8,128)(2,1)S(1)} %make_shard.1.refs_0_), channel_id=1, source_target_pairs={{0,2},{1,3},{4,0},{5,1},{8,4},{9,5},{12,8},{13,9},{14,12},{15,13},... | collective-permute-start | bytes 460808 | tf_op jit(solution)/shard_map/ppermute | solution.py:927
  54.1 0.9 %collective-permute-start.3 = (bf16[24,3200]{1,0:T(8,128)(2,1)S(1)}, bf16[24,3200]{1,0:T(8,128)(2,1)S(1)}, u32[]{:S(2)}, u32[]{:S(2)}) collective-permute-start(bf16[24,3200]{1,0:T(8,128)(2,1)S(1)} %make_shard.1.refs_0_), channel_id=1, source_target_pairs={{0,1},{1,0},{2,3},{3,2},{4,5},{5,4},{6,7},{7,6},{8,9},{9,8},{10,11... | collective-permute-start | bytes 460808 | tf_op jit(solution)/shard_map/ppermute | solution.py:920
  55.0 1.8 %adjoint_step.1 = bf16[128,768]{1,0:T(8,128)(2,1)} custom-call(bf16[48,768]{1,0:T(8,128)(2,1)S(1)} %get-tuple-element.65.g_ref, bf16[8,96,512]{2,1,0:T(8,128)(2,1)S(1)} %get-tuple-element.66.w_ref, bf16[128,48]{1,0:T(8,128)(2,1)S(1)} %get-tuple-element.47.i_ref), custom_call_target="tpu_custom_call" | custom-call | flops 301989888 | bytes 1572864 | tf_op jit(solution)/shard_map/adjoint_step/pallas_call | solution.py:466
  56.8 1.0 %collective-permute-done.1.refs_2_ = bf16[24,3200]{1,0:T(8,128)(2,1)S(1)} collective-permute-done((bf16[24,3200]{1,0:T(8,128)(2,1)S(1)}, bf16[24,3200]{1,0:T(8,128)(2,1)S(1)}, u32[]{:S(2)}, u32[]{:S(2)}) %collective-permute-start.1) | collective-permute-done | bytes 153632 | tf_op jit(solution)/shard_map/ppermute | solution.py:925
  57.8 1.2 %collective-permute-start.4 = (bf16[24,3200]{1,0:T(8,128)(2,1)S(1)}, bf16[24,3200]{1,0:T(8,128)(2,1)S(1)}, u32[]{:S(2)}, u32[]{:S(2)}) collective-permute-start(bf16[24,3200]{1,0:T(8,128)(2,1)S(1)} %collective-permute-done.1.refs_2_), channel_id=1, source_target_pairs={{0,1},{1,0},{2,3},{3,2},{4,5},{5,4},{6,7},{7,6},{8,9},{9,8},{10,11... | collective-permute-start | bytes 460808 | tf_op jit(solution)/shard_map/ppermute | solution.py:920
  59.0 0.0 collective-permute-done.5.refs_4_
  59.0 0.1 collective-permute-start.6
  59.1 0.6 collective-permute-start.2
  59.7 3.8 %all-to-all-start.3 = ((bf16[16,8,768]{2,1,0:T(8,128)(2,1)}), bf16[16,8,768]{2,1,0:T(8,128)(2,1)S(1)}, u32[]{:S(2)}, u32[]{:S(2)}) async-start(bf16[16,8,768]{2,1,0:T(8,128)(2,1)} %bitcast.18), calls=%async_computation.3 | async-start | bytes 393216 | tf_op jit(solution)/shard_map/all_to_all | solution.py:900
  63.5 1.4 %collective-permute-start.10 = (bf16[24,3200]{1,0:T(8,128)(2,1)S(1)}, bf16[24,3200]{1,0:T(8,128)(2,1)S(1)}, u32[]{:S(2)}, u32[]{:S(2)}) collective-permute-start(bf16[24,3200]{1,0:T(8,128)(2,1)S(1)} %collective-permute-done.5.refs_4_), channel_id=1, source_target_pairs={{0,2},{1,3},{4,0},{5,1},{8,4},{9,5},{12,8},{13,9},{14,12},{15,13},... | collective-permute-start | bytes 460808 | tf_op jit(solution)/shard_map/ppermute | solution.py:927
  64.9 0.0 collective-permute-done.3.refs_1_
  64.9 0.0 collective-permute-done.4.refs_3_
  64.9 0.0 collective-permute-done.6.refs_5_
  64.9 0.0 collective-permute-done.2.refs_6_
  64.9 0.3 collective-permute-start.7
  65.3 7.0 %collective-permute-done.10.refs_8_ = bf16[24,3200]{1,0:T(8,128)(2,1)S(1)} collective-permute-done((bf16[24,3200]{1,0:T(8,128)(2,1)S(1)}, bf16[24,3200]{1,0:T(8,128)(2,1)S(1)}, u32[]{:S(2)}, u32[]{:S(2)}) %collective-permute-start.10) | collective-permute-done | bytes 153632 | tf_op jit(solution)/shard_map/ppermute | solution.py:927
  72.3 0.0 collective-permute-start.13
  72.3 0.9 collective-permute-start.9
  73.2 0.0 collective-permute-start.11
  73.2 0.0 collective-permute-done.7.refs_0_
  73.2 2.2 %collective-permute-start.8 = (bf16[24,3200]{1,0:T(8,128)(2,1)S(1)}, bf16[24,3200]{1,0:T(8,128)(2,1)S(1)}, u32[]{:S(2)}, u32[]{:S(2)}) collective-permute-start(bf16[24,3200]{1,0:T(8,128)(2,1)S(1)} %collective-permute-done.7.refs_0_), channel_id=1, source_target_pairs={{0,4},{1,5},{4,8},{5,9},{8,12},{9,13},{12,14},{13,15},{14,10},{15,... | collective-permute-start | bytes 460808 | tf_op jit(solution)/shard_map/ppermute | solution.py:925
  75.4 0.8 collective-permute-start.12
  76.2 1.8 %collective-permute-done.13.refs_2_ = bf16[24,3200]{1,0:T(8,128)(2,1)S(1)} collective-permute-done((bf16[24,3200]{1,0:T(8,128)(2,1)S(1)}, bf16[24,3200]{1,0:T(8,128)(2,1)S(1)}, u32[]{:S(2)}, u32[]{:S(2)}) %collective-permute-start.13) | collective-permute-done | bytes 153632 | tf_op jit(solution)/shard_map/ppermute | solution.py:927
  78.0 1.5 %collective-permute-start.14 = (bf16[24,3200]{1,0:T(8,128)(2,1)S(1)}, bf16[24,3200]{1,0:T(8,128)(2,1)S(1)}, u32[]{:S(2)}, u32[]{:S(2)}) collective-permute-start(bf16[24,3200]{1,0:T(8,128)(2,1)S(1)} %collective-permute-done.13.refs_2_), channel_id=1, source_target_pairs={{0,1},{1,0},{2,3},{3,2},{4,5},{5,4},{6,7},{7,6},{8,9},{9,8},{10,11... | collective-permute-start | bytes 460808 | tf_op jit(solution)/shard_map/ppermute | solution.py:920
  79.5 0.0 all-to-all-done.3
  79.5 3.7 %back_to_field.1 = bf16[4,512,512]{2,1,0:T(8,128)(2,1)} custom-call(bf16[4,512,512]{2,1,0:T(8,128)(2,1)} %get-tuple-element.58.d_hbm, bf16[128,768]{1,0:T(8,128)(2,1)S(1)} %bitcast.11, bf16[512,48]{1,0:T(8,128)(2,1)S(1)} %get-tuple-element.72.tt_ref, bf16[256,256]{1,0:T(8,128)(2,1)S(1)} %get-tuple-element.73.w_ref), custom_call_target="tpu_custom_call" | custom-call | flops 524288000 | bytes 4194304 | tf_op jit(solution)/shard_map/back_to_field/pallas_call | solution.py:881
  83.2 0.0 collective-permute-done.9.refs_7_
  83.2 0.0 collective-permute-done.11.refs_9_
  83.2 0.8 assemble_first.1
  84.0 0.0 collective-permute-done.8.refs_4_
  84.0 0.1 collective-permute-start.15
  84.1 0.0 collective-permute-done.14.refs_3_
  84.1 0.0 collective-permute-done.12.refs_1_
  84.1 1.3 %collective-permute-done.15.refs_5_ = bf16[24,3200]{1,0:T(8,128)(2,1)S(1)} collective-permute-done((bf16[24,3200]{1,0:T(8,128)(2,1)S(1)}, bf16[24,3200]{1,0:T(8,128)(2,1)S(1)}, u32[]{:S(2)}, u32[]{:S(2)}) %collective-permute-start.15) | collective-permute-done | bytes 153632 | tf_op jit(solution)/shard_map/ppermute | solution.py:920
  85.4 2.6 %assemble.1 = (f32[16,600,128]{2,1,0:T(8,128)S(1)}, bf16[24,24,2048]{2,1,0:T(8,128)(2,1)}, f32[32,32]{1,0:T(8,128)}, f32[1,32]{1,0:T(1,128)}) custom-call(s32[1]{0:T(128)} %bitcast.2.me_ref, f32[16,600,128]{2,1,0:T(8,128)S(1)} %get-tuple-element.78.scr_in, f32[6,16,128]{2,1,0:T(8,128)S(1)} %early_sums.1.e_ref, ...), custom_call_target="tpu_custom_call", output_to_operand_aliasing={{0}: (1, {})} | custom-call | flops 1000000 | bytes 8388608 | tf_op jit(solution)/shard_map/assemble/pallas_call | solution.py:836
  (2 shorter events, 0.0 us)
Async XLA Ops:
  0.6 10.2 %copy-start.1 = (f32[32]{0:T(128)S(1)}, f32[32]{0:T(128)}, u32[]{:S(2)}) copy-start(f32[32]{0:T(128)} %param.14) | copy-start | bytes 388
  0.6 10.2 %copy-start = (bf16[32,32]{1,0:T(8,128)(2,1)S(1)}, bf16[32,32]{1,0:T(8,128)(2,1)}, u32[]{:S(2)}) copy-start(bf16[32,32]{1,0:T(8,128)(2,1)} %l_ref.1) | copy-start | bytes 6148
  3.4 15.7 %all-to-all-start = ((bf16[16,8,768]{2,1,0:T(8,128)(2,1)}), bf16[16,8,768]{2,1,0:T(8,128)(2,1)S(1)}, u32[]{:S(2)}, u32[]{:S(2)}) async-start(bf16[16,8,768]{2,1,0:T(8,128)(2,1)} %bitcast.17), calls=%async_computation | async-start | bytes 393216 | tf_op jit(solution)/shard_map/all_to_all | solution.py:900
  36.6 12.5 %all-to-all-start.2 = ((bf16[16,8,768]{2,1,0:T(8,128)(2,1)}), bf16[16,8,768]{2,1,0:T(8,128)(2,1)S(1)}, u32[]{:S(2)}, u32[]{:S(2)}) async-start(bf16[16,8,768]{2,1,0:T(8,128)(2,1)} %bitcast.19), calls=%async_computation.2 | async-start | bytes 393216 | tf_op jit(solution)/shard_map/all_to_all | solution.py:900
  50.2 2.3 %collective-permute-start = (f32[24,2048]{1,0:T(8,128)S(1)}, f32[24,2048]{1,0:T(8,128)S(1)}, u32[]{:S(2)}, u32[]{:S(2)}) collective-permute-start(f32[24,2048]{1,0:T(8,128)S(1)} %get-tuple-element.61.s_ref), channel_id=1, source_target_pairs={{0,1},{1,0},{2,3},{3,2},{4,5},{5,4},{6,7},{7,6},{8,9},{9,8},{10,11... | collective-permute-start | bytes 589832 | tf_op jit(solution)/shard_map/ppermute | solution.py:981
  52.6 5.2 %collective-permute-start.1 = (bf16[24,3200]{1,0:T(8,128)(2,1)S(1)}, bf16[24,3200]{1,0:T(8,128)(2,1)S(1)}, u32[]{:S(2)}, u32[]{:S(2)}) collective-permute-start(bf16[24,3200]{1,0:T(8,128)(2,1)S(1)} %make_shard.1.refs_0_), channel_id=1, source_target_pairs={{0,4},{1,5},{4,8},{5,9},{8,12},{9,13},{12,14},{13,15},{14,10},{15,... | collective-permute-start | bytes 460808 | tf_op jit(solution)/shard_map/ppermute | solution.py:925
  52.6 6.4 %collective-permute-start.5 = (bf16[24,3200]{1,0:T(8,128)(2,1)S(1)}, bf16[24,3200]{1,0:T(8,128)(2,1)S(1)}, u32[]{:S(2)}, u32[]{:S(2)}) collective-permute-start(bf16[24,3200]{1,0:T(8,128)(2,1)S(1)} %make_shard.1.refs_0_), channel_id=1, source_target_pairs={{0,2},{1,3},{4,0},{5,1},{8,4},{9,5},{12,8},{13,9},{14,12},{15,13},... | collective-permute-start | bytes 460808 | tf_op jit(solution)/shard_map/ppermute | solution.py:927
  54.1 10.8 %collective-permute-start.3 = (bf16[24,3200]{1,0:T(8,128)(2,1)S(1)}, bf16[24,3200]{1,0:T(8,128)(2,1)S(1)}, u32[]{:S(2)}, u32[]{:S(2)}) collective-permute-start(bf16[24,3200]{1,0:T(8,128)(2,1)S(1)} %make_shard.1.refs_0_), channel_id=1, source_target_pairs={{0,1},{1,0},{2,3},{3,2},{4,5},{5,4},{6,7},{7,6},{8,9},{9,8},{10,11... | collective-permute-start | bytes 460808 | tf_op jit(solution)/shard_map/ppermute | solution.py:920
  57.8 7.1 %collective-permute-start.4 = (bf16[24,3200]{1,0:T(8,128)(2,1)S(1)}, bf16[24,3200]{1,0:T(8,128)(2,1)S(1)}, u32[]{:S(2)}, u32[]{:S(2)}) collective-permute-start(bf16[24,3200]{1,0:T(8,128)(2,1)S(1)} %collective-permute-done.1.refs_2_), channel_id=1, source_target_pairs={{0,1},{1,0},{2,3},{3,2},{4,5},{5,4},{6,7},{7,6},{8,9},{9,8},{10,11... | collective-permute-start | bytes 460808 | tf_op jit(solution)/shard_map/ppermute | solution.py:920
  59.0 5.9 %collective-permute-start.6 = (bf16[24,3200]{1,0:T(8,128)(2,1)S(1)}, bf16[24,3200]{1,0:T(8,128)(2,1)S(1)}, u32[]{:S(2)}, u32[]{:S(2)}) collective-permute-start(bf16[24,3200]{1,0:T(8,128)(2,1)S(1)} %collective-permute-done.5.refs_4_), channel_id=1, source_target_pairs={{0,1},{1,0},{2,3},{3,2},{4,5},{5,4},{6,7},{7,6},{8,9},{9,8},{10,11... | collective-permute-start | bytes 460808 | tf_op jit(solution)/shard_map/ppermute | solution.py:920
  59.1 5.9 %collective-permute-start.2 = (bf16[24,3200]{1,0:T(8,128)(2,1)S(1)}, bf16[24,3200]{1,0:T(8,128)(2,1)S(1)}, u32[]{:S(2)}, u32[]{:S(2)}) collective-permute-start(bf16[24,3200]{1,0:T(8,128)(2,1)S(1)} %collective-permute-done.1.refs_2_), channel_id=1, source_target_pairs={{0,4},{1,5},{4,8},{5,9},{8,12},{9,13},{12,14},{13,15},{14,10},{15,... | collective-permute-start | bytes 460808 | tf_op jit(solution)/shard_map/ppermute | solution.py:925
  59.7 19.8 %all-to-all-start.3 = ((bf16[16,8,768]{2,1,0:T(8,128)(2,1)}), bf16[16,8,768]{2,1,0:T(8,128)(2,1)S(1)}, u32[]{:S(2)}, u32[]{:S(2)}) async-start(bf16[16,8,768]{2,1,0:T(8,128)(2,1)} %bitcast.18), calls=%async_computation.3 | async-start | bytes 393216 | tf_op jit(solution)/shard_map/all_to_all | solution.py:900
  63.5 8.8 %collective-permute-start.10 = (bf16[24,3200]{1,0:T(8,128)(2,1)S(1)}, bf16[24,3200]{1,0:T(8,128)(2,1)S(1)}, u32[]{:S(2)}, u32[]{:S(2)}) collective-permute-start(bf16[24,3200]{1,0:T(8,128)(2,1)S(1)} %collective-permute-done.5.refs_4_), channel_id=1, source_target_pairs={{0,2},{1,3},{4,0},{5,1},{8,4},{9,5},{12,8},{13,9},{14,12},{15,13},... | collective-permute-start | bytes 460808 | tf_op jit(solution)/shard_map/ppermute | solution.py:927
  64.9 8.3 %collective-permute-start.7 = (bf16[24,3200]{1,0:T(8,128)(2,1)S(1)}, bf16[24,3200]{1,0:T(8,128)(2,1)S(1)}, u32[]{:S(2)}, u32[]{:S(2)}) collective-permute-start(bf16[24,3200]{1,0:T(8,128)(2,1)S(1)} %collective-permute-done.2.refs_6_), channel_id=1, source_target_pairs={{0,4},{1,5},{4,8},{5,9},{8,12},{9,13},{12,14},{13,15},{14,10},{15,... | collective-permute-start | bytes 460808 | tf_op jit(solution)/shard_map/ppermute | solution.py:925
  72.3 5.7 %collective-permute-start.13 = (bf16[24,3200]{1,0:T(8,128)(2,1)S(1)}, bf16[24,3200]{1,0:T(8,128)(2,1)S(1)}, u32[]{:S(2)}, u32[]{:S(2)}) collective-permute-start(bf16[24,3200]{1,0:T(8,128)(2,1)S(1)} %collective-permute-done.10.refs_8_), channel_id=1, source_target_pairs={{0,2},{1,3},{4,0},{5,1},{8,4},{9,5},{12,8},{13,9},{14,12},{15,13},... | collective-permute-start | bytes 460808 | tf_op jit(solution)/shard_map/ppermute | solution.py:927
  72.3 10.9 %collective-permute-start.9 = (bf16[24,3200]{1,0:T(8,128)(2,1)S(1)}, bf16[24,3200]{1,0:T(8,128)(2,1)S(1)}, u32[]{:S(2)}, u32[]{:S(2)}) collective-permute-start(bf16[24,3200]{1,0:T(8,128)(2,1)S(1)} %collective-permute-done.2.refs_6_), channel_id=1, source_target_pairs={{0,1},{1,0},{2,3},{3,2},{4,5},{5,4},{6,7},{7,6},{8,9},{9,8},{10,11... | collective-permute-start | bytes 460808 | tf_op jit(solution)/shard_map/ppermute | solution.py:920
  73.2 10.0 %collective-permute-start.11 = (bf16[24,3200]{1,0:T(8,128)(2,1)S(1)}, bf16[24,3200]{1,0:T(8,128)(2,1)S(1)}, u32[]{:S(2)}, u32[]{:S(2)}) collective-permute-start(bf16[24,3200]{1,0:T(8,128)(2,1)S(1)} %collective-permute-done.10.refs_8_), channel_id=1, source_target_pairs={{0,1},{1,0},{2,3},{3,2},{4,5},{5,4},{6,7},{7,6},{8,9},{9,8},{10,11... | collective-permute-start | bytes 460808 | tf_op jit(solution)/shard_map/ppermute | solution.py:920
  73.2 10.8 %collective-permute-start.8 = (bf16[24,3200]{1,0:T(8,128)(2,1)S(1)}, bf16[24,3200]{1,0:T(8,128)(2,1)S(1)}, u32[]{:S(2)}, u32[]{:S(2)}) collective-permute-start(bf16[24,3200]{1,0:T(8,128)(2,1)S(1)} %collective-permute-done.7.refs_0_), channel_id=1, source_target_pairs={{0,4},{1,5},{4,8},{5,9},{8,12},{9,13},{12,14},{13,15},{14,10},{15,... | collective-permute-start | bytes 460808 | tf_op jit(solution)/shard_map/ppermute | solution.py:925
  75.4 8.6 %collective-permute-start.12 = (bf16[24,3200]{1,0:T(8,128)(2,1)S(1)}, bf16[24,3200]{1,0:T(8,128)(2,1)S(1)}, u32[]{:S(2)}, u32[]{:S(2)}) collective-permute-start(bf16[24,3200]{1,0:T(8,128)(2,1)S(1)} %collective-permute-done.7.refs_0_), channel_id=1, source_target_pairs={{0,1},{1,0},{2,3},{3,2},{4,5},{5,4},{6,7},{7,6},{8,9},{9,8},{10,11... | collective-permute-start | bytes 460808 | tf_op jit(solution)/shard_map/ppermute | solution.py:920
  78.0 6.0 %collective-permute-start.14 = (bf16[24,3200]{1,0:T(8,128)(2,1)S(1)}, bf16[24,3200]{1,0:T(8,128)(2,1)S(1)}, u32[]{:S(2)}, u32[]{:S(2)}) collective-permute-start(bf16[24,3200]{1,0:T(8,128)(2,1)S(1)} %collective-permute-done.13.refs_2_), channel_id=1, source_target_pairs={{0,1},{1,0},{2,3},{3,2},{4,5},{5,4},{6,7},{7,6},{8,9},{9,8},{10,11... | collective-permute-start | bytes 460808 | tf_op jit(solution)/shard_map/ppermute | solution.py:920
  84.0 1.4 %collective-permute-start.15 = (bf16[24,3200]{1,0:T(8,128)(2,1)S(1)}, bf16[24,3200]{1,0:T(8,128)(2,1)S(1)}, u32[]{:S(2)}, u32[]{:S(2)}) collective-permute-start(bf16[24,3200]{1,0:T(8,128)(2,1)S(1)} %collective-permute-done.8.refs_4_), channel_id=1, source_target_pairs={{0,1},{1,0},{2,3},{3,2},{4,5},{5,4},{6,7},{7,6},{8,9},{9,8},{10,11... | collective-permute-start | bytes 460808 | tf_op jit(solution)/shard_map/ppermute | solution.py:920
